TPU v7x, 32 devices: a whole 2x2x4 slice. The times are simulated.
32 devices in a mesh: row: 4 (over y, x), col: 8 (over z, core).
Axes of the slice: x: 2, y: 2, z: 4, core: 2. Of those that a mesh axis runs over, the one named last changes fastest.
Arguments:
- layer_input: bfloat16 [2, 4096, 1536], P(None, ('row', 'col')), may hold values from -6 to 6
- out_grad: bfloat16 [2, 4096, 1536], P(None, ('row', 'col')), may hold values from -6 to 6
- seq_lengths: int32 [2, 4], P(None, 'row'), may hold values from 256 to 1024, as said below
- routes: int32 [2, 4096, 6], P(None, 'row'), may hold values from 0 to 63, all different within a row; in each aligned block of 1024 rows (0 to 1023, 1024 to 2047, ..., all dimensions but the last counted through in order) at most 144 rows name the same one
- route_gates: float32 [2, 4096, 6], P(None, 'row'), may hold values from 0.2 to 0.6
- first_gain: float32 [1536], replicated, may hold values from 0.5 to 1.5
- gate_branch_proj: bfloat16 [1536, 3072], P('row', 'col'), may hold values from -0.15625 to 0.15625
- conv_in_proj: bfloat16 [1536, 3072], P('row', 'col'), may hold values from -0.15625 to 0.15625
- state_io_proj: bfloat16 [1536, 256], P('row', 'col'), may hold values from -0.15625 to 0.15625
- step_proj: bfloat16 [1536, 48], P('row', 'col'), may hold values from -0.15625 to 0.15625
- conv_kernel: float32 [4, 3072], P(None, 'col'), may hold values from -3 to 3
- conv_offset: float32 [3072], P('col'), may hold values from -1.5 to 1.5
- state_conv_kernel: float32 [4, 256], P(None, 'col'), may hold values from -3 to 3
- state_conv_offset: float32 [256], P('col'), may hold values from -1.5 to 1.5
- decay_log: float32 [48], P('col'), may hold values from 0 to 2.5
- step_offset: float32 [48], P('col'), may hold values from -9 to -3
- skip_scale: float32 [48], P('col'), may hold values from 0.5 to 1.5
- mixer_gain: float32 [3072], P('col'), may hold values from 0.5 to 1.5
- out_proj: bfloat16 [3072, 1536], P('col', 'row'), may hold values from -0.109375 to 0.109375
- second_gain: float32 [1536], replicated, may hold values from 0.5 to 1.5
- expert_gate: bfloat16 [64, 1536, 512], P('col', 'row'), may hold values from -0.15625 to 0.15625
- expert_up: bfloat16 [64, 1536, 512], P('col', 'row'), may hold values from -0.15625 to 0.15625
- expert_down: bfloat16 [64, 512, 1536], P('col', None, 'row'), may hold values from -0.25 to 0.25
- shared_gate: bfloat16 [1536, 1024], P('row', 'col'), may hold values from -0.15625 to 0.15625
- shared_up: bfloat16 [1536, 1024], P('row', 'col'), may hold values from -0.15625 to 0.15625
- shared_down: bfloat16 [1024, 1536], P('col', 'row'), may hold values from -0.1875 to 0.1875
Outputs:
- layer_output: bfloat16 [2, 4096, 1536], P(None, ('row', 'col'))
- input_grad: float32 [2, 4096, 1536], P(None, ('row', 'col'))
- first_gain_grad: float32 [1536], replicated
- gate_branch_proj_grad: float32 [1536, 3072], P('row', 'col')
- conv_in_proj_grad: float32 [1536, 3072], P('row', 'col')
- state_io_proj_grad: float32 [1536, 256], P('row', 'col')
- step_proj_grad: float32 [1536, 48], P('row', 'col')
- conv_kernel_grad: float32 [4, 3072], P(None, 'col')
- conv_offset_grad: float32 [3072], P('col')
- state_conv_kernel_grad: float32 [4, 256], P(None, 'col')
- state_conv_offset_grad: float32 [256], P('col')
- decay_log_grad: float32 [48], P('col')
- step_offset_grad: float32 [48], P('col')
- skip_scale_grad: float32 [48], P('col')
- mixer_gain_grad: float32 [3072], P('col')
- out_proj_grad: float32 [3072, 1536], P('col', 'row')
- second_gain_grad: float32 [1536], replicated
- expert_gate_grad: float32 [64, 1536, 512], P('col', 'row')
- expert_up_grad: float32 [64, 1536, 512], P('col', 'row')
- expert_down_grad: float32 [64, 512, 1536], P('col', None, 'row')
- shared_gate_grad: float32 [1536, 1024], P('row', 'col')
- shared_up_grad: float32 [1536, 1024], P('row', 'col')
- shared_down_grad: float32 [1024, 1536], P('col', 'row')
Inputs may be any that keep to these rules, and one draw needn't show every extreme that they name: `seq_lengths`: in each micro-batch one sequence has length 1024. `routes`: each token names 6 different experts. Within the 1024 rows of one sequence slot no expert is named more than 144 times, a bound that some block reaches.
All inputs are finite; a program needn't handle non-finite values.
Results may differ from a plain program's by a relative error of at most 0.015.
Values may be sent and summed in bfloat16 or wider, within the bound.
A program may use at most 384 MiB of HBM per device.

v0:
```python
import jax
import jax.numpy as jnp
from jax import lax
from jax.sharding import PartitionSpec as P

NH = 48
NS = 128
CONV = 4
BLOCK = 256
DI = 3072
CAP = 144


EPS = 1e-05
PRECISE = lax.Precision.HIGHEST


def add_up(summed, term):
    return summed + term


def dot_plain(left_op, right_op):
    return jnp.dot(left_op, right_op, preferred_element_type=jnp.float32)


def dot_first(left_op, right_op):
    return lax.dot_general(
        left_op, right_op, (((0,), (0,)), ((), ())), preferred_element_type=jnp.float32
    )


def dot_last(left_op, right_op):
    return lax.dot_general(
        left_op, right_op, (((1,), (1,)), ((), ())), preferred_element_type=jnp.float32
    )


def row_norm(values, scale_gain):
    return values * lax.rsqrt(jnp.mean(values * values, axis=1, keepdims=True) + EPS) * scale_gain


def silu_slope(values):
    logistic = jax.nn.sigmoid(values)
    return logistic * (1.0 + values * (1.0 - logistic))


def causal_conv(values, kernel, offset):
    length = values.shape[0]
    padded = jnp.pad(values, ((CONV - 1, 0), (0, 0)))
    summed = jnp.zeros_like(values) + offset
    for shift_back in range(CONV):
        summed = summed + kernel[shift_back] * padded[shift_back : shift_back + length]
    return summed


def block_scan(x_heads, step_size, rates, write_rows, read_rows):
    length, head_count, head_width = x_heads.shape
    blocks = length // BLOCK
    states_n = write_rows.shape[1]
    log_decay = -(step_size * rates)
    cumulative = jnp.cumsum(log_decay.reshape(blocks, BLOCK, head_count), axis=1)
    cum_heads = jnp.transpose(cumulative, (0, 2, 1))
    weighted = (x_heads * step_size[:, :, None]).reshape(blocks, BLOCK, head_count, head_width)
    write_block = write_rows.reshape(blocks, BLOCK, states_n)
    read_block = read_rows.reshape(blocks, BLOCK, states_n)
    places = jnp.arange(BLOCK)
    causal = places[:, None] >= places[None, :]
    spread = cum_heads[:, :, :, None] - cum_heads[:, :, None, :]
    decays = jnp.exp(jnp.where(causal[None, None], spread, -jnp.inf))
    scores = jnp.einsum("cin,cjn->cij", read_block, write_block, precision=PRECISE)
    mixing = scores[:, None] * decays
    within = jnp.einsum("chij,cjhp->cihp", mixing, weighted, precision=PRECISE)
    to_end = jnp.exp(cum_heads[:, :, -1:] - cum_heads)
    block_states = jnp.einsum(
        "cjn,chj,cjhp->chpn", write_block, to_end, weighted, precision=PRECISE
    )
    through = jnp.exp(cum_heads[:, :, -1])

    def advance(carried, element):
        fresh_state, factor = element
        return (carried * factor[:, None, None] + fresh_state, carried)

    initial = jnp.zeros((head_count, head_width, states_n), jnp.float32)
    unused, starts = lax.scan(advance, initial, (block_states, through))
    carried_out = jnp.einsum(
        "cin,chpn,chi->cihp", read_block, starts, jnp.exp(cum_heads), precision=PRECISE
    )
    return (within + carried_out).reshape(length, head_count, head_width)


def mixer_local(
    conv_pre,
    step_pre,
    branch_pre,
    state_io,
    conv_kernel,
    conv_offset,
    decay_log,
    step_offset,
    skip_scale,
):
    length = conv_pre.shape[0]
    head_count = step_pre.shape[1]
    conv_out = jax.nn.silu(causal_conv(conv_pre, conv_kernel, conv_offset))
    step_size = jax.nn.softplus(step_pre + step_offset)
    x_heads = conv_out.reshape(length, head_count, -1)
    scanned = block_scan(x_heads, step_size, jnp.exp(decay_log), state_io[:, :NS], state_io[:, NS:])
    scanned = scanned + skip_scale[:, None] * x_heads
    gated_out = scanned.reshape(length, -1) * jax.nn.silu(branch_pre)
    return (gated_out, jnp.sum(gated_out * gated_out, axis=1))


def io_local(io_pre, kernel, offset):
    return jax.nn.silu(causal_conv(io_pre, kernel, offset))


def expert_slots(route_rows, gate_rows, first_expert, expert_count):
    token_count, pick_count = route_rows.shape
    flat_routes = route_rows.reshape(-1) - first_expert
    owner = (flat_routes[:, None] == jnp.arange(expert_count, dtype=jnp.int32)[None, :]).astype(
        jnp.int32
    )
    ranks = jnp.sum((jnp.cumsum(owner, axis=0) - 1) * owner, axis=1)
    inside = jnp.sum(owner, axis=1) > 0
    dump_slot = expert_count * CAP
    target = jnp.where(inside, flat_routes * CAP + ranks, dump_slot)
    row_ids = jnp.arange(token_count * pick_count, dtype=jnp.int32) // pick_count
    slot_token = jnp.zeros((dump_slot + 1,), jnp.int32).at[target].set(row_ids)[:dump_slot]
    slot_gate = (
        jnp.zeros((dump_slot + 1,), jnp.float32).at[target].set(gate_rows.reshape(-1))[:dump_slot]
    )
    return (slot_token, slot_gate)


def widen(part_grad, full_size, start_at, along):
    shape_full = list(part_grad.shape)
    shape_full[along] = full_size
    return lax.dynamic_update_slice_in_dim(
        jnp.zeros(shape_full, jnp.float32), part_grad, start_at, along
    )


def local(
    layer_input,
    out_grad,
    seq_lengths,
    routes,
    route_gates,
    first_gain,
    gate_branch_proj,
    conv_in_proj,
    state_io_proj,
    step_proj,
    conv_kernel,
    conv_offset,
    state_conv_kernel,
    state_conv_offset,
    decay_log,
    step_offset,
    skip_scale,
    mixer_gain,
    out_proj,
    second_gain,
    expert_gate,
    expert_up,
    expert_down,
    shared_gate,
    shared_up,
    shared_down,
):
    micro_count = layer_input.shape[0]
    own_count = layer_input.shape[1]
    col_index = lax.axis_index("col")
    local_experts = expert_gate.shape[0]
    first_expert = col_index * local_experts
    channel_share = conv_kernel.shape[1]
    io_width = state_conv_kernel.shape[1]
    head_share = decay_log.shape[0]

    def fetch_weights():
        return (
            lax.all_gather(gate_branch_proj, "row", axis=0, tiled=True),
            lax.all_gather(conv_in_proj, "row", axis=0, tiled=True),
            lax.all_gather(state_io_proj, "row", axis=0, tiled=True),
            lax.all_gather(step_proj, "row", axis=0, tiled=True),
            lax.all_gather(out_proj, "row", axis=1, tiled=True),
            lax.all_gather(expert_gate, "row", axis=1, tiled=True),
            lax.all_gather(expert_up, "row", axis=1, tiled=True),
            lax.all_gather(expert_down, "row", axis=2, tiled=True),
            lax.all_gather(shared_gate, "row", axis=0, tiled=True),
            lax.all_gather(shared_up, "row", axis=0, tiled=True),
            lax.all_gather(shared_down, "row", axis=1, tiled=True),
        )

    outputs = []
    input_grads = []
    big_sums = None
    small_sums = None
    for micro_index in range(micro_count):
        (
            full_branch,
            full_conv,
            full_io,
            full_step,
            full_out,
            full_expert_gate,
            full_expert_up,
            full_expert_down,
            full_shared_gate,
            full_shared_up,
            full_shared_down,
        ) = fetch_weights()
        own_rows = layer_input[micro_index].astype(jnp.float32)
        all_rows, all_grad = (
            lax.all_gather(layer_input[micro_index], "col", axis=0, tiled=True),
            lax.all_gather(out_grad[micro_index], "col", axis=0, tiled=True),
        )
        seq_rows = all_rows.shape[0]
        first_normed = row_norm(all_rows.astype(jnp.float32), first_gain).astype(jnp.bfloat16)
        branch_pre = dot_plain(first_normed, full_branch)
        conv_pre = dot_plain(first_normed, full_conv)
        io_pre = dot_plain(first_normed, full_io)
        step_pre = dot_plain(first_normed, full_step)
        io_part, io_back = jax.vjp(io_local, io_pre, state_conv_kernel, state_conv_offset)
        state_io = lax.all_gather(io_part.astype(jnp.bfloat16), "col", axis=1, tiled=True)
        (gated_out, square_sums), mixer_back = jax.vjp(
            mixer_local,
            conv_pre,
            step_pre,
            branch_pre,
            state_io.astype(jnp.float32),
            conv_kernel,
            conv_offset,
            decay_log,
            step_offset,
            skip_scale,
        )
        total_squares = lax.psum(square_sums, "col")
        inverse_rms = lax.rsqrt(total_squares / DI + EPS)[:, None]
        mixed_out = (gated_out * inverse_rms * mixer_gain).astype(jnp.bfloat16)
        residual = own_rows + lax.psum_scatter(
            dot_plain(mixed_out, full_out), "col", scatter_dimension=0, tiled=True
        )
        second_own, second_back = jax.vjp(row_norm, residual, second_gain)
        second_normed = lax.all_gather(second_own.astype(jnp.bfloat16), "col", axis=0, tiled=True)
        slot_token, slot_gate = expert_slots(
            routes[micro_index], route_gates[micro_index], first_expert, local_experts
        )
        picked = second_normed[slot_token].reshape(local_experts, CAP, -1)
        gate_pre = jnp.einsum(
            "ecd,edh->ech", picked, full_expert_gate, preferred_element_type=jnp.float32
        )
        up_pre = jnp.einsum(
            "ecd,edh->ech", picked, full_expert_up, preferred_element_type=jnp.float32
        )
        hidden = (jax.nn.silu(gate_pre) * up_pre).astype(jnp.bfloat16)
        expert_out = jnp.einsum(
            "ech,ehd->ecd", hidden, full_expert_down, preferred_element_type=jnp.float32
        )
        weighted = (slot_gate.reshape(local_experts, CAP, 1) * expert_out).reshape(
            local_experts * CAP, -1
        )
        shared_gate_pre = dot_plain(second_normed, full_shared_gate)
        shared_up_pre = dot_plain(second_normed, full_shared_up)
        shared_hidden = (jax.nn.silu(shared_gate_pre) * shared_up_pre).astype(jnp.bfloat16)
        branch_sum = dot_plain(shared_hidden, full_shared_down).at[slot_token].add(weighted)
        branch_share = lax.psum_scatter(
            branch_sum.astype(jnp.bfloat16), "col", scatter_dimension=0, tiled=True
        ).astype(jnp.float32)
        outputs.append((residual + branch_share).astype(jnp.bfloat16))
        (
            full_branch,
            full_conv,
            full_io,
            full_step,
            full_out,
            full_expert_gate,
            full_expert_up,
            full_expert_down,
            full_shared_gate,
            full_shared_up,
            full_shared_down,
        ) = fetch_weights()
        valid_full = (jnp.arange(seq_rows) < seq_lengths[micro_index, 0]).astype(jnp.float32)
        valid_own = lax.dynamic_slice_in_dim(valid_full, col_index * own_count, own_count, 0)
        out_cot = all_grad.astype(jnp.float32) * valid_full[:, None]
        own_cot = out_grad[micro_index].astype(jnp.float32) * valid_own[:, None]
        cot_low = out_cot.astype(jnp.bfloat16)
        shared_dhidden = dot_last(cot_low, full_shared_down)
        shared_down_grad = dot_first(shared_hidden, cot_low)
        shared_dgate = (shared_dhidden * shared_up_pre * silu_slope(shared_gate_pre)).astype(
            jnp.bfloat16
        )
        shared_dup = (shared_dhidden * jax.nn.silu(shared_gate_pre)).astype(jnp.bfloat16)
        shared_gate_grad = dot_first(second_normed, shared_dgate)
        shared_up_grad = dot_first(second_normed, shared_dup)
        normed_grad = dot_last(shared_dgate, full_shared_gate) + dot_last(
            shared_dup, full_shared_up
        )
        slot_cot = (
            (slot_gate[:, None] * out_cot[slot_token])
            .astype(jnp.bfloat16)
            .reshape(local_experts, CAP, -1)
        )
        dhidden = jnp.einsum(
            "ecd,ehd->ech", slot_cot, full_expert_down, preferred_element_type=jnp.float32
        )
        expert_down_grad = jnp.einsum(
            "ech,ecd->ehd", hidden, slot_cot, preferred_element_type=jnp.float32
        )
        dgate_pre = (dhidden * up_pre * silu_slope(gate_pre)).astype(jnp.bfloat16)
        dup_pre = (dhidden * jax.nn.silu(gate_pre)).astype(jnp.bfloat16)
        dpicked = jnp.einsum(
            "ech,edh->ecd", dgate_pre, full_expert_gate, preferred_element_type=jnp.float32
        ) + jnp.einsum("ech,edh->ecd", dup_pre, full_expert_up, preferred_element_type=jnp.float32)
        expert_gate_grad = jnp.einsum(
            "ecd,ech->edh", picked, dgate_pre, preferred_element_type=jnp.float32
        )
        expert_up_grad = jnp.einsum(
            "ecd,ech->edh", picked, dup_pre, preferred_element_type=jnp.float32
        )
        normed_grad = normed_grad.at[slot_token].add(dpicked.reshape(local_experts * CAP, -1))
        normed_share = lax.psum_scatter(normed_grad, "col", scatter_dimension=0, tiled=True)
        residual_back, second_gain_grad = second_back(normed_share)
        residual_grad = own_cot + residual_back
        residual_low = lax.all_gather(residual_grad.astype(jnp.bfloat16), "col", axis=0, tiled=True)
        dmixed = dot_last(residual_low, full_out)
        out_proj_grad = dot_first(mixed_out, residual_low)
        scaled_grad = dmixed * mixer_gain
        mixer_gain_grad = jnp.sum(dmixed * gated_out * inverse_rms, axis=0)
        cross_sums = lax.psum(jnp.sum(scaled_grad * gated_out, axis=1), "col")
        cube_rms = inverse_rms[:, 0] * inverse_rms[:, 0] * inverse_rms[:, 0]
        square_cot = -0.5 * cross_sums * cube_rms / DI
        (
            conv_cot,
            step_cot,
            branch_cot,
            io_cot,
            kernel_grad,
            offset_grad,
            decay_grad,
            step_offset_grad,
            skip_grad,
        ) = mixer_back((scaled_grad * inverse_rms, square_cot))
        io_share_cot = lax.psum_scatter(io_cot, "col", scatter_dimension=1, tiled=True)
        io_pre_cot, io_kernel_grad, io_offset_grad = io_back(io_share_cot)
        branch_low = branch_cot.astype(jnp.bfloat16)
        conv_low = conv_cot.astype(jnp.bfloat16)
        io_low = io_pre_cot.astype(jnp.bfloat16)
        step_low = step_cot.astype(jnp.bfloat16)
        first_part = (
            dot_last(branch_low, full_branch)
            + dot_last(conv_low, full_conv)
            + dot_last(io_low, full_io)
            + dot_last(step_low, full_step)
        )
        first_share = lax.psum_scatter(
            first_part.astype(jnp.bfloat16), "col", scatter_dimension=0, tiled=True
        ).astype(jnp.float32)
        own_normed, first_back = jax.vjp(row_norm, own_rows, first_gain)
        rows_back, first_gain_grad = first_back(first_share)
        input_grads.append(residual_grad + rows_back)
        big_grads = (
            dot_first(first_normed, branch_low),
            dot_first(first_normed, conv_low),
            dot_first(first_normed, io_low),
            dot_first(first_normed, step_low),
            out_proj_grad,
            expert_gate_grad,
            expert_up_grad,
            expert_down_grad,
            shared_gate_grad,
            shared_up_grad,
            shared_down_grad,
        )
        small_grads = (
            first_gain_grad,
            second_gain_grad,
            kernel_grad,
            offset_grad,
            io_kernel_grad,
            io_offset_grad,
            decay_grad,
            step_offset_grad,
            skip_grad,
            mixer_gain_grad,
        )
        big_grads = (
            lax.psum_scatter(
                big_grads[0].astype(jnp.bfloat16), "row", scatter_dimension=0, tiled=True
            ).astype(jnp.float32),
            lax.psum_scatter(
                big_grads[1].astype(jnp.bfloat16), "row", scatter_dimension=0, tiled=True
            ).astype(jnp.float32),
            lax.psum_scatter(
                big_grads[2].astype(jnp.bfloat16), "row", scatter_dimension=0, tiled=True
            ).astype(jnp.float32),
            lax.psum_scatter(
                big_grads[3].astype(jnp.bfloat16), "row", scatter_dimension=0, tiled=True
            ).astype(jnp.float32),
            lax.psum_scatter(
                big_grads[4].astype(jnp.bfloat16), "row", scatter_dimension=1, tiled=True
            ).astype(jnp.float32),
            lax.psum_scatter(
                big_grads[5].astype(jnp.bfloat16), "row", scatter_dimension=1, tiled=True
            ).astype(jnp.float32),
            lax.psum_scatter(
                big_grads[6].astype(jnp.bfloat16), "row", scatter_dimension=1, tiled=True
            ).astype(jnp.float32),
            lax.psum_scatter(
                big_grads[7].astype(jnp.bfloat16), "row", scatter_dimension=2, tiled=True
            ).astype(jnp.float32),
            lax.psum_scatter(
                big_grads[8].astype(jnp.bfloat16), "row", scatter_dimension=0, tiled=True
            ).astype(jnp.float32),
            lax.psum_scatter(
                big_grads[9].astype(jnp.bfloat16), "row", scatter_dimension=0, tiled=True
            ).astype(jnp.float32),
            lax.psum_scatter(
                big_grads[10].astype(jnp.bfloat16), "row", scatter_dimension=1, tiled=True
            ).astype(jnp.float32),
        )
        big_sums = big_grads if micro_index == 0 else jax.tree.map(add_up, big_sums, big_grads)
        small_sums = (
            small_grads if micro_index == 0 else jax.tree.map(add_up, small_sums, small_grads)
        )
    channel_start = col_index * channel_share
    io_start = col_index * io_width
    head_start = col_index * head_share
    (
        first_sum,
        second_sum,
        kernel_sum,
        offset_sum,
        io_kernel_sum,
        io_offset_sum,
        decay_sum,
        step_sum,
        skip_sum,
        gain_sum,
    ) = small_sums
    totals = lax.psum(
        (
            first_sum,
            second_sum,
            widen(kernel_sum, DI, channel_start, 1),
            widen(offset_sum, DI, channel_start, 0),
            widen(io_kernel_sum, 2 * NS, io_start, 1),
            widen(io_offset_sum, 2 * NS, io_start, 0),
            widen(decay_sum, NH, head_start, 0),
            widen(step_sum, NH, head_start, 0),
            widen(skip_sum, NH, head_start, 0),
            widen(gain_sum, DI, channel_start, 0),
        ),
        ("row", "col"),
    )
    conv_kernel_grad = lax.dynamic_slice_in_dim(totals[2], channel_start, channel_share, 1)
    conv_offset_grad = lax.dynamic_slice_in_dim(totals[3], channel_start, channel_share, 0)
    state_conv_kernel_grad = lax.dynamic_slice_in_dim(totals[4], io_start, io_width, 1)
    state_conv_offset_grad = lax.dynamic_slice_in_dim(totals[5], io_start, io_width, 0)
    decay_log_grad = lax.dynamic_slice_in_dim(totals[6], head_start, head_share, 0)
    step_offset_grad = lax.dynamic_slice_in_dim(totals[7], head_start, head_share, 0)
    skip_scale_grad = lax.dynamic_slice_in_dim(totals[8], head_start, head_share, 0)
    mixer_gain_grad = lax.dynamic_slice_in_dim(totals[9], channel_start, channel_share, 0)
    return (
        jnp.stack(outputs),
        jnp.stack(input_grads),
        totals[0],
        big_sums[0],
        big_sums[1],
        big_sums[2],
        big_sums[3],
        conv_kernel_grad,
        conv_offset_grad,
        state_conv_kernel_grad,
        state_conv_offset_grad,
        decay_log_grad,
        step_offset_grad,
        skip_scale_grad,
        mixer_gain_grad,
        big_sums[4],
        totals[1],
        big_sums[5],
        big_sums[6],
        big_sums[7],
        big_sums[8],
        big_sums[9],
        big_sums[10],
    )


def solution(mesh):
    placed = (
        P(None, ("row", "col"), None),
        P(None, ("row", "col"), None),
        P(None, "row"),
        P(None, "row", None),
        P(None, "row", None),
        P(),
        P("row", "col"),
        P("row", "col"),
        P("row", "col"),
        P("row", "col"),
        P(None, "col"),
        P("col"),
        P(None, "col"),
        P("col"),
        P("col"),
        P("col"),
        P("col"),
        P("col"),
        P("col", "row"),
        P(),
        P("col", "row", None),
        P("col", "row", None),
        P("col", None, "row"),
        P("row", "col"),
        P("row", "col"),
        P("col", "row"),
    )
    return jax.shard_map(
        local,
        mesh=mesh,
        in_specs=placed,
        out_specs=(
            P(None, ("row", "col"), None),
            P(None, ("row", "col"), None),
            P(),
            P("row", "col"),
            P("row", "col"),
            P("row", "col"),
            P("row", "col"),
            P(None, "col"),
            P("col"),
            P(None, "col"),
            P("col"),
            P("col"),
            P("col"),
            P("col"),
            P("col"),
            P("col", "row"),
            P(),
            P("col", "row", None),
            P("col", "row", None),
            P("col", None, "row"),
            P("row", "col"),
            P("row", "col"),
            P("col", "row"),
        ),
        check_vma=False,
    )
```

profile of v0, /device:TPU:0, one launch (start us, length us, event | category | flops | bytes accessed | tf_op | source)
XLA Modules:
  0.0 3053.1 jit_solution(11569796470170964914)
XLA Ops:
  34.0 17.3 all-gather.41.cloned.1.call-done
  53.9 36.8 %all-gather.39.cloned.1.call-done = bf16[1,1024,1536]{2,1,0:T(8,128)(2,1)} async-done(((bf16[1,128,1536]{2,1,0:T(8,128)(2,1)}), bf16[1,1024,1536]{2,1,0:T(8,128)(2,1)}) %all-gather.39.cloned.1.call-update) | async-done | bytes 3145744 | tf_op jit(solution)/shard_map/all_gather | solution.py:215
  159.1 14.7 all_gather.46
  185.6 14.9 all_gather.111
  303.0 15.2 all-reduce.46
  333.1 59.7 %reduce-scatter.53.cloned.1.call-done = f32[128,1536]{1,0:T(8,128)} async-done(((f32[1024,1536]{1,0:T(8,128)}), f32[128,1536]{1,0:T(8,128)}) %reduce-scatter.53.cloned.1.call-update) | async-done | bytes 786448 | tf_op jit(solution)/shard_map/reduce_scatter | solution.py:241
  392.8 71.1 %reduce-scatter.57.cloned.1.call-done = f32[128,1536]{1,0:T(8,128)} async-done(((f32[1024,1536]{1,0:T(8,128)}), f32[128,1536]{1,0:T(8,128)}) %reduce-scatter.57.cloned.1.call-update) | async-done | bytes 786448 | tf_op jit(solution)/shard_map/reduce_scatter | solution.py:241
  477.9 23.0 scatter_custom_fusion
  500.9 23.0 scatter_custom_fusion.1
  594.1 71.3 %all-gather.29.cloned.1.call-done = bf16[8,1536,512]{2,1,0:T(8,128)(2,1)} async-done(((bf16[8,384,512]{2,1,0:T(8,128)(2,1)}), bf16[8,1536,512]{2,1,0:T(8,128)(2,1)}) %all-gather.29.cloned.1.call-update) | async-done | bytes 12582928 | tf_op jit(solution)/shard_map/all_gather | solution.py:188
  673.3 116.4 %all-gather.27.cloned.1.call-done = bf16[8,1536,512]{2,1,0:T(8,128)(2,1)} async-done(((bf16[8,384,512]{2,1,0:T(8,128)(2,1)}), bf16[8,1536,512]{2,1,0:T(8,128)(2,1)}) %all-gather.27.cloned.1.call-update) | async-done | bytes 12582928 | tf_op jit(solution)/shard_map/all_gather | solution.py:187
  797.7 116.1 %all-gather.31.cloned.1.call-done = bf16[8,512,1536]{2,1,0:T(8,128)(2,1)} async-done(((bf16[8,512,384]{2,1,0:T(8,128)(2,1)}), bf16[8,512,1536]{2,1,0:T(8,128)(2,1)}) %all-gather.31.cloned.1.call-update) | async-done | bytes 12582928 | tf_op jit(solution)/shard_map/all_gather | solution.py:189
  937.8 13.6 convolution_add_fusion.1
  951.4 22.0 scatter_fusion.2
  974.3 69.2 %reduce-scatter.61.cloned.1.call-done = f32[128,1536]{1,0:T(8,128)} async-done(((f32[1024,1536]{1,0:T(8,128)}), f32[128,1536]{1,0:T(8,128)}) %reduce-scatter.61.cloned.1.call-update) | async-done | bytes 786448 | tf_op jit(solution)/shard_map/reduce_scatter | solution.py:323
  1051.1 23.2 scatter_custom_fusion.3
  1074.9 23.0 scatter_custom_fusion.4
  1179.3 13.7 convolution_add_fusion
  1193.1 22.0 scatter_fusion.3
  1229.5 22.2 scatter_fusion
  1270.7 22.1 scatter_fusion.1
  1301.4 23.4 reduce-scatter.55.cloned.1.call-done
  1324.8 41.6 %reduce-scatter.59.cloned.1.call-done = bf16[128,1536]{1,0:T(8,128)(2,1)} async-done(((bf16[1024,1536]{1,0:T(8,128)(2,1)}), bf16[128,1536]{1,0:T(8,128)(2,1)}) %reduce-scatter.59.cloned.1.call-update) | async-done | bytes 393232 | tf_op jit(solution)/shard_map/reduce_scatter | solution.py:267
  1370.9 36.9 %all-gather.37.cloned.1.call-done = bf16[1024,1536]{1,0:T(8,128)(2,1)} async-done(((bf16[128,1536]{1,0:T(8,128)(2,1)}), bf16[1024,1536]{1,0:T(8,128)(2,1)}) %all-gather.37.cloned.1.call-update) | async-done | bytes 3145744 | tf_op jit(solution)/shard_map/all_gather | solution.py:326
  1412.9 34.1 %all-gather.35.cloned.1.call-done = bf16[1024,1536]{1,0:T(8,128)(2,1)} async-done(((bf16[128,1536]{1,0:T(8,128)(2,1)}), bf16[1024,1536]{1,0:T(8,128)(2,1)}) %all-gather.35.cloned.1.call-update) | async-done | bytes 3145744 | tf_op jit(solution)/shard_map/all_gather | solution.py:326
  1453.3 15.9 all-reduce.45
  1503.5 17.6 while.71
  1595.3 16.9 copy.651
  1659.9 30.2 reduce-window.54
  1690.3 30.3 reduce-window.56
  1830.9 17.1 copy.653
  1937.0 15.4 reduce-scatter.101.cloned.1.call-done
  1954.7 25.6 reduce-scatter.99.cloned.1.call-done
  1981.2 26.7 reduce-scatter.97.cloned.1.call-done
  2009.5 29.9 reduce-scatter.107.cloned.1.call-done
  2040.6 30.3 reduce-scatter.105.cloned.1.call-done
  2073.0 29.3 reduce-scatter.75.cloned.1.call-done
  2102.3 31.3 %reduce-scatter.73.cloned.1.call-done = bf16[384,384]{1,0:T(8,128)(2,1)} async-done(((bf16[1536,384]{1,0:T(8,128)(2,1)}), bf16[384,384]{1,0:T(8,128)(2,1)}) %reduce-scatter.73.cloned.1.call-update) | async-done | bytes 294928 | tf_op jit(solution)/shard_map/reduce_scatter | solution.py:389
  2135.6 29.5 reduce-scatter.79.cloned.1.call-done
  2165.1 31.9 %reduce-scatter.77.cloned.1.call-done = bf16[384,384]{1,0:T(8,128)(2,1)} async-done(((bf16[1536,384]{1,0:T(8,128)(2,1)}), bf16[384,384]{1,0:T(8,128)(2,1)}) %reduce-scatter.77.cloned.1.call-update) | async-done | bytes 294928 | tf_op jit(solution)/shard_map/reduce_scatter | solution.py:392
  2198.9 121.9 %reduce-scatter.111.cloned.1.call-done = bf16[384,4096]{1,0:T(8,128)(2,1)} async-done(((bf16[1536,4096]{1,0:T(8,128)(2,1)}), bf16[384,4096]{1,0:T(8,128)(2,1)}) %reduce-scatter.111.cloned.1.call-update) | async-done | bytes 3145744
  2333.8 110.9 %reduce-scatter.85.cloned.1.call-done = bf16[8,384,512]{2,1,0:T(8,128)(2,1)} async-done(((bf16[8,1536,512]{2,1,0:T(8,128)(2,1)}), bf16[8,384,512]{2,1,0:T(8,128)(2,1)}) %reduce-scatter.85.cloned.1.call-update) | async-done | bytes 3145744 | tf_op jit(solution)/shard_map/reduce_scatter | solution.py:407
  2444.7 123.9 %reduce-scatter.87.cloned.1.call-done = bf16[8,384,512]{2,1,0:T(8,128)(2,1)} async-done(((bf16[8,1536,512]{2,1,0:T(8,128)(2,1)}), bf16[8,384,512]{2,1,0:T(8,128)(2,1)}) %reduce-scatter.87.cloned.1.call-update) | async-done | bytes 3145744 | tf_op jit(solution)/shard_map/reduce_scatter | solution.py:407
  2575.2 117.2 %reduce-scatter.81.cloned.1.call-done = bf16[8,384,512]{2,1,0:T(8,128)(2,1)} async-done(((bf16[8,1536,512]{2,1,0:T(8,128)(2,1)}), bf16[8,384,512]{2,1,0:T(8,128)(2,1)}) %reduce-scatter.81.cloned.1.call-update) | async-done | bytes 3145744 | tf_op jit(solution)/shard_map/reduce_scatter | solution.py:404
  2692.3 123.9 %reduce-scatter.83.cloned.1.call-done = bf16[8,384,512]{2,1,0:T(8,128)(2,1)} async-done(((bf16[8,1536,512]{2,1,0:T(8,128)(2,1)}), bf16[8,384,512]{2,1,0:T(8,128)(2,1)}) %reduce-scatter.83.cloned.1.call-update) | async-done | bytes 3145744 | tf_op jit(solution)/shard_map/reduce_scatter | solution.py:404
  2822.7 36.0 %reduce-scatter.65.cloned.1.call-done = bf16[128,1536]{1,0:T(8,128)(2,1)} async-done(((bf16[1024,1536]{1,0:T(8,128)(2,1)}), bf16[128,1536]{1,0:T(8,128)(2,1)}) %reduce-scatter.65.cloned.1.call-update) | async-done | bytes 393232 | tf_op jit(solution)/shard_map/reduce_scatter | solution.py:357
  2858.7 41.6 %reduce-scatter.71.cloned.1.call-done = bf16[128,1536]{1,0:T(8,128)(2,1)} async-done(((bf16[1024,1536]{1,0:T(8,128)(2,1)}), bf16[128,1536]{1,0:T(8,128)(2,1)}) %reduce-scatter.71.cloned.1.call-update) | async-done | bytes 393232 | tf_op jit(solution)/shard_map/reduce_scatter | solution.py:357
  2905.7 127.6 %all-reduce.49.cloned.1.call-done = (f32[1536]{0:T(1024)}, f32[4,3072]{1,0:T(4,128)}, f32[3072]{0:T(1024)}, f32[4,256]{1,0:T(4,128)}, f32[256]{0:T(256)}, /*inde...) async-done(((f32[1536]{0:T(1024)}, f32[4,3072]{1,0:T(4,128)}, f32[3072]{0:T(1024)}, f32[4,256]{1,0:T(4,128)}, f32[256]{0:T(256)}, ...) | async-done | bytes 91728 | tf_op jit(solution)/shard_map/psum | solution.py:442
  (1143 shorter events, 945.9 us)
Async XLA Ops:
  7.3 44.1 %all-gather.41.cloned.1.call-start = ((), (), s32[]{:S(2)}) async-start(), calls=%async_computation.65 | async-start | bytes 3538944 | tf_op jit(solution)/shard_map/all_gather | solution.py:215
  9.4 81.3 %all-gather.39.cloned.1.call-start = ((), (), s32[]{:S(2)}) async-start(), calls=%async_computation.64 | async-start | bytes 3538944 | tf_op jit(solution)/shard_map/all_gather | solution.py:215
  10.1 202.3 %all-gather.19.cloned.1.call-start = ((), (), s32[]{:S(2)}) async-start(), calls=%async_computation.32 | async-start | bytes 1474560 | tf_op jit(solution)/shard_map/all_gather | solution.py:183
  10.9 266.9 %all-gather.21.cloned.1.call-start = ((), (), s32[]{:S(2)}) async-start(), calls=%async_computation.33 | async-start | bytes 1474560 | tf_op jit(solution)/shard_map/all_gather | solution.py:182
  11.4 306.9 %all-gather.23.cloned.1.call-start = ((), (), s32[]{:S(2)}) async-start(), calls=%async_computation.34 | async-start | bytes 1474560 | tf_op jit(solution)/shard_map/all_gather | solution.py:186
  12.0 380.8 %reduce-scatter.53.cloned.1.call-start = ((), (), s32[]{:S(2)}) async-start(), calls=%async_computation.35 | async-start | bytes 7077888 | tf_op jit(solution)/shard_map/reduce_scatter | solution.py:241
  324.7 139.2 %reduce-scatter.57.cloned.1.call-start = ((), (), s32[]{:S(2)}) async-start(), calls=%async_computation.41 | async-start | bytes 7077888 | tf_op jit(solution)/shard_map/reduce_scatter | solution.py:241
  331.0 225.5 %all-gather.43.cloned.1.call-start = ((), (), s32[]{:S(2)}) async-start(), calls=%async_computation.66 | async-start | bytes 3538944 | tf_op jit(solution)/shard_map/all_gather | solution.py:216
  333.1 240.0 %all-gather.25.cloned.1.call-start = ((), (), s32[]{:S(2)}) async-start(), calls=%async_computation.36 | async-start | bytes 3538944 | tf_op jit(solution)/shard_map/all_gather | solution.py:245
  468.8 196.5 %all-gather.29.cloned.1.call-start = ((), (), s32[]{:S(2)}) async-start(), calls=%async_computation.38 | async-start | bytes 15728640 | tf_op jit(solution)/shard_map/all_gather | solution.py:188
  469.4 320.3 %all-gather.27.cloned.1.call-start = ((), (), s32[]{:S(2)}) async-start(), calls=%async_computation.37 | async-start | bytes 15728640 | tf_op jit(solution)/shard_map/all_gather | solution.py:187
  470.2 443.6 %all-gather.31.cloned.1.call-start = ((), (), s32[]{:S(2)}) async-start(), calls=%async_computation.39 | async-start | bytes 15728640 | tf_op jit(solution)/shard_map/all_gather | solution.py:189
  470.8 572.7 %reduce-scatter.61.cloned.1.call-start = ((), (), s32[]{:S(2)}) async-start(), calls=%async_computation.44 | async-start | bytes 7077888 | tf_op jit(solution)/shard_map/reduce_scatter | solution.py:323
  524.0 389.9 %copy-start.139 = (f32[8,144]{1,0:T(8,128)}, f32[8,144]{1,0:T(8,128)S(1)}, u32[]{:S(2)}) copy-start(f32[8,144]{1,0:T(8,128)S(1)} %mul.1291) | copy-start | bytes 13828
  973.5 125.2 %all-gather.45.cloned.1.call-start = ((), (), s32[]{:S(2)}) async-start(), calls=%async_computation.67 | async-start | bytes 3538944 | tf_op jit(solution)/shard_map/all_gather | solution.py:216
  974.0 147.4 %all-gather.33.cloned.1.call-start = ((), (), s32[]{:S(2)}) async-start(), calls=%async_computation.42 | async-start | bytes 3538944 | tf_op jit(solution)/shard_map/all_gather | solution.py:245
  1046.2 253.2 %reduce-scatter.67.cloned.1.call-start = ((), (), s32[]{:S(2)}) async-start(), calls=%async_computation.48 | async-start | bytes 7077888 | tf_op jit(solution)/shard_map/reduce_scatter | solution.py:323
  1215.1 109.7 %reduce-scatter.55.cloned.1.call-start = ((), (), s32[]{:S(2)}) async-start(), calls=%async_computation.40 | async-start | bytes 3538944 | tf_op jit(solution)/shard_map/reduce_scatter | solution.py:267
  1256.5 109.9 %reduce-scatter.59.cloned.1.call-start = ((), (), s32[]{:S(2)}) async-start(), calls=%async_computation.43 | async-start | bytes 3538944 | tf_op jit(solution)/shard_map/reduce_scatter | solution.py:267
  1297.7 110.0 %all-gather.37.cloned.1.call-start = ((), (), s32[]{:S(2)}) async-start(), calls=%async_computation.49 | async-start | bytes 3538944 | tf_op jit(solution)/shard_map/all_gather | solution.py:326
  1370.2 76.8 %all-gather.35.cloned.1.call-start = ((), (), s32[]{:S(2)}) async-start(), calls=%async_computation.45 | async-start | bytes 3538944 | tf_op jit(solution)/shard_map/all_gather | solution.py:326
  1370.7 358.8 %reduce-scatter.69.cloned.1.call-start = ((), (), s32[]{:S(2)}) async-start(), calls=%async_computation.50 | async-start | bytes 1179648 | tf_op jit(solution)/shard_map/reduce_scatter | solution.py:345
  1549.3 182.8 %reduce-scatter.63.cloned.1.call-start = ((), (), s32[]{:S(2)}) async-start(), calls=%async_computation.46 | async-start | bytes 1179648 | tf_op jit(solution)/shard_map/reduce_scatter | solution.py:345
  1564.5 354.6 %reduce-scatter.113.cloned.1.call-start = ((), (), s32[]{:S(2)}) async-start(), calls=%async_computation.76 | async-start | bytes 491520
  1568.2 352.0 %reduce-scatter.115.cloned.1.call-start = ((), (), s32[]{:S(2)}) async-start(), calls=%async_computation.77 | async-start | bytes 491520
  1573.8 348.1 %reduce-scatter.93.cloned.1.call-start = ((), (), s32[]{:S(2)}) async-start(), calls=%async_computation.62 | async-start | bytes 491520 | tf_op jit(solution)/shard_map/reduce_scatter | solution.py:416
  1575.7 346.2 %reduce-scatter.95.cloned.1.call-start = ((), (), s32[]{:S(2)}) async-start(), calls=%async_computation.63 | async-start | bytes 491520 | tf_op jit(solution)/shard_map/reduce_scatter | solution.py:416
  1579.5 344.1 %reduce-scatter.89.cloned.1.call-start = ((), (), s32[]{:S(2)}) async-start(), calls=%async_computation.60 | async-start | bytes 491520 | tf_op jit(solution)/shard_map/reduce_scatter | solution.py:413
  1581.6 342.0 %reduce-scatter.91.cloned.1.call-start = ((), (), s32[]{:S(2)}) async-start(), calls=%async_computation.61 | async-start | bytes 491520 | tf_op jit(solution)/shard_map/reduce_scatter | solution.py:413
  1585.5 339.7 %reduce-scatter.109.cloned.1.call-start = ((), (), s32[]{:S(2)}) async-start(), calls=%async_computation.74 | async-start | bytes 15728640
  1625.2 310.9 %reduce-scatter.103.cloned.1.call-start = ((), (), s32[]{:S(2)}) async-start(), calls=%async_computation.71 | async-start | bytes 491520
  1727.5 225.0 %reduce-scatter.101.cloned.1.call-start = ((), (), s32[]{:S(2)}) async-start(), calls=%async_computation.70 | async-start | bytes 491520
  1729.5 250.8 %reduce-scatter.99.cloned.1.call-start = ((), (), s32[]{:S(2)}) async-start(), calls=%async_computation.69 | async-start | bytes 491520
  1741.1 266.8 %reduce-scatter.97.cloned.1.call-start = ((), (), s32[]{:S(2)}) async-start(), calls=%async_computation.68 | async-start | bytes 491520
  1744.0 295.5 %reduce-scatter.107.cloned.1.call-start = ((), (), s32[]{:S(2)}) async-start(), calls=%async_computation.73 | async-start | bytes 1474560
  1751.4 319.6 %reduce-scatter.105.cloned.1.call-start = ((), (), s32[]{:S(2)}) async-start(), calls=%async_computation.72 | async-start | bytes 1474560
  1758.7 343.6 %reduce-scatter.75.cloned.1.call-start = ((), (), s32[]{:S(2)}) async-start(), calls=%async_computation.53 | async-start | bytes 1474560 | tf_op jit(solution)/shard_map/reduce_scatter | solution.py:389
  1763.8 369.9 %reduce-scatter.73.cloned.1.call-start = ((), (), s32[]{:S(2)}) async-start(), calls=%async_computation.52 | async-start | bytes 1474560 | tf_op jit(solution)/shard_map/reduce_scatter | solution.py:389
  1792.1 373.0 %reduce-scatter.79.cloned.1.call-start = ((), (), s32[]{:S(2)}) async-start(), calls=%async_computation.55 | async-start | bytes 1474560 | tf_op jit(solution)/shard_map/reduce_scatter | solution.py:392
  1811.7 385.4 %reduce-scatter.77.cloned.1.call-start = ((), (), s32[]{:S(2)}) async-start(), calls=%async_computation.54 | async-start | bytes 1474560 | tf_op jit(solution)/shard_map/reduce_scatter | solution.py:392
  1819.6 501.3 %reduce-scatter.111.cloned.1.call-start = ((), (), s32[]{:S(2)}) async-start(), calls=%async_computation.75 | async-start | bytes 15728640
  1860.9 583.8 %reduce-scatter.85.cloned.1.call-start = ((), (), s32[]{:S(2)}) async-start(), calls=%async_computation.58 | async-start | bytes 15728640 | tf_op jit(solution)/shard_map/reduce_scatter | solution.py:407
  1871.1 697.5 %reduce-scatter.87.cloned.1.call-start = ((), (), s32[]{:S(2)}) async-start(), calls=%async_computation.59 | async-start | bytes 15728640 | tf_op jit(solution)/shard_map/reduce_scatter | solution.py:407
  1882.0 810.3 %reduce-scatter.81.cloned.1.call-start = ((), (), s32[]{:S(2)}) async-start(), calls=%async_computation.56 | async-start | bytes 15728640 | tf_op jit(solution)/shard_map/reduce_scatter | solution.py:404
  1890.1 926.1 %reduce-scatter.83.cloned.1.call-start = ((), (), s32[]{:S(2)}) async-start(), calls=%async_computation.57 | async-start | bytes 15728640 | tf_op jit(solution)/shard_map/reduce_scatter | solution.py:404
  1900.0 958.7 %reduce-scatter.65.cloned.1.call-start = ((), (), s32[]{:S(2)}) async-start(), calls=%async_computation.47 | async-start | bytes 3538944 | tf_op jit(solution)/shard_map/reduce_scatter | solution.py:357
  1909.3 991.0 %reduce-scatter.71.cloned.1.call-start = ((), (), s32[]{:S(2)}) async-start(), calls=%async_computation.51 | async-start | bytes 3538944 | tf_op jit(solution)/shard_map/reduce_scatter | solution.py:357
  1918.0 1115.3 %all-reduce.49.cloned.1.call-start = ((), (), s32[]{:S(2)}) async-start(), calls=%async_computation.78 | async-start | bytes 193536 | tf_op jit(solution)/shard_map/psum | solution.py:442
  (286 other events, 6753.4 us)
Sparse Core Ops, SparseCore 0:
  10.3 40.9 all-gather.40
  53.5 37.1 all-gather.38
  92.6 26.5 all-gather.18
  120.9 27.7 all-gather.20
  150.3 27.5 all-gather.22
  324.8 67.9 reduce-scatter.52
  395.7 68.1 reduce-scatter.56
  466.1 36.6 all-gather.42
  505.0 37.1 all-gather.24
  543.9 121.3 all-gather.28
  667.2 122.5 all-gather.26
  791.4 122.3 all-gather.30
  973.6 69.8 reduce-scatter.60
  1045.5 36.6 all-gather.44
  1084.2 37.1 all-gather.32
  1215.2 68.6 reduce-scatter.66
  1286.1 38.6 reduce-scatter.54
  1327.0 39.4 reduce-scatter.58
  1370.3 37.3 all-gather.36
  1409.8 37.1 all-gather.34
  1549.4 30.2 reduce-scatter.68
  1581.9 30.5 reduce-scatter.62
  1615.4 22.8 reduce-scatter.112
  1640.9 24.4 reduce-scatter.114
  1668.2 24.4 reduce-scatter.92
  1695.4 24.4 reduce-scatter.94
  1722.5 24.4 reduce-scatter.88
  1749.8 24.4 reduce-scatter.90
  1777.3 120.7 reduce-scatter.108
  1900.7 24.4 reduce-scatter.102
  1928.0 24.3 reduce-scatter.100
  1955.8 24.4 reduce-scatter.98
  1983.5 24.4 reduce-scatter.96
  2010.8 28.5 reduce-scatter.106
  2042.4 28.5 reduce-scatter.104
  2073.7 28.5 reduce-scatter.74
  2105.1 28.5 reduce-scatter.72
  2136.5 28.5 reduce-scatter.78
  2168.5 28.5 reduce-scatter.76
  2200.1 120.7 reduce-scatter.110
  2324.0 120.7 reduce-scatter.84
  2447.9 120.7 reduce-scatter.86
  2571.6 120.7 reduce-scatter.80
  2695.4 120.7 reduce-scatter.82
  2818.3 40.3 reduce-scatter.64
  2860.9 39.4 reduce-scatter.70
  2908.3 124.8 all-reduce.48
where the time goes:
time: 3070 us; the launch traced here: 3050 us
  waiting for transfers between devices  1760 us (57%)
  matrix products  407 us (13%)
  local copies, waits for them, and re-layouts  406 us (13%)
  other arithmetic  348 us (11%)
  blocking collectives  111 us (4%)
    unnamed x57, waiting for transfers between devices  256 us
    reduce_scatter x2, waiting for transfers between devices, local(): lax.psum_scatter(big_grads[5].astype(jnp.bfloat16), 'row', scatter_dimens...  241 us
    reduce_scatter x2, waiting for transfers between devices, local(): lax.psum_scatter(big_grads[6].astype(jnp.bfloat16), 'row', scatter_dimens...  235 us
    unnamed x608, local copies, waits for them, and re-layouts  132 us
    reduce_scatter x2, waiting for transfers between devices, local(): lax.psum_scatter(dot_plain(mixed_out, full_out), 'col', scatter_dimension...  131 us
    psum x1, waiting for transfers between devices, local(): lax.psum((first_sum, second_sum, widen(kernel_sum, DI, channel_start, 1),...  128 us
    all_gather x1, waiting for transfers between devices, fetch_weights(): lax.all_gather(expert_gate, 'row', axis=1, tiled=True)  116 us
    all_gather x1, waiting for transfers between devices, fetch_weights(): lax.all_gather(expert_down, 'row', axis=2, tiled=True)  116 us
  transfers between devices with their start and end apart: 47, of which 30 were waited for; matrix products, arithmetic and copies ran while one was open for 28% of the time, Pallas kernels for 0%

commit v1 on v0

v1 whole, which is shorter than its diff:
```python
import functools

import jax
import jax.numpy as jnp
from jax import lax
from jax.experimental import pallas as pl
from jax.experimental.pallas import tpu as pltpu
from jax.sharding import PartitionSpec as P

NS = 128
BLOCK = 256
CAP = 144
EPS = 1e-05
HEAD_ROWS = 16
LANES = 128
F32 = jnp.float32
BF16 = jnp.bfloat16
VMEM = pl.BlockSpec(memory_space=pltpu.VMEM)
VMEM_LIMIT = 56 * 1024 * 1024


def contract(left_op, right_op, left_dim, right_dim, precision=None):
    return lax.dot_general(
        left_op,
        right_op,
        (((left_dim,), (right_dim,)), ((), ())),
        preferred_element_type=F32,
        precision=precision,
    )


def dot_plain(left_op, right_op):
    return contract(left_op, right_op, 1, 0)


def dot_first(left_op, right_op):
    return contract(left_op, right_op, 0, 0)


def dot_last(left_op, right_op):
    return contract(left_op, right_op, 1, 1)


def silu_slope(values):
    logistic = jax.nn.sigmoid(values)
    return logistic * (1.0 + values * (1.0 - logistic))


def softplus(values):
    return jnp.maximum(values, 0.0) + jnp.log1p(jnp.exp(-jnp.abs(values)))


def shifts_back(current, before):
    joined = jnp.concatenate([before, current], axis=1)
    return [pltpu.roll(joined, step, 1)[:, LANES:] for step in (1, 2, 3)]


def load_block(ref, rows, block):
    cols = pl.ds(pl.multiple_of(block * BLOCK, BLOCK), BLOCK)
    current = ref[rows, cols]
    ahead = pl.multiple_of(jnp.maximum(block * BLOCK - LANES, 0), LANES)
    before = jnp.where(block > 0, ref[rows, pl.ds(ahead, LANES)], 0.0)
    return current, shifts_back(current, before)


def convolved(current, back, taps):
    return (
        taps[:, 4:5]
        + taps[:, 3:4] * current
        + taps[:, 2:3] * back[0]
        + taps[:, 1:2] * back[1]
        + taps[:, 0:1] * back[2]
    )


def conv_adjoint(adjoint, after, taps):
    joined = jnp.concatenate([adjoint, after], axis=1)
    width = joined.shape[1]
    total = taps[:, 3:4] * adjoint
    for step in (1, 2, 3):
        ahead = pltpu.roll(joined, width - step, 1)[:, :BLOCK]
        total = total + taps[:, 3 - step : 4 - step] * ahead
    return total


def lane_tile(columns):
    rows = columns[0].shape[0]
    lane = lax.broadcasted_iota(jnp.int32, (rows, LANES), 1)
    tile = jnp.zeros((rows, LANES), F32)
    for place, column in enumerate(columns):
        tile = jnp.where(lane == place, column, tile)
    return tile


def row_sum(values):
    return jnp.sum(values, axis=1, keepdims=True)


def decay_block(cum_row, cum_cols, head):
    lane = lax.broadcasted_iota(jnp.int32, cum_cols.shape, 1)
    cum_col = row_sum(jnp.where(lane == head, cum_cols, 0.0))
    place_j = lax.broadcasted_iota(jnp.int32, (BLOCK, BLOCK), 0)
    place_i = lax.broadcasted_iota(jnp.int32, (BLOCK, BLOCK), 1)
    return jnp.exp(jnp.where(place_j <= place_i, cum_row - cum_col, -1e30))


def step_rows(step_pre, head_params, step_s, cum_s, cum_t_s, blocks):
    step = softplus(step_pre + head_params[:, 0:1])
    step_s[...] = step
    log_decay = -(step * head_params[:, 1:2])
    place_j = lax.broadcasted_iota(jnp.int32, (BLOCK, BLOCK), 0)
    place_i = lax.broadcasted_iota(jnp.int32, (BLOCK, BLOCK), 1)
    upper = jnp.where(place_j <= place_i, 1.0, 0.0)
    for block in range(blocks):
        cols = slice(block * BLOCK, (block + 1) * BLOCK)
        cum = contract(log_decay[:, cols], upper, 1, 0, lax.Precision.HIGHEST)
        cum_s[:, cols] = cum
        cum_t_s[cols, :] = jnp.transpose(cum)


def score_blocks(io, scores_s, blocks):
    for block in range(blocks):
        cols = slice(block * BLOCK, (block + 1) * BLOCK)
        scores_s[block] = dot_first(io[:NS, cols], io[NS:, cols])


def block_cols(block):
    return pl.ds(pl.multiple_of(block * BLOCK, BLOCK), BLOCK)


def mixer_forward_kernel(
    heads,
    xn,
    wb,
    wc,
    wio,
    ws,
    wo,
    chan,
    io_taps,
    head_params,
    y,
    squares,
    branch,
    conv,
    io_pre,
    io,
    step_pre,
    starts,
    step_s,
    cum_s,
    cum_t_s,
    scores_s,
    z_s,
):
    length = xn.shape[0]
    blocks = length // BLOCK
    size = wb.shape[0] // heads
    step_pre[...] = dot_last(ws[...], xn[...])
    step_rows(step_pre[...], head_params[...], step_s, cum_s, cum_t_s, blocks)

    def project(block, carry):
        cols = block_cols(block)
        rows = xn[cols, :]
        io_pre[:, cols] = dot_last(wio[...], rows)
        branch[:, cols] = dot_last(wb[...], rows)
        conv[:, cols] = dot_last(wc[...], rows)
        return carry

    lax.fori_loop(0, blocks, project, 0)

    def io_step(at, carry):
        rows = pl.ds(pl.multiple_of((at // blocks) * 64, 64), 64)
        block = at % blocks
        current, back = load_block(io_pre, rows, block)
        io[rows, block_cols(block)] = jax.nn.silu(
            convolved(current, back, io_taps[rows, :])
        ).astype(BF16)
        return carry

    lax.fori_loop(0, blocks * (2 * NS // 64), io_step, 0)
    score_blocks(io, scores_s, blocks)
    squares[...] = jnp.zeros_like(squares)

    def head_step(head, carry):
        rows = pl.ds(pl.multiple_of(head * size, size), size)
        params = chan[rows, :]

        def block_step(block, state):
            cols = block_cols(block)
            current, back = load_block(conv, rows, block)
            x = jax.nn.silu(convolved(current, back, params))
            step_row = step_s[pl.ds(head, 1), cols]
            cum_row = cum_s[pl.ds(head, 1), cols]
            last = cum_row[:, BLOCK - 1 : BLOCK]
            mixing = (scores_s[block] * decay_block(cum_row, cum_t_s[cols, :], head)).astype(BF16)
            weighted = x * step_row
            starts[pl.ds(pl.multiple_of((head * blocks + block) * size, size), size), :] = state
            scanned = dot_plain(weighted.astype(BF16), mixing)
            scanned = scanned + dot_plain(state.astype(BF16), io[NS:, cols]) * jnp.exp(cum_row)
            scanned = scanned + params[:, 6:7] * x
            gated = scanned * jax.nn.silu(branch[rows, cols])
            squares[:, cols] += jnp.sum((gated * gated).reshape(size // 8, 8, BLOCK), axis=0)
            z_s[rows, cols] = (gated * params[:, 5:6]).astype(BF16)
            to_end = (weighted * jnp.exp(last - cum_row)).astype(BF16)
            return state * jnp.exp(last) + dot_last(to_end, io[:NS, cols])

        lax.fori_loop(0, blocks, block_step, jnp.zeros((size, NS), F32))
        return carry

    lax.fori_loop(0, heads, head_step, 0)

    def out_step(block, carry):
        cols = block_cols(block)
        y[cols, :] = dot_first(z_s[:, cols], wo[...]).astype(BF16)
        return carry

    lax.fori_loop(0, blocks, out_step, 0)


def mixer_forward(xn, wb, wc, wio, ws, wo, chan, io_taps, head_params, heads):
    length, width = xn.shape
    share = wb.shape[0]
    blocks = length // BLOCK
    size = share // heads
    shape = jax.ShapeDtypeStruct
    flops = 2 * length * width * (3 * share + 2 * NS + HEAD_ROWS) + 10**8
    return pl.pallas_call(
        functools.partial(mixer_forward_kernel, heads),
        out_shape=(
            shape((length, width), BF16),
            shape((8, length), F32),
            shape((share, length), F32),
            shape((share, length), F32),
            shape((2 * NS, length), F32),
            shape((2 * NS, length), BF16),
            shape((HEAD_ROWS, length), F32),
            shape((heads * blocks * size, NS), F32),
        ),
        in_specs=[VMEM] * 9,
        out_specs=[VMEM] * 8,
        scratch_shapes=[
            pltpu.VMEM((HEAD_ROWS, length), F32),
            pltpu.VMEM((HEAD_ROWS, length), F32),
            pltpu.VMEM((length, HEAD_ROWS), F32),
            pltpu.VMEM((blocks, BLOCK, BLOCK), F32),
            pltpu.VMEM((share, length), BF16),
        ],
        compiler_params=pltpu.CompilerParams(vmem_limit_bytes=VMEM_LIMIT),
        cost_estimate=pl.CostEstimate(
            flops=4 * flops, bytes_accessed=4 * 2 * length * width, transcendentals=10**7
        ),
    )(xn, wb, wc, wio, ws, wo, chan, io_taps, head_params)


def mixer_backward_kernel(
    heads,
    d_res,
    scale_rows,
    xn,
    wb,
    wc,
    wio,
    ws,
    wo,
    chan,
    io_taps,
    head_params,
    branch,
    conv,
    io_pre,
    io,
    step_pre,
    starts,
    first_part,
    gain_part,
    mixed,
    d_branch,
    d_conv,
    d_io,
    d_step,
    chan_grad,
    io_grad,
    head_grad,
    step_s,
    cum_s,
    cum_t_s,
    scores_s,
    d_scores_s,
    d_mixed_s,
    d_io_s,
    d_cum_s,
    d_size_s,
    adjoint_s,
):
    length = xn.shape[0]
    blocks = length // BLOCK
    size = wb.shape[0] // heads
    step_rows(step_pre[...], head_params[...], step_s, cum_s, cum_t_s, blocks)
    score_blocks(io, scores_s, blocks)
    d_scores_s[...] = jnp.zeros_like(d_scores_s)
    d_io_s[...] = jnp.zeros_like(d_io_s)
    d_cum_s[...] = jnp.zeros_like(d_cum_s)
    d_size_s[...] = jnp.zeros_like(d_size_s)
    chan_grad[...] = jnp.zeros_like(chan_grad)
    io_grad[...] = jnp.zeros_like(io_grad)
    adjoint_s[:, length:] = jnp.zeros((adjoint_s.shape[0], LANES), F32)

    def project(block, carry):
        cols = block_cols(block)
        d_mixed_s[:, cols] = dot_last(wo[...], d_res[cols, :])
        return carry

    lax.fori_loop(0, blocks, project, 0)

    def head_step(head, carry):
        rows = pl.ds(pl.multiple_of(head * size, size), size)
        params = chan[rows, :]

        def block_step(reverse, d_state):
            block = blocks - 1 - reverse
            cols = block_cols(block)
            state = starts[pl.ds(pl.multiple_of((head * blocks + block) * size, size), size), :]
            state_low = state.astype(BF16)
            d_state_low = d_state.astype(BF16)
            write_rows = io[:NS, cols]
            read_rows = io[NS:, cols]
            step_row = step_s[pl.ds(head, 1), cols]
            cum_row = cum_s[pl.ds(head, 1), cols]
            last = cum_row[:, BLOCK - 1 : BLOCK]
            decays = decay_block(cum_row, cum_t_s[cols, :], head)
            mixing = (scores_s[block] * decays).astype(BF16)
            current, back = load_block(conv, rows, block)
            conv_act = convolved(current, back, params)
            logistic = jax.nn.sigmoid(conv_act)
            x = conv_act * logistic
            slope = logistic * (1.0 + conv_act * (1.0 - logistic))
            weighted = x * step_row
            weighted_low = weighted.astype(BF16)
            grown = jnp.exp(cum_row)
            within = dot_plain(weighted_low, mixing)
            carried = dot_plain(state_low, read_rows) * grown
            scanned = within + carried + params[:, 6:7] * x

            inverse_rms = scale_rows[0:1, cols]
            gate_in = branch[rows, cols]
            gate_logistic = jax.nn.sigmoid(gate_in)
            gate_out = gate_in * gate_logistic
            gated = scanned * gate_out
            d_mixed = d_mixed_s[rows, cols]
            gain = params[:, 5:6]
            mixed[rows, cols] = (gated * inverse_rms * gain).astype(BF16)
            d_gated = inverse_rms * (d_mixed * gain) - gated * scale_rows[1:2, cols]
            d_gain = row_sum(d_mixed * gated * inverse_rms)
            d_scanned = d_gated * gate_out
            d_branch[rows, cols] = (
                d_gated * scanned * (gate_logistic * (1.0 + gate_in * (1.0 - gate_logistic)))
            ).astype(BF16)
            d_low = d_scanned.astype(BF16)
            d_skip = row_sum(d_scanned * x)

            d_within = dot_last(d_low, mixing)
            shrunk = jnp.exp(last - cum_row)
            d_fed = dot_plain(d_state_low, write_rows) * shrunk
            d_weighted = d_within + d_fed
            d_scores_s[block] += dot_first(weighted_low, d_low) * decays
            d_grown = (d_scanned * grown).astype(BF16)
            fed = (weighted * shrunk).astype(BF16)
            d_io_s[NS:, cols] += dot_first(state_low, d_grown)
            d_io_s[:NS, cols] += dot_first(d_state_low, fed)
            d_before = d_state * jnp.exp(last) + dot_last(d_grown, read_rows)

            fed_terms = weighted * d_fed
            d_cum = jnp.sum(
                d_low.astype(F32) * within
                - weighted_low.astype(F32) * d_within
                + d_scanned * carried
                - fed_terms,
                axis=0,
                keepdims=True,
            )
            at_end = jnp.sum(row_sum(fed_terms), axis=0, keepdims=True) + jnp.exp(last) * jnp.sum(
                row_sum(d_state * state), axis=0, keepdims=True
            )
            lane = lax.broadcasted_iota(jnp.int32, (1, BLOCK), 1)
            d_cum_s[pl.ds(head, 1), cols] = d_cum + jnp.where(lane == BLOCK - 1, at_end, 0.0)
            d_size_s[pl.ds(head, 1), cols] = jnp.sum(d_weighted * x, axis=0, keepdims=True)

            d_act = (d_weighted * step_row + params[:, 6:7] * d_scanned) * slope
            adjoint_s[:, cols] = d_act
            after = adjoint_s[:, pl.ds(pl.multiple_of((block + 1) * BLOCK, BLOCK), LANES)]
            d_conv[rows, cols] = conv_adjoint(d_act, after, params).astype(BF16)
            chan_grad[rows, :] += lane_tile(
                [
                    row_sum(d_act * back[2]),
                    row_sum(d_act * back[1]),
                    row_sum(d_act * back[0]),
                    row_sum(d_act * current),
                    row_sum(d_act),
                    d_gain,
                    d_skip,
                ]
            )
            return d_before

        lax.fori_loop(0, blocks, block_step, jnp.zeros((size, NS), F32))
        return carry

    lax.fori_loop(0, heads, head_step, 0)

    def scores_step(block, carry):
        cols = block_cols(block)
        d_scores = d_scores_s[block].astype(BF16)
        d_io_s[NS:, cols] += dot_plain(io[:NS, cols], d_scores)
        d_io_s[:NS, cols] += dot_last(io[NS:, cols], d_scores)
        return carry

    lax.fori_loop(0, blocks, scores_step, 0)

    def io_step(at, carry):
        rows = pl.ds(pl.multiple_of((at // blocks) * 64, 64), 64)
        block = blocks - 1 - at % blocks
        cols = block_cols(block)
        taps = io_taps[rows, :]
        current, back = load_block(io_pre, rows, block)
        d_act = d_io_s[rows, cols] * silu_slope(convolved(current, back, taps))
        adjoint_s[:64, cols] = d_act
        after = adjoint_s[:64, pl.ds(pl.multiple_of((block + 1) * BLOCK, BLOCK), LANES)]
        d_io[rows, cols] = conv_adjoint(d_act, after, taps).astype(BF16)
        io_grad[rows, :] += lane_tile(
            [
                row_sum(d_act * back[2]),
                row_sum(d_act * back[1]),
                row_sum(d_act * back[0]),
                row_sum(d_act * current),
                row_sum(d_act),
            ]
        )
        return carry

    lax.fori_loop(0, blocks * (2 * NS // 64), io_step, 0)

    place_j = lax.broadcasted_iota(jnp.int32, (BLOCK, BLOCK), 0)
    place_i = lax.broadcasted_iota(jnp.int32, (BLOCK, BLOCK), 1)
    lower = jnp.where(place_j >= place_i, 1.0, 0.0)
    rate = head_params[:, 1:2]
    decay_grad = jnp.zeros((HEAD_ROWS, 1), F32)
    offset_grad = jnp.zeros((HEAD_ROWS, 1), F32)
    for block in range(blocks):
        cols = slice(block * BLOCK, (block + 1) * BLOCK)
        d_log = contract(d_cum_s[:, cols], lower, 1, 0, lax.Precision.HIGHEST)
        decay_grad = decay_grad - row_sum(step_s[:, cols] * rate * d_log)
        d_size = d_size_s[:, cols] - rate * d_log
        d_pre = d_size * jax.nn.sigmoid(step_pre[:, cols] + head_params[:, 0:1])
        offset_grad = offset_grad + row_sum(d_pre)
        d_step[:, cols] = d_pre.astype(BF16)
    head_grad[...] = lane_tile([decay_grad, offset_grad])
    gain_part[...] = jnp.zeros_like(gain_part)

    def first_step(block, carry):
        cols = block_cols(block)
        part = (
            dot_first(d_branch[:, cols], wb[...])
            + dot_first(d_conv[:, cols], wc[...])
            + dot_first(d_io[:, cols], wio[...])
            + dot_first(d_step[:, cols], ws[...])
        )
        first_part[cols, :] = part.astype(BF16)
        product = part * xn[cols, :].astype(F32)
        gain_part[...] += jnp.sum(product.reshape(BLOCK // 8, 8, -1), axis=0)
        return carry

    lax.fori_loop(0, blocks, first_step, 0)


def mixer_backward(d_res, scale_rows, xn, weights, saved, heads):
    length, width = xn.shape
    share = weights[0].shape[0]
    blocks = length // BLOCK
    size = share // heads
    shape = jax.ShapeDtypeStruct
    flops = 2 * length * width * (3 * share + 2 * NS + HEAD_ROWS) + 10**8
    return pl.pallas_call(
        functools.partial(mixer_backward_kernel, heads),
        out_shape=(
            shape((length, width), BF16),
            shape((8, width), F32),
            shape((share, length), BF16),
            shape((share, length), BF16),
            shape((share, length), BF16),
            shape((2 * NS, length), BF16),
            shape((HEAD_ROWS, length), BF16),
            shape((share, LANES), F32),
            shape((2 * NS, LANES), F32),
            shape((HEAD_ROWS, LANES), F32),
        ),
        in_specs=[VMEM] * 17,
        out_specs=[VMEM] * 10,
        scratch_shapes=[
            pltpu.VMEM((HEAD_ROWS, length), F32),
            pltpu.VMEM((HEAD_ROWS, length), F32),
            pltpu.VMEM((length, HEAD_ROWS), F32),
            pltpu.VMEM((blocks, BLOCK, BLOCK), F32),
            pltpu.VMEM((blocks, BLOCK, BLOCK), F32),
            pltpu.VMEM((share, length), F32),
            pltpu.VMEM((2 * NS, length), F32),
            pltpu.VMEM((HEAD_ROWS, length), F32),
            pltpu.VMEM((HEAD_ROWS, length), F32),
            pltpu.VMEM((size, length + LANES), F32),
        ],
        compiler_params=pltpu.CompilerParams(vmem_limit_bytes=VMEM_LIMIT),
        cost_estimate=pl.CostEstimate(
            flops=8 * flops, bytes_accessed=8 * 2 * length * width, transcendentals=10**7
        ),
    )(d_res, scale_rows, xn, *weights, *saved)


def row_norm(values, scale_gain):
    return values * lax.rsqrt(jnp.mean(values * values, axis=1, keepdims=True) + EPS) * scale_gain


def norm_adjoint(values, scale_gain, cotangent):
    inverse = lax.rsqrt(jnp.mean(values * values, axis=1, keepdims=True) + EPS)
    unit = values * inverse
    scaled = cotangent * scale_gain
    back = inverse * (scaled - unit * jnp.mean(scaled * unit, axis=1, keepdims=True))
    return back, jnp.sum(cotangent * unit, axis=0)


def local(
    layer_input,
    out_grad,
    seq_lengths,
    routes,
    route_gates,
    first_gain,
    gate_branch_proj,
    conv_in_proj,
    state_io_proj,
    step_proj,
    conv_kernel,
    conv_offset,
    state_conv_kernel,
    state_conv_offset,
    decay_log,
    step_offset,
    skip_scale,
    mixer_gain,
    out_proj,
    second_gain,
    expert_gate,
    expert_up,
    expert_down,
    shared_gate,
    shared_up,
    shared_down,
):
    rows_n = lax.axis_size("row")
    cols_n = lax.axis_size("col")
    row_index = lax.axis_index("row")
    col_index = lax.axis_index("col")
    micro_count, own_count, width = layer_input.shape
    length = own_count * cols_n
    local_experts, depth, hidden_width = expert_gate.shape
    share = conv_kernel.shape[1]
    heads = decay_log.shape[0]
    size = share // heads
    inner = share * cols_n
    io_width = state_conv_kernel.shape[1]
    shared_width = shared_gate.shape[1]
    per_device = max(1, local_experts // rows_n)
    split = max(1, rows_n // local_experts)
    part_width = hidden_width // split
    slots = per_device * CAP

    def swap(values, k):
        if k == 0:
            return values
        return lax.ppermute(values, "row", [(i, i ^ k) for i in range(rows_n)])

    def peer(k):
        return row_index ^ k

    def unit_of(member):
        return (member * per_device) // split, (member % split) * part_width

    def gather_width(pack):
        full = jnp.zeros((pack.shape[0], width), pack.dtype)
        for k in range(rows_n):
            full = lax.dynamic_update_slice(full, swap(pack, k), (0, peer(k) * depth))
        return full

    def add_shares(full):
        total = None
        for k in range(rows_n):
            part = lax.dynamic_slice(full, (0, peer(k) * depth), (full.shape[0], depth))
            part = swap(part, k).astype(F32)
            total = part if total is None else total + part
        return total

    micro = range(micro_count)
    own_rows = [layer_input[m].astype(F32) for m in micro]
    normed = [
        lax.all_gather(row_norm(own_rows[m], first_gain).astype(BF16), "col", axis=0, tiled=True)
        for m in micro
    ]

    io_gathered = lax.all_gather(
        jnp.concatenate(
            [state_io_proj.astype(F32), state_conv_kernel, state_conv_offset[None, :]], axis=0
        ),
        "col",
        axis=1,
        tiled=True,
    )
    step_rows_t = jnp.pad(step_proj.T, ((0, HEAD_ROWS - heads), (0, 0)))
    in_full = gather_width(
        jnp.concatenate(
            [gate_branch_proj.T, conv_in_proj.T, io_gathered[:depth].astype(BF16).T, step_rows_t],
            axis=0,
        )
    )
    out_full = gather_width(
        jnp.concatenate([out_proj, shared_gate.T, shared_up.T, shared_down], axis=0)
    )
    wb, wc = in_full[:share], in_full[share : 2 * share]
    wio = in_full[2 * share : 2 * share + 2 * NS]
    ws = in_full[2 * share + 2 * NS :]
    wo = out_full[:share]
    shared_in = out_full[share : share + 2 * shared_width]
    shared_out = out_full[share + 2 * shared_width :]
    chan = jnp.concatenate(
        [
            conv_kernel.T,
            conv_offset[:, None],
            mixer_gain[:, None],
            jnp.repeat(skip_scale, size)[:, None],
            jnp.zeros((share, 1), F32),
        ],
        axis=1,
    )
    io_taps = jnp.pad(io_gathered[depth:].T, ((0, 0), (0, 3)))
    head_params = jnp.pad(
        jnp.stack([step_offset, jnp.exp(decay_log)], axis=1), ((0, HEAD_ROWS - heads), (0, 6))
    )
    weights = (wb, wc, wio, ws, wo, chan, io_taps, head_params)

    gate_up = jnp.zeros((per_device, width, 2 * part_width), BF16)
    down = jnp.zeros((per_device, part_width, width), BF16)
    for k in range(rows_n):
        first, hidden_at = unit_of(peer(k))
        cut = (first, 0, hidden_at)
        sizes = (per_device, depth, part_width)
        up_part = jnp.concatenate(
            [
                lax.dynamic_slice(expert_gate, cut, sizes),
                lax.dynamic_slice(expert_up, cut, sizes),
            ],
            axis=2,
        )
        down_part = lax.dynamic_slice(
            expert_down, (first, hidden_at, 0), (per_device, part_width, depth)
        )
        at = peer(k) * depth
        gate_up = lax.dynamic_update_slice(gate_up, swap(up_part, k), (0, at, 0))
        down = lax.dynamic_update_slice(down, swap(down_part, k), (0, 0, at))

    place_j = lax.broadcasted_iota(jnp.int32, (length, length), 0)
    place_i = lax.broadcasted_iota(jnp.int32, (length, length), 1)
    upper = (place_j <= place_i).astype(BF16)
    expert_ids = col_index * local_experts + jnp.arange(local_experts, dtype=jnp.int32)

    def dispatch(m):
        hit = routes[m].T[None] == expert_ids[:, None, None]
        mask = jnp.any(hit, axis=1)
        gates = jnp.sum(jnp.where(hit, route_gates[m].T[None], 0.0), axis=1)
        rank = dot_plain(mask.astype(BF16), upper).astype(jnp.int32) - 1
        slot = jnp.where(mask, rank, -1)
        picks, slot_gates = [], []
        for k in range(rows_n):
            first, _ = unit_of(peer(k))
            slot_k = lax.dynamic_slice(slot, (first, 0), (per_device, length))
            gates_k = lax.dynamic_slice(gates, (first, 0), (per_device, length))
            chosen = slot_k[:, None, :] == jnp.arange(CAP, dtype=jnp.int32)[None, :, None]
            slot_gates.append(
                jnp.sum(jnp.where(chosen, gates_k[:, None, :], 0.0), axis=2).reshape(slots, 1)
            )
            picks.append(chosen.astype(BF16).reshape(slots, length))
        return picks, slot_gates

    def stack_rows(parts):
        return jnp.stack(
            [part.reshape(per_device, CAP, width) for part in parts], axis=1
        ).reshape(per_device, rows_n * CAP, width)

    def send_back(rows):
        rows = rows.astype(BF16).reshape(per_device, rows_n, CAP, width)
        return [swap(rows[:, k].reshape(slots, width), k) for k in range(rows_n)]

    outputs, input_grads = [], []
    dense_grads, gate_up_grads, down_grads = [], [], []
    all_sums, row_sums = [], []
    for m in micro:
        positions = col_index * own_count + jnp.arange(own_count)
        valid = (positions < seq_lengths[m, 0])[:, None]
        own_cot = jnp.where(valid, out_grad[m], jnp.zeros_like(out_grad[m]))
        cot = lax.all_gather(own_cot, "col", axis=0, tiled=True)
        xn = normed[m]
        y, squares, *saved = mixer_forward(xn, *weights, heads)
        mean_square = lax.psum(jnp.sum(squares, axis=0), "col") / inner
        inverse_rms = lax.rsqrt(mean_square + EPS)
        y_own = lax.psum_scatter(y, "col", scatter_dimension=0, tiled=True).astype(F32)
        own_rms = lax.dynamic_slice(inverse_rms, (col_index * own_count,), (own_count,))
        residual = own_rows[m] + own_rms[:, None] * y_own
        second = lax.all_gather(
            row_norm(residual, second_gain).astype(BF16), "col", axis=0, tiled=True
        )

        picks, slot_gates = dispatch(m)
        cot_rows = stack_rows(
            [
                swap((dot_plain(picks[k], cot) * slot_gates[k]).astype(BF16), k)
                for k in range(rows_n)
            ]
        )
        token_rows = stack_rows(
            [swap(dot_plain(picks[k], second).astype(BF16), k) for k in range(rows_n)]
        )
        pre = jnp.einsum("ecd,edh->ech", token_rows, gate_up, preferred_element_type=F32)
        gate_pre, up_pre = pre[..., :part_width], pre[..., part_width:]
        hidden = (jax.nn.silu(gate_pre) * up_pre).astype(BF16)
        d_hidden = jnp.einsum("ecd,ehd->ech", cot_rows, down, preferred_element_type=F32)
        d_pre = jnp.concatenate(
            [
                (d_hidden * up_pre * silu_slope(gate_pre)).astype(BF16),
                (d_hidden * jax.nn.silu(gate_pre)).astype(BF16),
            ],
            axis=2,
        )
        d_rows = jnp.einsum("ech,edh->ecd", d_pre, gate_up, preferred_element_type=F32)
        out_rows = jnp.einsum("ech,ehd->ecd", hidden, down, preferred_element_type=F32)
        gate_up_grads.append(
            jnp.einsum("ecd,ech->edh", token_rows, d_pre, preferred_element_type=F32)
        )
        down_grads.append(
            jnp.einsum("ech,ecd->ehd", hidden, cot_rows, preferred_element_type=F32)
        )

        shared_pre = dot_last(second, shared_in)
        shared_gate_pre = shared_pre[:, :shared_width]
        shared_up_pre = shared_pre[:, shared_width:]
        shared_hidden = (jax.nn.silu(shared_gate_pre) * shared_up_pre).astype(BF16)
        d_shared = dot_last(cot, shared_out)
        d_shared_pre = jnp.concatenate(
            [
                (d_shared * shared_up_pre * silu_slope(shared_gate_pre)).astype(BF16),
                (d_shared * jax.nn.silu(shared_gate_pre)).astype(BF16),
            ],
            axis=1,
        )

        pick_all = jnp.concatenate(picks, axis=0)
        back_rows = jnp.concatenate(send_back(d_rows), axis=0)
        second_part = dot_first(pick_all, back_rows) + dot_plain(d_shared_pre, shared_in)
        second_share = lax.psum_scatter(
            second_part.astype(BF16), "col", scatter_dimension=0, tiled=True
        ).astype(F32)
        residual_back, second_gain_grad = norm_adjoint(residual, second_gain, second_share)
        residual_grad = own_cot.astype(F32) + residual_back
        residual_low = residual_grad.astype(BF16)
        d_res = lax.all_gather(residual_low, "col", axis=0, tiled=True)
        cross = lax.all_gather(
            jnp.sum(residual_low.astype(F32) * y_own, axis=1), "col", axis=0, tiled=True
        )
        cube = inverse_rms * inverse_rms * inverse_rms * cross / inner
        scale_rows = jnp.pad(jnp.stack([inverse_rms, cube]), ((0, 6), (0, 0)))
        (
            first_part,
            gain_part,
            mixed,
            d_branch,
            d_conv,
            d_io,
            d_step,
            chan_grad,
            io_grad,
            head_grad,
        ) = mixer_backward(d_res, scale_rows, xn, weights, saved, heads)
        first_share = lax.psum_scatter(
            first_part, "col", scatter_dimension=0, tiled=True
        ).astype(F32)
        rows_back, _ = norm_adjoint(own_rows[m], first_gain, first_share)
        input_grads.append(residual_grad + rows_back)

        out_back = jnp.concatenate(
            [
                (gate * rows.astype(F32)).astype(BF16)
                for gate, rows in zip(slot_gates, send_back(out_rows))
            ],
            axis=0,
        )
        branch_part = dot_first(pick_all, out_back) + dot_plain(shared_hidden, shared_out)
        branch_share = lax.psum_scatter(
            branch_part.astype(BF16), "col", scatter_dimension=0, tiled=True
        ).astype(F32)
        outputs.append((residual + branch_share).astype(BF16))

        dense_grads.append(
            (
                dot_plain(d_branch, xn),
                dot_plain(d_conv, xn),
                dot_plain(d_io, xn),
                dot_plain(d_step, xn),
                dot_plain(mixed, d_res),
                dot_first(d_shared_pre, second),
                dot_first(shared_hidden, cot),
            )
        )
        all_sums.append(
            (jnp.sum(gain_part, axis=0) / first_gain, second_gain_grad, io_grad[:, :5].reshape(-1))
        )
        row_sums.append(
            (
                chan_grad[:, :6].reshape(-1),
                jnp.sum(chan_grad[:, 6].reshape(heads, size), axis=1),
                head_grad[:heads, 0],
                head_grad[:heads, 1],
            )
        )

    def total_of(parts):
        return jax.tree.map(lambda *terms: functools.reduce(jnp.add, terms), *parts)

    gate_up_total = total_of(gate_up_grads).astype(BF16)
    down_total = total_of(down_grads).astype(BF16)
    expert_gate_grad = jnp.zeros(expert_gate.shape, F32)
    expert_up_grad = jnp.zeros(expert_up.shape, F32)
    expert_down_grad = jnp.zeros(expert_down.shape, F32)
    for k in range(rows_n):
        at = peer(k) * depth
        first, hidden_at = unit_of(peer(k))
        part = swap(
            lax.dynamic_slice(gate_up_total, (0, at, 0), (per_device, depth, 2 * part_width)), k
        ).astype(F32)
        place = (first, 0, hidden_at)
        expert_gate_grad = lax.dynamic_update_slice(expert_gate_grad, part[..., :part_width], place)
        expert_up_grad = lax.dynamic_update_slice(expert_up_grad, part[..., part_width:], place)
        part = swap(
            lax.dynamic_slice(down_total, (0, 0, at), (per_device, part_width, depth)), k
        ).astype(F32)
        expert_down_grad = lax.dynamic_update_slice(expert_down_grad, part, (first, hidden_at, 0))

    dense = add_shares(jnp.concatenate(total_of(dense_grads), axis=0).astype(BF16))
    ends = []
    at = 0
    for rows in (share, share, 2 * NS, HEAD_ROWS, share, 2 * shared_width, shared_width):
        ends.append(dense[at : at + rows])
        at += rows
    branch_grad, conv_grad, io_proj_part, step_grad, out_grad_sum, shared_in_grad, down_grad = ends
    io_proj_grad = lax.psum_scatter(io_proj_part, "col", scatter_dimension=0, tiled=True)

    all_total = total_of(all_sums)
    row_total = total_of(row_sums)
    sums = lax.psum(jnp.concatenate(all_total + row_total), "row")
    all_count = sum(part.shape[0] for part in all_total)
    all_values = lax.psum(sums[:all_count], "col")
    first_gain_grad = all_values[:width]
    second_gain_grad = all_values[width : 2 * width]
    io_values = lax.dynamic_slice(
        all_values[2 * width :].reshape(2 * NS, 5), (col_index * io_width, 0), (io_width, 5)
    )
    chan_values = sums[all_count : all_count + 6 * share].reshape(share, 6)
    head_values = sums[all_count + 6 * share :]
    return (
        jnp.stack(outputs),
        jnp.stack(input_grads),
        first_gain_grad,
        branch_grad.T,
        conv_grad.T,
        io_proj_grad.T,
        step_grad[:heads].T,
        chan_values[:, :4].T,
        chan_values[:, 4],
        io_values[:, :4].T,
        io_values[:, 4],
        head_values[heads : 2 * heads],
        head_values[2 * heads :],
        head_values[:heads],
        chan_values[:, 5],
        out_grad_sum,
        second_gain_grad,
        expert_gate_grad,
        expert_up_grad,
        expert_down_grad,
        shared_in_grad[:shared_width].T,
        shared_in_grad[shared_width:].T,
        down_grad,
    )


def solution(mesh):
    both = P(None, ("row", "col"), None)
    placed = (
        both,
        both,
        P(None, "row"),
        P(None, "row", None),
        P(None, "row", None),
        P(),
        P("row", "col"),
        P("row", "col"),
        P("row", "col"),
        P("row", "col"),
        P(None, "col"),
        P("col"),
        P(None, "col"),
        P("col"),
        P("col"),
        P("col"),
        P("col"),
        P("col"),
        P("col", "row"),
        P(),
        P("col", "row", None),
        P("col", "row", None),
        P("col", None, "row"),
        P("row", "col"),
        P("row", "col"),
        P("col", "row"),
    )
    return jax.shard_map(
        local,
        mesh=mesh,
        in_specs=placed,
        out_specs=(both, both, P()) + placed[6:19] + (P(),) + placed[20:],
        check_vma=False,
    )
```

time: 3070 us -> 1210 us (0.39)
  waiting for transfers between devices: 1760 us -> 479 us
  local copies, waits for them, and re-layouts: 406 us -> 112 us
  other arithmetic: 348 us -> 72.7 us
  matrix products: 407 us -> 171 us
  Pallas kernels: 0 us -> 150 us
  starting transfers between devices: 3.89 us -> 57.5 us
  blocking collectives: 111 us -> 145 us
    reduce_scatter x22 -> x9, waiting for transfers between devices: 940 us -> 100 us  [the longest x2 48.6 us: local(): lax.psum_scatter(second_part.astype(BF16), 'col', scatter_dimension=0, ti...]
    all_gather x14 -> x8, waiting for transfers between devices: 435 us -> 27.6 us  [the longest x2 27.6 us: local(): d_res = lax.all_gather(residual_low, 'col', axis=0, tiled=True)]
    ppermute x0 -> x45, waiting for transfers between devices: none -> 349 us  [swap(): return lax.ppermute(values, 'row', [(i, i ^ k) for i in range(rows_n)])]
    unnamed x57 -> x17, waiting for transfers between devices: 256 us -> 1.97 us
    dot_general x90 -> x56, matrix products: 407 us -> 171 us  [the longest x44 102 us: contract(): lax.dot_general(left_op, right_op, (((left_dim,), (right_dim,)), ((), ())...]
    pallas_call x0 -> x4, Pallas kernels: none -> 150 us  [the longest x2 94 us: mixer_backward(): pl.pallas_call(functools.partial(mixer_backward_kernel, heads), out_shape...]
    psum x1 -> x0, waiting for transfers between devices: 128 us -> none  [local(): lax.psum((first_sum, second_sum, widen(kernel_sum, DI, channel_start, 1),...]
    unnamed x608 -> x365, local copies, waits for them, and re-layouts: 132 us -> 26 us
  transfers between devices with their start and end apart: 47 -> 62, of which waited for: 30 -> 20; matrix products, arithmetic and copies ran while one was open for 28% -> 27% of each run, Pallas kernels for 0% -> 12%
where the time goes in v1:
time: 1210 us; the launch traced here: 1200 us
  waiting for transfers between devices  479 us (40%)
  matrix products  171 us (14%)
  Pallas kernels  150 us (12%)
  blocking collectives  145 us (12%)
  local copies, waits for them, and re-layouts  112 us (9%)
  other arithmetic  72.7 us (6%)
  starting transfers between devices  57.5 us (5%)
  between operations  16.4 us (1%)
    ppermute x45, waiting for transfers between devices, swap(): return lax.ppermute(values, 'row', [(i, i ^ k) for i in range(rows_n)])  349 us
    dot_general x44, matrix products, contract(): lax.dot_general(left_op, right_op, (((left_dim,), (right_dim,)), ((), ())...  102 us
    pallas_call x2, Pallas kernels, mixer_backward(): pl.pallas_call(functools.partial(mixer_backward_kernel, heads), out_shape...  94 us
    psum x1, blocking collectives, local(): sums = lax.psum(jnp.concatenate(all_total + row_total), 'row')  66.9 us
    ppermute x45, starting transfers between devices, swap(): return lax.ppermute(values, 'row', [(i, i ^ k) for i in range(rows_n)])  56.4 us
    pallas_call x2, Pallas kernels, mixer_forward(): pl.pallas_call(functools.partial(mixer_forward_kernel, heads), out_shape=...  56 us
    reduce_scatter x2, waiting for transfers between devices, local(): lax.psum_scatter(second_part.astype(BF16), 'col', scatter_dimension=0, ti...  48.6 us
    reduce_scatter x2, waiting for transfers between devices, local(): lax.psum_scatter(y, 'col', scatter_dimension=0, tiled=True).astype(F32)  32.8 us
  transfers between devices with their start and end apart: 62, of which 20 were waited for; matrix products, arithmetic and copies ran while one was open for 27% of the time, Pallas kernels for 12%

profile of v1, /device:TPU:0, one launch (start us, length us, event | category | flops | bytes accessed | tf_op | source)
XLA Modules:
  0.0 1204.1 jit_solution(17705000007524799956)
XLA Ops:
  18.9 17.6 %all_gather.34 = f32[389,256]{0,1:T(8,128)S(1)} all-gather(f32[389,32]{0,1:T(8,128)S(1)} %pad_maximum_fusion.22), channel_id=1, replica_groups=mesh['row'=4,'col'=8] {'col'}, dimensions={1}, use_global_device_ids=true | all-gather | bytes 448128 | tf_op jit(solution)/shard_map/all_gather | solution.py:608
  48.4 54.2 %collective-permute-done.4 = bf16[768,384]{1,0:T(8,128)(2,1)} collective-permute-done((bf16[768,384]{1,0:T(8,128)(2,1)}, bf16[768,384]{1,0:T(8,128)(2,1)}, u32[]{:S(2)}, u32[]{:S(2)}) %collective-permute-start.4) | collective-permute-done | bytes 589856 | tf_op jit(solution)/shard_map/ppermute | solution.py:579
  117.8 28.0 %shard_map.425 = (bf16[1024,1536]{1,0:T(8,128)(2,1)}, f32[8,1024]{1,0:T(8,128)}, f32[384,1024]{1,0:T(8,128)}, f32[384,1024]{1,0:T(8,128)}, f32[256,1024]{1,0:T(8...) custom-call(bf16[1024,1536]{1,0:T(8,128)(2,1)} %all-gather.11.cloned.1.call-done.xn, ...), custom_call_target="tpu_custom_call" | custom-call | flops 18318065664 | bytes 12582912 | tf_op jit(solution)/shard_map/pallas_call | solution.py:228
  145.9 28.0 %shard_map.426 = (bf16[1024,1536]{1,0:T(8,128)(2,1)}, f32[8,1024]{1,0:T(8,128)}, f32[384,1024]{1,0:T(8,128)}, f32[384,1024]{1,0:T(8,128)}, f32[256,1024]{1,0:T(8...) custom-call(bf16[1024,1536]{1,0:T(8,128)(2,1)} %all-gather.15.cloned.1.call-done.xn, ...), custom_call_target="tpu_custom_call" | custom-call | flops 18318065664 | bytes 12582912 | tf_op jit(solution)/shard_map/pallas_call | solution.py:228
  179.3 16.4 %all-reduce.5 = (f32[1024]{0:T(1024)S(1)}, f32[1024]{0:T(1024)S(1)}) all-reduce(f32[1024]{0:T(1024)S(1)} %reduce_sum.269, f32[1024]{0:T(1024)S(1)} %reduce_sum.277), channel_id=1, replica_groups=mesh['row'=4,'col'=8] {'col'}, use_global_device_ids=true, to_apply=%region_2.3 | all-reduce | flops 2048 | bytes 16384 | tf_op jit(solution)/shard_map/psum | solution.py:710
  197.1 32.8 %reduce-scatter.14.cloned.1.call-done = bf16[128,1536]{1,0:T(8,128)(2,1)} async-done(((bf16[1024,1536]{1,0:T(8,128)(2,1)}), bf16[128,1536]{1,0:T(8,128)(2,1)}) %reduce-scatter.14.cloned.1.call-update) | async-done | bytes 393232 | tf_op jit(solution)/shard_map/reduce_scatter | solution.py:712
  234.2 4.2 constant_dynamic-slice_fusion.24
  254.5 69.8 %collective-permute-done.12 = bf16[2,512,384]{2,1,0:T(8,128)(2,1)} collective-permute-done((bf16[2,512,384]{2,1,0:T(8,128)(2,1)}, bf16[2,512,384]{2,1,0:T(8,128)(2,1)}, u32[]{:S(2)}, u32[]{:S(2)}) %collective-permute-start.12) | collective-permute-done | bytes 786464 | tf_op jit(solution)/shard_map/ppermute | solution.py:579
  338.1 5.5 collective-permute-done.13
  356.1 4.1 fusion.41
  375.8 8.2 collective-permute-done.26
  387.1 18.7 %collective-permute-done.25 = bf16[288,1536]{1,0:T(8,128)(2,1)} collective-permute-done((bf16[288,1536]{1,0:T(8,128)(2,1)}, bf16[288,1536]{1,0:T(8,128)(2,1)}, u32[]{:S(2)}, u32[]{:S(2)}) %collective-permute-start.25) | collective-permute-done | bytes 884768 | tf_op jit(solution)/shard_map/ppermute | solution.py:579
  410.1 11.7 collective-permute-done.32
  421.8 10.3 collective-permute-done.31
  434.6 4.1 convolution_convert_fusion.8
  446.4 4.1 convolution_convert_fusion.4
  462.6 19.0 %collective-permute-done.7 = bf16[288,1536]{1,0:T(8,128)(2,1)} collective-permute-done((bf16[288,1536]{1,0:T(8,128)(2,1)}, bf16[288,1536]{1,0:T(8,128)(2,1)}, u32[]{:S(2)}, u32[]{:S(2)}) %collective-permute-start.7) | collective-permute-done | bytes 884768 | tf_op jit(solution)/shard_map/ppermute | solution.py:579
  483.9 7.5 fusion.158
  491.4 3.9 multiply_convert_fusion.3
  495.4 8.0 convolution_convert_fusion.1
  512.2 14.9 %collective-permute-done.29 = bf16[288,1536]{1,0:T(8,128)(2,1)S(1)} collective-permute-done((bf16[288,1536]{1,0:T(8,128)(2,1)S(1)}, bf16[288,1536]{1,0:T(8,128)(2,1)S(1)}, u32[]{:S(2)}, u32[]{:S(2)}) %collective-permute-start.29) | collective-permute-done | bytes 884768 | tf_op jit(solution)/shard_map/ppermute | solution.py:579
  528.6 27.1 %collective-permute-done.28 = bf16[288,1536]{1,0:T(8,128)(2,1)S(1)} collective-permute-done((bf16[288,1536]{1,0:T(8,128)(2,1)S(1)}, bf16[288,1536]{1,0:T(8,128)(2,1)S(1)}, u32[]{:S(2)}, u32[]{:S(2)}) %collective-permute-start.28) | collective-permute-done | bytes 884768 | tf_op jit(solution)/shard_map/ppermute | solution.py:579
  557.0 7.8 add_convert_fusion.3
  567.8 7.3 fusion.159
  579.0 8.0 convolution_convert_fusion
  595.8 15.0 %collective-permute-done.35 = bf16[288,1536]{1,0:T(8,128)(2,1)S(1)} collective-permute-done((bf16[288,1536]{1,0:T(8,128)(2,1)S(1)}, bf16[288,1536]{1,0:T(8,128)(2,1)S(1)}, u32[]{:S(2)}, u32[]{:S(2)}) %collective-permute-start.35) | collective-permute-done | bytes 884768 | tf_op jit(solution)/shard_map/ppermute | solution.py:579
  610.8 18.1 %collective-permute-done.34 = bf16[288,1536]{1,0:T(8,128)(2,1)S(1)} collective-permute-done((bf16[288,1536]{1,0:T(8,128)(2,1)S(1)}, bf16[288,1536]{1,0:T(8,128)(2,1)S(1)}, u32[]{:S(2)}, u32[]{:S(2)}) %collective-permute-start.34) | collective-permute-done | bytes 884768 | tf_op jit(solution)/shard_map/ppermute | solution.py:579
  629.0 6.2 add_convert_fusion.2
  635.3 48.6 %reduce-scatter.22.cloned.1.call-done = bf16[128,1536]{1,0:T(8,128)(2,1)} async-done(((bf16[1024,1536]{1,0:T(8,128)(2,1)}), bf16[128,1536]{1,0:T(8,128)(2,1)}) %reduce-scatter.22.cloned.1.call-update) | async-done | bytes 393232 | tf_op jit(solution)/shard_map/reduce_scatter | solution.py:765
  690.9 8.7 all-gather.1
  700.2 27.6 %all-gather.25.cloned.1.call-done.d_res = bf16[1024,1536]{1,0:T(8,128)(2,1)} async-done(((bf16[128,1536]{1,0:T(8,128)(2,1)}), bf16[1024,1536]{1,0:T(8,128)(2,1)}) %all-gather.25.cloned.1.call-update) | async-done | bytes 3145744 | tf_op jit(solution)/shard_map/all_gather | solution.py:771
  727.8 47.0 %shard_map.428 = (bf16[1024,1536]{1,0:T(8,128)(2,1)}, f32[8,1536]{1,0:T(8,128)}, bf16[384,1024]{1,0:T(8,128)(2,1)}, bf16[384,1024]{1,0:T(8,128)(2,1)}, bf16[384,...) custom-call(bf16[1024,1536]{1,0:T(8,128)(2,1)} %all-gather.25.cloned, ...), custom_call_target="tpu_custom_call" | custom-call | flops 36636131328 | bytes 25165824 | tf_op jit(solution)/shard_map/pallas_call | solution.py:483
  789.7 9.7 all-gather
  800.0 47.0 %shard_map.427 = (bf16[1024,1536]{1,0:T(8,128)(2,1)}, f32[8,1536]{1,0:T(8,128)}, bf16[384,1024]{1,0:T(8,128)(2,1)}, bf16[384,1024]{1,0:T(8,128)(2,1)}, bf16[384,...) custom-call(bf16[1024,1536]{1,0:T(8,128)(2,1)} %all-gather.21.cloned, ...), custom_call_target="tpu_custom_call" | custom-call | flops 36636131328 | bytes 25165824 | tf_op jit(solution)/shard_map/pallas_call | solution.py:483
  847.1 4.3 convolution_convert_fusion.3
  858.9 8.3 fusion.59
  867.3 4.2 add_convert_fusion.1
  876.1 4.5 fusion.10
  889.2 9.3 add_convert_fusion
  905.0 3.9 broadcast.222.clone.1
  913.3 24.0 %collective-permute-done.43 = bf16[2,512,384]{2,1,0:T(8,128)(2,1)S(1)} collective-permute-done((bf16[2,512,384]{2,1,0:T(8,128)(2,1)}, bf16[2,512,384]{2,1,0:T(8,128)(2,1)S(1)}, u32[]{:S(2)}, u32[]{:S(2)}) %collective-permute-start.43) | collective-permute-done | bytes 786464 | tf_op jit(solution)/shard_map/ppermute | solution.py:579
  945.2 4.5 fusion.2
  952.7 26.0 %collective-permute-done.39 = bf16[2,384,1024]{2,1,0:T(8,128)(2,1)} collective-permute-done((bf16[2,384,1024]{2,1,0:T(8,128)(2,1)}, bf16[2,384,1024]{2,1,0:T(8,128)(2,1)}, u32[]{:S(2)}, u32[]{:S(2)}) %collective-permute-start.39) | collective-permute-done | bytes 1572896 | tf_op jit(solution)/shard_map/ppermute | solution.py:579
  986.3 25.7 %collective-permute-done.41 = bf16[2,384,1024]{2,1,0:T(8,128)(2,1)} collective-permute-done((bf16[2,384,1024]{2,1,0:T(8,128)(2,1)}, bf16[2,384,1024]{2,1,0:T(8,128)(2,1)}, u32[]{:S(2)}, u32[]{:S(2)}) %collective-permute-start.41) | collective-permute-done | bytes 1572896 | tf_op jit(solution)/shard_map/ppermute | solution.py:579
  1054.2 66.9 %psum.30 = f32[6674]{0:T(1024)S(1)} all-reduce(f32[6674]{0:T(1024)S(1)} %concatenate.87), channel_id=1, replica_groups=mesh['row'=4,'col'=8] {'row'}, use_global_device_ids=true, to_apply=%region_40.41 | all-reduce | flops 6674 | bytes 53392 | tf_op jit(solution)/shard_map/psum | solution.py:864
  1122.1 25.9 %psum.31 = f32[4352]{0:T(1024)S(1)} all-reduce(f32[4352]{0:T(1024)S(1)} %slice.371), channel_id=1, replica_groups=mesh['row'=4,'col'=8] {'col'}, use_global_device_ids=true, to_apply=%region_41.42 | all-reduce | flops 4352 | bytes 34816 | tf_op jit(solution)/shard_map/psum | solution.py:866
  1151.7 4.0 convert_add_fusion
  1178.6 18.7 %reduce-scatter.26.cloned.1.call-done = f32[32,384]{1,0:T(8,128)} async-done(((f32[256,384]{1,0:T(8,128)}), f32[32,384]{1,0:T(8,128)}) %reduce-scatter.26.cloned.1.call-update) | async-done | bytes 49168 | tf_op jit(solution)/shard_map/reduce_scatter | solution.py:860
  (697 shorter events, 308.4 us)
Async XLA Ops:
  7.2 110.6 %all-gather.11.cloned.1.call-start = ((), (), s32[]{:S(2)}) async-start(), calls=%async_computation.9 | async-start | bytes 3538944 | tf_op jit(solution)/shard_map/all_gather | solution.py:604
  11.7 134.2 %all-gather.15.cloned.1.call-start = ((), (), s32[]{:S(2)}) async-start(), calls=%async_computation.13 | async-start | bytes 3538944 | tf_op jit(solution)/shard_map/all_gather | solution.py:604
  12.4 184.7 %reduce-scatter.10.cloned.1.call-start = ((), (), s32[]{:S(2)}) async-start(), calls=%async_computation.10 | async-start | bytes 3538944 | tf_op jit(solution)/shard_map/reduce_scatter | solution.py:712
  39.8 66.3 %collective-permute-start = (bf16[1040,384]{1,0:T(8,128)(2,1)}, bf16[1040,384]{1,0:T(8,128)(2,1)}, u32[]{:S(2)}, u32[]{:S(2)}) collective-permute-start(bf16[1040,384]{1,0:T(8,128)(2,1)} %get-tuple-element.310), channel_id=1, source_target_pairs={{0,8},{8,0},{16,24},{24,16},{1,9},{9,1},{17,25},{25,17},{2,10},{10... | collective-permute-start | bytes 2396168 | tf_op jit(solution)/shard_map/ppermute | solution.py:579
  39.8 68.3 %collective-permute-start.1 = (bf16[1040,384]{1,0:T(8,128)(2,1)}, bf16[1040,384]{1,0:T(8,128)(2,1)}, u32[]{:S(2)}, u32[]{:S(2)}) collective-permute-start(bf16[1040,384]{1,0:T(8,128)(2,1)} %get-tuple-element.310), channel_id=1, source_target_pairs={{0,16},{8,24},{16,0},{24,8},{1,17},{9,25},{17,1},{25,9},{2,18},{10... | collective-permute-start | bytes 2396168 | tf_op jit(solution)/shard_map/ppermute | solution.py:579
  41.2 61.3 %collective-permute-start.4 = (bf16[768,384]{1,0:T(8,128)(2,1)}, bf16[768,384]{1,0:T(8,128)(2,1)}, u32[]{:S(2)}, u32[]{:S(2)}) collective-permute-start(bf16[768,384]{1,0:T(8,128)(2,1)} %get-tuple-element.314), channel_id=1, source_target_pairs={{0,16},{8,24},{16,0},{24,8},{1,17},{9,25},{17,1},{25,9},{2,18},{10... | collective-permute-start | bytes 1769480 | tf_op jit(solution)/shard_map/ppermute | solution.py:579
  41.8 61.9 %collective-permute-start.5 = (bf16[768,384]{1,0:T(8,128)(2,1)}, bf16[768,384]{1,0:T(8,128)(2,1)}, u32[]{:S(2)}, u32[]{:S(2)}) collective-permute-start(bf16[768,384]{1,0:T(8,128)(2,1)} %get-tuple-element.314), channel_id=1, source_target_pairs={{0,24},{8,16},{16,8},{24,0},{1,25},{9,17},{17,9},{25,1},{2,26},{10... | collective-permute-start | bytes 1769480 | tf_op jit(solution)/shard_map/ppermute | solution.py:579
  47.2 63.0 %collective-permute-start.2 = (bf16[1040,384]{1,0:T(8,128)(2,1)}, bf16[1040,384]{1,0:T(8,128)(2,1)S(1)}, u32[]{:S(2)}, u32[]{:S(2)}) collective-permute-start(bf16[1040,384]{1,0:T(8,128)(2,1)} %get-tuple-element.310), channel_id=1, source_target_pairs={{0,24},{8,16},{16,8},{24,0},{1,25},{9,17},{17,9},{25,1},{2,26},{10... | collective-permute-start | bytes 2396168 | tf_op jit(solution)/shard_map/ppermute | solution.py:579
  145.8 84.1 %reduce-scatter.14.cloned.1.call-start = ((), (), s32[]{:S(2)}) async-start(), calls=%async_computation.14 | async-start | bytes 3538944 | tf_op jit(solution)/shard_map/reduce_scatter | solution.py:712
  174.0 182.1 %all-gather.19.cloned.1.call-start = ((), (), s32[]{:S(2)}) async-start(), calls=%async_computation.17 | async-start | bytes 3538944 | tf_op jit(solution)/shard_map/all_gather | solution.py:707
  178.6 189.2 %all-gather.23.cloned.1.call-start = ((), (), s32[]{:S(2)}) async-start(), calls=%async_computation.21 | async-start | bytes 3538944 | tf_op jit(solution)/shard_map/all_gather | solution.py:707
  179.2 255.4 %all-gather.13.cloned.1.call-start = ((), (), s32[]{:S(2)}) async-start(), calls=%async_computation.11 | async-start | bytes 3538944 | tf_op jit(solution)/shard_map/all_gather | solution.py:715
  234.0 212.4 %all-gather.17.cloned.1.call-start = ((), (), s32[]{:S(2)}) async-start(), calls=%async_computation.15 | async-start | bytes 3538944 | tf_op jit(solution)/shard_map/all_gather | solution.py:715
  239.8 108.2 %collective-permute-start.9 = (bf16[2,384,1024]{2,1,0:T(8,128)(2,1)}, bf16[2,384,1024]{2,1,0:T(8,128)(2,1)}, u32[]{:S(2)}, u32[]{:S(2)}) collective-permute-start(bf16[2,384,1024]{2,1,0:T(8,128)(2,1)} %pad_maximum_fusion.6), channel_id=1, source_target_pairs={{0,8},{8,0},{16,24},{24,16},{1,9},{9,1},{17,25},{25,17},{2,10},{10... | collective-permute-start | bytes 4718600 | tf_op jit(solution)/shard_map/ppermute | solution.py:579
  242.5 108.1 %collective-permute-start.10 = (bf16[2,384,1024]{2,1,0:T(8,128)(2,1)}, bf16[2,384,1024]{2,1,0:T(8,128)(2,1)}, u32[]{:S(2)}, u32[]{:S(2)}) collective-permute-start(bf16[2,384,1024]{2,1,0:T(8,128)(2,1)} %pad_maximum_fusion.7), channel_id=1, source_target_pairs={{0,16},{8,24},{16,0},{24,8},{1,17},{9,25},{17,1},{25,9},{2,18},{10... | collective-permute-start | bytes 4718600 | tf_op jit(solution)/shard_map/ppermute | solution.py:579
  245.4 107.9 %collective-permute-start.11 = (bf16[2,384,1024]{2,1,0:T(8,128)(2,1)}, bf16[2,384,1024]{2,1,0:T(8,128)(2,1)}, u32[]{:S(2)}, u32[]{:S(2)}) collective-permute-start(bf16[2,384,1024]{2,1,0:T(8,128)(2,1)} %pad_maximum_fusion.8), channel_id=1, source_target_pairs={{0,24},{8,16},{16,8},{24,0},{1,25},{9,17},{17,9},{25,1},{2,26},{10... | collective-permute-start | bytes 4718600 | tf_op jit(solution)/shard_map/ppermute | solution.py:579
  249.8 74.6 %collective-permute-start.12 = (bf16[2,512,384]{2,1,0:T(8,128)(2,1)}, bf16[2,512,384]{2,1,0:T(8,128)(2,1)}, u32[]{:S(2)}, u32[]{:S(2)}) collective-permute-start(bf16[2,512,384]{2,1,0:T(8,128)(2,1)} %get-tuple-element.277), channel_id=1, source_target_pairs={{0,8},{8,0},{16,24},{24,16},{1,9},{9,1},{17,25},{25,17},{2,10},{10... | collective-permute-start | bytes 2359304 | tf_op jit(solution)/shard_map/ppermute | solution.py:579
  250.9 92.7 %collective-permute-start.13 = (bf16[2,512,384]{2,1,0:T(8,128)(2,1)}, bf16[2,512,384]{2,1,0:T(8,128)(2,1)}, u32[]{:S(2)}, u32[]{:S(2)}) collective-permute-start(bf16[2,512,384]{2,1,0:T(8,128)(2,1)} %get-tuple-element.279), channel_id=1, source_target_pairs={{0,16},{8,24},{16,0},{24,8},{1,17},{9,25},{17,1},{25,9},{2,18},{10... | collective-permute-start | bytes 2359304 | tf_op jit(solution)/shard_map/ppermute | solution.py:579
  332.7 302.7 %reduce-scatter.18.cloned.1.call-start = ((), (), s32[]{:S(2)}) async-start(), calls=%async_computation.18 | async-start | bytes 3538944 | tf_op jit(solution)/shard_map/reduce_scatter | solution.py:765
  363.9 41.9 %collective-permute-start.25 = (bf16[288,1536]{1,0:T(8,128)(2,1)}, bf16[288,1536]{1,0:T(8,128)(2,1)}, u32[]{:S(2)}, u32[]{:S(2)}) collective-permute-start(bf16[288,1536]{1,0:T(8,128)(2,1)} %fusion.40), channel_id=1, source_target_pairs={{0,16},{8,24},{16,0},{24,8},{1,17},{9,25},{17,1},{25,9},{2,18},{10... | collective-permute-start | bytes 2654216 | tf_op jit(solution)/shard_map/ppermute | solution.py:579
  366.6 39.2 %collective-permute-start.24 = (bf16[288,1536]{1,0:T(8,128)(2,1)}, bf16[288,1536]{1,0:T(8,128)(2,1)}, u32[]{:S(2)}, u32[]{:S(2)}) collective-permute-start(bf16[288,1536]{1,0:T(8,128)(2,1)} %fusion.39), channel_id=1, source_target_pairs={{0,8},{8,0},{16,24},{24,16},{1,9},{9,1},{17,25},{25,17},{2,10},{10... | collective-permute-start | bytes 2654216 | tf_op jit(solution)/shard_map/ppermute | solution.py:579
  371.2 50.7 %collective-permute-start.32 = (bf16[288,1536]{1,0:T(8,128)(2,1)S(1)}, bf16[288,1536]{1,0:T(8,128)(2,1)S(1)}, u32[]{:S(2)}, u32[]{:S(2)}) collective-permute-start(bf16[288,1536]{1,0:T(8,128)(2,1)S(1)} %fusion.45), channel_id=1, source_target_pairs={{0,24},{8,16},{16,8},{24,0},{1,25},{9,17},{17,9},{25,1},{2,26},{10... | collective-permute-start | bytes 2654216 | tf_op jit(solution)/shard_map/ppermute | solution.py:579
  374.0 58.1 %collective-permute-start.31 = (bf16[288,1536]{1,0:T(8,128)(2,1)S(1)}, bf16[288,1536]{1,0:T(8,128)(2,1)S(1)}, u32[]{:S(2)}, u32[]{:S(2)}) collective-permute-start(bf16[288,1536]{1,0:T(8,128)(2,1)S(1)} %fusion.44), channel_id=1, source_target_pairs={{0,16},{8,24},{16,0},{24,8},{1,17},{9,25},{17,1},{25,9},{2,18},{10... | collective-permute-start | bytes 2654216 | tf_op jit(solution)/shard_map/ppermute | solution.py:579
  384.0 48.2 %collective-permute-start.30 = (bf16[288,1536]{1,0:T(8,128)(2,1)S(1)}, bf16[288,1536]{1,0:T(8,128)(2,1)S(1)}, u32[]{:S(2)}, u32[]{:S(2)}) collective-permute-start(bf16[288,1536]{1,0:T(8,128)(2,1)S(1)} %fusion.43), channel_id=1, source_target_pairs={{0,8},{8,0},{16,24},{24,16},{1,9},{9,1},{17,25},{25,17},{2,10},{10... | collective-permute-start | bytes 2654216 | tf_op jit(solution)/shard_map/ppermute | solution.py:579
  450.5 114.3 %collective-permute-start.20 = (bf16[288,1536]{1,0:T(8,128)(2,1)}, bf16[288,1536]{1,0:T(8,128)(2,1)}, u32[]{:S(2)}, u32[]{:S(2)}) collective-permute-start(bf16[288,1536]{1,0:T(8,128)(2,1)} %convolution_convert_fusion.4), channel_id=1, source_target_pairs={{0,24},{8,16},{16,8},{24,0},{1,25},{9,17},{17,9},{25,1},{2,26},{10... | collective-permute-start | bytes 2654216 | tf_op jit(solution)/shard_map/ppermute | solution.py:579
  455.2 109.7 %collective-permute-start.19 = (bf16[288,1536]{1,0:T(8,128)(2,1)}, bf16[288,1536]{1,0:T(8,128)(2,1)}, u32[]{:S(2)}, u32[]{:S(2)}) collective-permute-start(bf16[288,1536]{1,0:T(8,128)(2,1)} %convolution_convert_fusion.5), channel_id=1, source_target_pairs={{0,16},{8,24},{16,0},{24,8},{1,17},{9,25},{17,1},{25,9},{2,18},{10... | collective-permute-start | bytes 2654216 | tf_op jit(solution)/shard_map/ppermute | solution.py:579
  505.4 50.4 %collective-permute-start.28 = (bf16[288,1536]{1,0:T(8,128)(2,1)S(1)}, bf16[288,1536]{1,0:T(8,128)(2,1)S(1)}, u32[]{:S(2)}, u32[]{:S(2)}) collective-permute-start(bf16[288,1536]{1,0:T(8,128)(2,1)S(1)} %bitcast.284), channel_id=1, source_target_pairs={{0,16},{8,24},{16,0},{24,8},{1,17},{9,25},{17,1},{25,9},{2,18},{10... | collective-permute-start | bytes 2654216 | tf_op jit(solution)/shard_map/ppermute | solution.py:579
  506.7 49.1 %collective-permute-start.27 = (bf16[288,1536]{1,0:T(8,128)(2,1)S(1)}, bf16[288,1536]{1,0:T(8,128)(2,1)S(1)}, u32[]{:S(2)}, u32[]{:S(2)}) collective-permute-start(bf16[288,1536]{1,0:T(8,128)(2,1)S(1)} %bitcast.280), channel_id=1, source_target_pairs={{0,8},{8,0},{16,24},{24,16},{1,9},{9,1},{17,25},{25,17},{2,10},{10... | collective-permute-start | bytes 2654216 | tf_op jit(solution)/shard_map/ppermute | solution.py:579
  564.8 119.2 %reduce-scatter.22.cloned.1.call-start = ((), (), s32[]{:S(2)}) async-start(), calls=%async_computation.22 | async-start | bytes 3538944 | tf_op jit(solution)/shard_map/reduce_scatter | solution.py:765
  588.7 40.3 %collective-permute-start.34 = (bf16[288,1536]{1,0:T(8,128)(2,1)S(1)}, bf16[288,1536]{1,0:T(8,128)(2,1)S(1)}, u32[]{:S(2)}, u32[]{:S(2)}) collective-permute-start(bf16[288,1536]{1,0:T(8,128)(2,1)S(1)} %bitcast.286), channel_id=1, source_target_pairs={{0,16},{8,24},{16,0},{24,8},{1,17},{9,25},{17,1},{25,9},{2,18},{10... | collective-permute-start | bytes 2654216 | tf_op jit(solution)/shard_map/ppermute | solution.py:579
  635.3 92.5 %all-gather.25.cloned.1.call-start = ((), (), s32[]{:S(2)}) async-start(), calls=%async_computation.23 | async-start | bytes 3538944 | tf_op jit(solution)/shard_map/all_gather | solution.py:771
  690.3 109.8 %all-gather.21.cloned.1.call-start = ((), (), s32[]{:S(2)}) async-start(), calls=%async_computation.19 | async-start | bytes 3538944 | tf_op jit(solution)/shard_map/all_gather | solution.py:771
  690.9 478.5 %reduce-scatter.24.cloned.1.call-start = ((), (), s32[]{:S(2)}) async-start(), calls=%async_computation.24 | async-start | bytes 3538944 | tf_op jit(solution)/shard_map/reduce_scatter | solution.py:789
  774.8 394.5 %reduce-scatter.20.cloned.1.call-start = ((), (), s32[]{:S(2)}) async-start(), calls=%async_computation.20 | async-start | bytes 3538944 | tf_op jit(solution)/shard_map/reduce_scatter | solution.py:789
  786.2 85.6 %collective-permute-start.23 = (bf16[288,1536]{1,0:T(8,128)(2,1)}, bf16[288,1536]{1,0:T(8,128)(2,1)}, u32[]{:S(2)}, u32[]{:S(2)}) collective-permute-start(bf16[288,1536]{1,0:T(8,128)(2,1)} %bitcast.51), channel_id=1, source_target_pairs={{0,24},{8,16},{16,8},{24,0},{1,25},{9,17},{17,9},{25,1},{2,26},{10... | collective-permute-start | bytes 2654216 | tf_op jit(solution)/shard_map/ppermute | solution.py:579
  788.7 84.6 %collective-permute-start.22 = (bf16[288,1536]{1,0:T(8,128)(2,1)}, bf16[288,1536]{1,0:T(8,128)(2,1)}, u32[]{:S(2)}, u32[]{:S(2)}) collective-permute-start(bf16[288,1536]{1,0:T(8,128)(2,1)} %bitcast.50), channel_id=1, source_target_pairs={{0,16},{8,24},{16,0},{24,8},{1,17},{9,25},{17,1},{25,9},{2,18},{10... | collective-permute-start | bytes 2654216 | tf_op jit(solution)/shard_map/ppermute | solution.py:579
  789.2 85.5 %collective-permute-start.21 = (bf16[288,1536]{1,0:T(8,128)(2,1)}, bf16[288,1536]{1,0:T(8,128)(2,1)}, u32[]{:S(2)}, u32[]{:S(2)}) collective-permute-start(bf16[288,1536]{1,0:T(8,128)(2,1)} %bitcast.49), channel_id=1, source_target_pairs={{0,8},{8,0},{16,24},{24,16},{1,9},{9,1},{17,25},{25,17},{2,10},{10... | collective-permute-start | bytes 2654216 | tf_op jit(solution)/shard_map/ppermute | solution.py:579
  847.0 324.5 %reduce-scatter.16.cloned.1.call-start = ((), (), s32[]{:S(2)}) async-start(), calls=%async_computation.16 | async-start | bytes 3538944 | tf_op jit(solution)/shard_map/reduce_scatter | solution.py:803
  853.3 87.1 %collective-permute-start.17 = (bf16[288,1536]{1,0:T(8,128)(2,1)}, bf16[288,1536]{1,0:T(8,128)(2,1)}, u32[]{:S(2)}, u32[]{:S(2)}) collective-permute-start(bf16[288,1536]{1,0:T(8,128)(2,1)} %bitcast.30), channel_id=1, source_target_pairs={{0,24},{8,16},{16,8},{24,0},{1,25},{9,17},{17,9},{25,1},{2,26},{10... | collective-permute-start | bytes 2654216 | tf_op jit(solution)/shard_map/ppermute | solution.py:579
  855.6 87.9 %collective-permute-start.16 = (bf16[288,1536]{1,0:T(8,128)(2,1)}, bf16[288,1536]{1,0:T(8,128)(2,1)}, u32[]{:S(2)}, u32[]{:S(2)}) collective-permute-start(bf16[288,1536]{1,0:T(8,128)(2,1)} %bitcast.29), channel_id=1, source_target_pairs={{0,16},{8,24},{16,0},{24,8},{1,17},{9,25},{17,1},{25,9},{2,18},{10... | collective-permute-start | bytes 2654216 | tf_op jit(solution)/shard_map/ppermute | solution.py:579
  883.4 291.0 %reduce-scatter.12.cloned.1.call-start = ((), (), s32[]{:S(2)}) async-start(), calls=%async_computation.12 | async-start | bytes 3538944 | tf_op jit(solution)/shard_map/reduce_scatter | solution.py:803
  937.3 41.5 %collective-permute-start.39 = (bf16[2,384,1024]{2,1,0:T(8,128)(2,1)}, bf16[2,384,1024]{2,1,0:T(8,128)(2,1)}, u32[]{:S(2)}, u32[]{:S(2)}) collective-permute-start(bf16[2,384,1024]{2,1,0:T(8,128)(2,1)} %get-tuple-element.242), channel_id=1, source_target_pairs={{0,8},{8,0},{16,24},{24,16},{1,9},{9,1},{17,25},{25,17},{2,10},{10... | collective-permute-start | bytes 4718600 | tf_op jit(solution)/shard_map/ppermute | solution.py:579
  938.6 41.9 %collective-permute-start.40 = (bf16[2,384,1024]{2,1,0:T(8,128)(2,1)}, bf16[2,384,1024]{2,1,0:T(8,128)(2,1)}, u32[]{:S(2)}, u32[]{:S(2)}) collective-permute-start(bf16[2,384,1024]{2,1,0:T(8,128)(2,1)} %get-tuple-element.241), channel_id=1, source_target_pairs={{0,16},{8,24},{16,0},{24,8},{1,17},{9,25},{17,1},{25,9},{2,18},{10... | collective-permute-start | bytes 4718600 | tf_op jit(solution)/shard_map/ppermute | solution.py:579
  940.3 71.7 %collective-permute-start.41 = (bf16[2,384,1024]{2,1,0:T(8,128)(2,1)}, bf16[2,384,1024]{2,1,0:T(8,128)(2,1)}, u32[]{:S(2)}, u32[]{:S(2)}) collective-permute-start(bf16[2,384,1024]{2,1,0:T(8,128)(2,1)} %get-tuple-element.240), channel_id=1, source_target_pairs={{0,24},{8,16},{16,8},{24,0},{1,25},{9,17},{17,9},{25,1},{2,26},{10... | collective-permute-start | bytes 4718600 | tf_op jit(solution)/shard_map/ppermute | solution.py:579
  952.5 244.8 %reduce-scatter.26.cloned.1.call-start = ((), (), s32[]{:S(2)}) async-start(), calls=%async_computation.25 | async-start | bytes 442368 | tf_op jit(solution)/shard_map/reduce_scatter | solution.py:860
  1049.6 102.1 %collective-permute-start.38 = (bf16[1808,384]{1,0:T(8,128)(2,1)}, bf16[1808,384]{1,0:T(8,128)(2,1)S(1)}, u32[]{:S(2)}, u32[]{:S(2)}) collective-permute-start(bf16[1808,384]{1,0:T(8,128)(2,1)} %get-tuple-element.245), channel_id=1, source_target_pairs={{0,24},{8,16},{16,8},{24,0},{1,25},{9,17},{17,9},{25,1},{2,26},{10... | collective-permute-start | bytes 4165640 | tf_op jit(solution)/shard_map/ppermute | solution.py:579
  1050.4 101.3 %collective-permute-start.37 = (bf16[1808,384]{1,0:T(8,128)(2,1)}, bf16[1808,384]{1,0:T(8,128)(2,1)S(1)}, u32[]{:S(2)}, u32[]{:S(2)}) collective-permute-start(bf16[1808,384]{1,0:T(8,128)(2,1)} %get-tuple-element.246), channel_id=1, source_target_pairs={{0,16},{8,24},{16,0},{24,8},{1,17},{9,25},{17,1},{25,9},{2,18},{10... | collective-permute-start | bytes 4165640 | tf_op jit(solution)/shard_map/ppermute | solution.py:579
  1051.9 99.8 %collective-permute-start.36 = (bf16[1808,384]{1,0:T(8,128)(2,1)}, bf16[1808,384]{1,0:T(8,128)(2,1)}, u32[]{:S(2)}, u32[]{:S(2)}) collective-permute-start(bf16[1808,384]{1,0:T(8,128)(2,1)} %get-tuple-element.244), channel_id=1, source_target_pairs={{0,8},{8,0},{16,24},{24,16},{1,9},{9,1},{17,25},{25,17},{2,10},{10... | collective-permute-start | bytes 4165640 | tf_op jit(solution)/shard_map/ppermute | solution.py:579
  (189 other events, 2920.8 us)
Sparse Core Ops, SparseCore 0:
  11.8 43.8 all-gather.10
  57.9 37.3 all-gather.14
  146.0 41.6 reduce-scatter.9
  190.4 39.4 reduce-scatter.13
  231.4 37.3 all-gather.18
  270.4 37.1 all-gather.22
  309.8 37.1 all-gather.12
  348.6 37.1 all-gather.16
  564.9 49.1 reduce-scatter.17
  635.4 48.5 reduce-scatter.21
  690.4 37.3 all-gather.24
  729.8 37.1 all-gather.20
  775.0 39.1 reduce-scatter.23
  847.2 38.9 reduce-scatter.19
  888.3 39.4 reduce-scatter.15
  952.6 38.4 reduce-scatter.11
  1169.4 27.8 reduce-scatter.25

commit v2 on v1

--- a/solution.py
+++ b/solution.py
@@ -17,6 +17,9 @@
 BF16 = jnp.bfloat16
 VMEM = pl.BlockSpec(memory_space=pltpu.VMEM)
 VMEM_LIMIT = 56 * 1024 * 1024
+KERNEL_COST = pl.CostEstimate(flops=3 * 10**10, bytes_accessed=2**20, transcendentals=0)
+ANY = pl.BlockSpec(memory_space=pl.ANY)
+MESH = pl.DeviceIdType.MESH
 
 
 def contract(left_op, right_op, left_dim, right_dim, precision=None):
@@ -128,6 +131,40 @@
     return pl.ds(pl.multiple_of(block * BLOCK, BLOCK), BLOCK)
 
 
+def greet(peers):
+    barrier = pltpu.get_barrier_semaphore()
+    for other in peers:
+        pl.semaphore_signal(barrier, inc=1, device_id=other, device_id_type=MESH)
+    pl.semaphore_wait(barrier, len(peers))
+
+
+def row_partners(members):
+    me = lax.axis_index("row")
+    return [{"row": me ^ k} for k in range(1, members)]
+
+
+def send(source, target, send_sem, recv_sem, other):
+    copy = pltpu.make_async_remote_copy(
+        src_ref=source,
+        dst_ref=target,
+        send_sem=send_sem,
+        recv_sem=recv_sem,
+        device_id=other,
+        device_id_type=MESH,
+    )
+    copy.start()
+    return copy
+
+
+def send_parts(parts, received, sems):
+    partners = row_partners(len(parts) + 1)
+    greet(partners)
+    return [
+        send(parts[k], received[k], sems.at[0, k], sems.at[1, k], other)
+        for k, other in enumerate(partners)
+    ]
+
+
 def mixer_forward_kernel(
     heads,
     xn,
@@ -139,20 +176,15 @@
     chan,
     io_taps,
     head_params,
-    y,
-    squares,
-    branch,
-    conv,
-    io_pre,
-    io,
-    step_pre,
-    starts,
-    step_s,
-    cum_s,
-    cum_t_s,
-    scores_s,
-    z_s,
+    *refs,
 ):
+    refs = list(refs)
+    count = (len(refs) - 14) // 2
+    parts, refs = refs[:count], refs[count:]
+    y, squares, branch, conv, io_pre, io, step_pre, starts = refs[:8]
+    received = refs[8 : 8 + count]
+    step_s, cum_s, cum_t_s, scores_s, z_s, sems = refs[8 + count :]
+    copies = send_parts(parts, received, sems)
     length = xn.shape[0]
     blocks = length // BLOCK
     size = wb.shape[0] // heads
@@ -216,16 +248,17 @@
         return carry
 
     lax.fori_loop(0, blocks, out_step, 0)
-
-
-def mixer_forward(xn, wb, wc, wio, ws, wo, chan, io_taps, head_params, heads):
+    for copy in copies:
+        copy.wait()
+
+
+def mixer_forward(parts, xn, wb, wc, wio, ws, wo, chan, io_taps, head_params, heads):
     length, width = xn.shape
     share = wb.shape[0]
     blocks = length // BLOCK
     size = share // heads
     shape = jax.ShapeDtypeStruct
-    flops = 2 * length * width * (3 * share + 2 * NS + HEAD_ROWS) + 10**8
-    return pl.pallas_call(
+    out = pl.pallas_call(
         functools.partial(mixer_forward_kernel, heads),
         out_shape=(
             shape((length, width), BF16),
@@ -236,21 +269,24 @@
             shape((2 * NS, length), BF16),
             shape((HEAD_ROWS, length), F32),
             shape((heads * blocks * size, NS), F32),
-        ),
-        in_specs=[VMEM] * 9,
-        out_specs=[VMEM] * 8,
+        )
+        + tuple(shape(part.shape, part.dtype) for part in parts),
+        in_specs=[VMEM] * 9 + [ANY] * len(parts),
+        out_specs=(VMEM,) * 8 + (ANY,) * len(parts),
         scratch_shapes=[
             pltpu.VMEM((HEAD_ROWS, length), F32),
             pltpu.VMEM((HEAD_ROWS, length), F32),
             pltpu.VMEM((length, HEAD_ROWS), F32),
             pltpu.VMEM((blocks, BLOCK, BLOCK), F32),
             pltpu.VMEM((share, length), BF16),
+            pltpu.SemaphoreType.DMA((2, len(parts))),
         ],
-        compiler_params=pltpu.CompilerParams(vmem_limit_bytes=VMEM_LIMIT),
-        cost_estimate=pl.CostEstimate(
-            flops=4 * flops, bytes_accessed=4 * 2 * length * width, transcendentals=10**7
+        compiler_params=pltpu.CompilerParams(
+            vmem_limit_bytes=VMEM_LIMIT, collective_id=2, has_side_effects=True
         ),
-    )(xn, wb, wc, wio, ws, wo, chan, io_taps, head_params)
+        cost_estimate=KERNEL_COST,
+    )(xn, wb, wc, wio, ws, wo, chan, io_taps, head_params, *parts)
+    return out[:8], out[8:]
 
 
 def mixer_backward_kernel(
@@ -272,28 +308,18 @@
     io,
     step_pre,
     starts,
-    first_part,
-    gain_part,
-    mixed,
-    d_branch,
-    d_conv,
-    d_io,
-    d_step,
-    chan_grad,
-    io_grad,
-    head_grad,
-    step_s,
-    cum_s,
-    cum_t_s,
-    scores_s,
-    d_scores_s,
-    d_mixed_s,
-    d_io_s,
-    d_cum_s,
-    d_size_s,
-    adjoint_s,
+    *refs,
 ):
-    length = xn.shape[0]
+    refs = list(refs)
+    count = (len(refs) - 22) // 2
+    parts, refs = refs[:count], refs[count:]
+    first_part, gain_part, mixed, d_branch, d_conv, d_io, d_step = refs[:7]
+    chan_grad, io_grad, head_grad = refs[7:10]
+    received, refs = refs[10 : 10 + count], refs[10 + count :]
+    step_s, cum_s, cum_t_s, scores_s, d_scores_s, d_mixed_s, d_io_s = refs[:7]
+    d_cum_s, d_size_s, adjoint_s, cube_s, sems = refs[7:]
+    copies = send_parts(parts, received, sems)
+    length, width = xn.shape
     blocks = length // BLOCK
     size = wb.shape[0] // heads
     step_rows(step_pre[...], head_params[...], step_s, cum_s, cum_t_s, blocks)
@@ -308,7 +334,11 @@
 
     def project(block, carry):
         cols = block_cols(block)
-        d_mixed_s[:, cols] = dot_last(wo[...], d_res[cols, :])
+        d_mixed_s[:, cols] = dot_last(wo[...], d_res[cols, :width])
+        cross = jnp.transpose(d_res[cols, width:].astype(F32))
+        cross = cross[0:1] + cross[1:2] + cross[2:3]
+        rms = scale_rows[0:1, cols]
+        cube_s[:, cols] = rms * rms * rms * cross * scale_rows[1:2, cols]
         return carry
 
     lax.fori_loop(0, blocks, project, 0)
@@ -350,7 +380,7 @@
             d_mixed = d_mixed_s[rows, cols]
             gain = params[:, 5:6]
             mixed[rows, cols] = (gated * inverse_rms * gain).astype(BF16)
-            d_gated = inverse_rms * (d_mixed * gain) - gated * scale_rows[1:2, cols]
+            d_gated = inverse_rms * (d_mixed * gain) - gated * cube_s[:, cols]
             d_gain = row_sum(d_mixed * gated * inverse_rms)
             d_scanned = d_gated * gate_out
             d_branch[rows, cols] = (
@@ -471,16 +501,17 @@
         return carry
 
     lax.fori_loop(0, blocks, first_step, 0)
-
-
-def mixer_backward(d_res, scale_rows, xn, weights, saved, heads):
+    for copy in copies:
+        copy.wait()
+
+
+def mixer_backward(parts, d_res, scale_rows, xn, weights, saved, heads):
     length, width = xn.shape
     share = weights[0].shape[0]
     blocks = length // BLOCK
     size = share // heads
     shape = jax.ShapeDtypeStruct
-    flops = 2 * length * width * (3 * share + 2 * NS + HEAD_ROWS) + 10**8
-    return pl.pallas_call(
+    out = pl.pallas_call(
         functools.partial(mixer_backward_kernel, heads),
         out_shape=(
             shape((length, width), BF16),
@@ -493,9 +524,10 @@
             shape((share, LANES), F32),
             shape((2 * NS, LANES), F32),
             shape((HEAD_ROWS, LANES), F32),
-        ),
-        in_specs=[VMEM] * 17,
-        out_specs=[VMEM] * 10,
+        )
+        + tuple(shape(part.shape, part.dtype) for part in parts),
+        in_specs=[VMEM] * 17 + [ANY] * len(parts),
+        out_specs=(VMEM,) * 10 + (ANY,) * len(parts),
         scratch_shapes=[
             pltpu.VMEM((HEAD_ROWS, length), F32),
             pltpu.VMEM((HEAD_ROWS, length), F32),
@@ -507,12 +539,394 @@
             pltpu.VMEM((HEAD_ROWS, length), F32),
             pltpu.VMEM((HEAD_ROWS, length), F32),
             pltpu.VMEM((size, length + LANES), F32),
+            pltpu.VMEM((1, length), F32),
+            pltpu.SemaphoreType.DMA((2, len(parts))),
         ],
+        compiler_params=pltpu.CompilerParams(
+            vmem_limit_bytes=VMEM_LIMIT, collective_id=3, has_side_effects=True
+        ),
+        cost_estimate=KERNEL_COST,
+    )(d_res, scale_rows, xn, *weights, *saved, *parts)
+    return out[:10], out[10:]
+
+
+def call(kernel, out_shape, scratch, in_specs, args):
+    return pl.pallas_call(
+        kernel,
+        out_shape=out_shape,
+        in_specs=in_specs,
+        out_specs=jax.tree.map(lambda _: VMEM, out_shape),
+        scratch_shapes=scratch,
         compiler_params=pltpu.CompilerParams(vmem_limit_bytes=VMEM_LIMIT),
-        cost_estimate=pl.CostEstimate(
-            flops=8 * flops, bytes_accessed=8 * 2 * length * width, transcendentals=10**7
+        cost_estimate=KERNEL_COST,
+    )(*args)
+
+
+def place_rows(slot_t, gates_t, placed):
+    length, units = slot_t.shape
+
+    def choose(block, carry):
+        at = block_cols(block)
+        slots = slot_t[at, :]
+        for tile in range(units * CAP // LANES):
+            low, high = tile * LANES // CAP, (tile * LANES + LANES - 1) // CAP
+            lane = lax.broadcasted_iota(jnp.int32, (BLOCK, LANES), 1) + tile * LANES
+            total = jnp.zeros((BLOCK, LANES), F32)
+            for unit in range(low, high + 1):
+                value = 1.0 if gates_t is None else gates_t[at, unit : unit + 1]
+                total = jnp.where(lane == slots[:, unit : unit + 1] + unit * CAP, value, total)
+            placed[at, tile * LANES : (tile + 1) * LANES] = total.astype(BF16)
+        return carry
+
+    lax.fori_loop(0, length // BLOCK, choose, 0)
+
+
+def combine_kernel(members, slot_t, gates_t, extra_left, extra_right, *refs):
+    rows, (out, chosen_s, rows_s, sems) = refs[:members], refs[members:]
+    length, units = slot_t.shape
+    part = units // members * CAP
+    copies = []
+    for member in range(members):
+        copies.append(
+            pltpu.make_async_copy(
+                rows[member], rows_s.at[pl.ds(member * part, part)], sems.at[member]
+            )
+        )
+        copies[-1].start()
+
+    place_rows(slot_t, gates_t, chosen_s)
+    for copy in copies:
+        copy.wait()
+
+    def columns(at, carry):
+        cols = block_cols(at)
+        total = dot_plain(chosen_s[...], rows_s[:, cols])
+        total = total + dot_plain(extra_left[...], extra_right[:, cols])
+        out[:, cols] = total.astype(BF16)
+        return carry
+
+    lax.fori_loop(0, out.shape[1] // BLOCK, columns, 0)
+
+
+def combine_rows(slot_t, gates_t, rows, extra_left, extra_right):
+    length, units = slot_t.shape
+    members = len(rows)
+    width = rows[0].shape[1]
+    return call(
+        functools.partial(combine_kernel, members),
+        jax.ShapeDtypeStruct((length, width), BF16),
+        [
+            pltpu.VMEM((length, units * CAP), BF16),
+            pltpu.VMEM((units * CAP, width), BF16),
+            pltpu.SemaphoreType.DMA((members,)),
+        ],
+        [VMEM] * 4 + [ANY] * members,
+        (slot_t, gates_t, extra_left, extra_right, *rows),
+    )
+
+
+def exchange_kernel(members, slot, gates, slot_t, second, cot, gate_sh, up_sh, down_sh, *refs):
+    refs = list(refs)
+    shards = [refs[at * members : (at + 1) * members] for at in range(3)]
+    part, out_rows, hidden_sh, d_gate_sh, d_up_sh, token_out, cot_out, hidden_s, d_pre_s = refs[
+        3 * members : 3 * members + 9
+    ]
+    (
+        token_s,
+        cot_s,
+        token_send,
+        cot_send,
+        back_s,
+        weights,
+        chosen_s,
+        gate_s,
+        places_s,
+        row_sems,
+        weight_sems,
+        out_sems,
+    ) = refs[3 * members + 9 :]
+    units, length = slot.shape
+    width = second.shape[1]
+    experts = units // members
+    rows = experts * CAP
+    hidden_width = weights.shape[3]
+    depth = width // members
+    chunk = min(BLOCK, hidden_width)
+    me = lax.axis_index("row")
+    partners = row_partners(members)
+    weight_copies = []
+    for member in range(members):
+        place = pl.ds(pl.multiple_of((me ^ member) * depth, depth), depth)
+        for which in range(3):
+            weight_copies.append(
+                pltpu.make_async_copy(
+                    shards[which][member],
+                    weights.at[which, :, place],
+                    weight_sems.at[which, member],
+                )
+            )
+            weight_copies[-1].start()
+    greet(partners)
+
+    def choose(unit, carry):
+        at = pl.ds(pl.multiple_of(unit * CAP, CAP), CAP)
+        place = lax.broadcasted_iota(jnp.int32, (CAP, length), 0)
+        hit = place == slot[pl.ds(unit, 1), :]
+        chosen_s[at, :] = jnp.where(hit, 1.0, 0.0).astype(BF16)
+        gate_s[at, :] = row_sum(jnp.where(hit, gates[pl.ds(unit, 1), :], 0.0))
+        return carry
+
+    lax.fori_loop(0, units, choose, 0)
+
+    def pick(source, weighted, kept, outgoing, first_sem):
+        def columns(at, carry):
+            cols = block_cols(at)
+            picked = dot_plain(chosen_s[...], source[:, cols])
+            if weighted:
+                picked = picked * gate_s[...]
+            picked = picked.astype(BF16)
+            for expert in range(experts):
+                kept[expert, :CAP, cols] = picked[expert * CAP : (expert + 1) * CAP]
+            outgoing[:, cols] = picked[rows:]
+            return carry
+
+        lax.fori_loop(0, width // BLOCK, columns, 0)
+        copies = []
+        for k, other in enumerate(partners):
+            for expert in range(experts):
+                copies.append(
+                    send(
+                        outgoing.at[pl.ds(k * rows + expert * CAP, CAP)],
+                        kept.at[expert, pl.ds((k + 1) * CAP, CAP)],
+                        row_sems.at[first_sem, k, expert],
+                        row_sems.at[first_sem + 1, k, expert],
+                        other,
+                    )
+                )
+        return copies
+
+    copies = pick(cot, True, cot_s, cot_send, 0)
+    copies += pick(second, False, token_s, token_send, 2)
+
+    def shared_step(at, carry):
+        at = block_cols(at)
+        gate_pre = dot_last(second[at, :], gate_sh[...])
+        up_pre = dot_last(second[at, :], up_sh[...])
+        d_hidden = dot_last(cot[at, :], down_sh[...])
+        logistic = jax.nn.sigmoid(gate_pre)
+        active = gate_pre * logistic
+        hidden_sh[at, :] = (active * up_pre).astype(BF16)
+        slope = logistic * (1.0 + gate_pre * (1.0 - logistic))
+        d_gate_sh[at, :] = (d_hidden * up_pre * slope).astype(BF16)
+        d_up_sh[at, :] = (d_hidden * active).astype(BF16)
+        return carry
+
+    lax.fori_loop(0, length // BLOCK, shared_step, 0)
+    for copy in weight_copies:
+        copy.wait()
+    for copy in copies:
+        copy.wait()
+    saves = [
+        pltpu.make_async_copy(token_s, token_out, out_sems.at[0]),
+        pltpu.make_async_copy(cot_s, cot_out, out_sems.at[1]),
+    ]
+    for copy in saves:
+        copy.start()
+
+    copies = []
+    for expert in range(experts):
+
+        def hidden_step(at, carry):
+            cols = pl.ds(pl.multiple_of(at * chunk, chunk), chunk)
+            up_cols = pl.ds(pl.multiple_of(hidden_width + at * chunk, chunk), chunk)
+            gate_pre = dot_plain(token_s[expert], weights[0, expert, :, cols])
+            up_pre = dot_plain(token_s[expert], weights[1, expert, :, cols])
+            d_hidden = dot_plain(cot_s[expert], weights[2, expert, :, cols])
+            logistic = jax.nn.sigmoid(gate_pre)
+            active = gate_pre * logistic
+            hidden_s[expert, :, cols] = (active * up_pre).astype(BF16)
+            slope = logistic * (1.0 + gate_pre * (1.0 - logistic))
+            d_pre_s[expert, :, cols] = (d_hidden * up_pre * slope).astype(BF16)
+            d_pre_s[expert, :, up_cols] = (d_hidden * active).astype(BF16)
+            return carry
+
+        lax.fori_loop(0, hidden_width // chunk, hidden_step, 0)
+
+        def back_step(at, carry):
+            cols = block_cols(at)
+            back = dot_last(d_pre_s[expert, :, :hidden_width], weights[0, expert, cols, :])
+            back = back + dot_last(d_pre_s[expert, :, hidden_width:], weights[1, expert, cols, :])
+            back = back.astype(BF16)
+            back_s[expert * CAP : (expert + 1) * CAP, cols] = back[:CAP]
+            for k in range(members - 1):
+                token_send[k * rows + expert * CAP : k * rows + (expert + 1) * CAP, cols] = back[
+                    (k + 1) * CAP : (k + 2) * CAP
+                ]
+            return carry
+
+        lax.fori_loop(0, width // BLOCK, back_step, 0)
+        for k, other in enumerate(partners):
+            copies.append(
+                send(
+                    token_send.at[pl.ds(k * rows + expert * CAP, CAP)],
+                    back_s.at[pl.ds((k + 1) * rows + expert * CAP, CAP)],
+                    row_sems.at[4, k, expert],
+                    row_sems.at[5, k, expert],
+                    other,
+                )
+            )
+
+    for expert in range(experts):
+
+        def ahead_step(at, carry):
+            cols = block_cols(at)
+            ahead = dot_last(hidden_s[expert], weights[2, expert, cols, :]).astype(BF16)
+            for member in range(members):
+                out_rows[member, expert * CAP : (expert + 1) * CAP, cols] = ahead[
+                    member * CAP : (member + 1) * CAP
+                ]
+            return carry
+
+        lax.fori_loop(0, width // BLOCK, ahead_step, 0)
+
+    place_rows(slot_t, None, places_s)
+    for copy in copies:
+        copy.wait()
+
+    def columns(at, carry):
+        cols = block_cols(at)
+        total = dot_plain(places_s[...], back_s[:, cols])
+        total = total + dot_plain(d_gate_sh[...], gate_sh[:, cols])
+        total = total + dot_plain(d_up_sh[...], up_sh[:, cols])
+        part[:, cols] = total.astype(BF16)
+        return carry
+
+    lax.fori_loop(0, width // BLOCK, columns, 0)
+    for copy in saves:
+        copy.wait()
+
+
+def exchange_rows(slot, gates, slot_t, second, cot, shared_w, gate_parts, up_parts, down_parts):
+    members = len(gate_parts)
+    units, length = slot.shape
+    width = second.shape[1]
+    experts = units // members
+    rows = experts * CAP
+    hidden_width = gate_parts[0].shape[2]
+    shared_width = shared_w[0].shape[0]
+    shape = jax.ShapeDtypeStruct
+    stacked = (experts, members * CAP, width)
+    shared = shape((length, shared_width), BF16)
+    return pl.pallas_call(
+        functools.partial(exchange_kernel, members),
+        out_shape=(
+            shape((length, width), BF16),
+            shape((members, rows, width), BF16),
+            shared,
+            shared,
+            shared,
+            shape(stacked, BF16),
+            shape(stacked, BF16),
+            shape((experts, members * CAP, hidden_width), BF16),
+            shape((experts, members * CAP, 2 * hidden_width), BF16),
         ),
-    )(d_res, scale_rows, xn, *weights, *saved)
+        in_specs=[VMEM] * 8 + [ANY] * (3 * members),
+        out_specs=(VMEM,) * 5 + (ANY,) * 2 + (VMEM,) * 2,
+        scratch_shapes=[
+            pltpu.VMEM(stacked, BF16),
+            pltpu.VMEM(stacked, BF16),
+            pltpu.VMEM(((members - 1) * rows, width), BF16),
+            pltpu.VMEM(((members - 1) * rows, width), BF16),
+            pltpu.VMEM((members * rows, width), BF16),
+            pltpu.VMEM((3, experts, width, hidden_width), BF16),
+            pltpu.VMEM((units * CAP, length), BF16),
+            pltpu.VMEM((units * CAP, 1), F32),
+            pltpu.VMEM((length, units * CAP), BF16),
+            pltpu.SemaphoreType.DMA((6, members - 1, experts)),
+            pltpu.SemaphoreType.DMA((3, members)),
+            pltpu.SemaphoreType.DMA((2,)),
+        ],
+        compiler_params=pltpu.CompilerParams(
+            vmem_limit_bytes=VMEM_LIMIT, collective_id=4, has_side_effects=True
+        ),
+        cost_estimate=KERNEL_COST,
+    )(slot, gates, slot_t, second, cot, *shared_w, *gate_parts, *up_parts, *down_parts)
+
+
+def gather_kernel(
+    rows_n, cols_n, pack, io, taps, pack_all, io_all, taps_all, row_sems, io_sems, tap_sems, own_sems
+):
+    me, at = lax.axis_index("row"), lax.axis_index("col")
+    io_rows = io.shape[0]
+    place = pl.ds(pl.multiple_of(at * io_rows, io_rows), io_rows)
+    row_peers = [{"row": me ^ k} for k in range(1, rows_n)]
+    col_peers = [{"col": at ^ k} for k in range(1, cols_n)]
+    barrier = pltpu.get_barrier_semaphore()
+    for other in row_peers + col_peers:
+        pl.semaphore_signal(barrier, inc=1, device_id=other, device_id_type=MESH)
+    pl.semaphore_wait(barrier, rows_n + cols_n - 2)
+
+    def send(source, target, sems, k, other):
+        copy = pltpu.make_async_remote_copy(
+            src_ref=source,
+            dst_ref=target,
+            send_sem=sems.at[0, k],
+            recv_sem=sems.at[1, k],
+            device_id=other,
+            device_id_type=MESH,
+        )
+        copy.start()
+        return copy
+
+    own = [
+        pltpu.make_async_copy(pack, pack_all.at[me], own_sems.at[0]),
+        pltpu.make_async_copy(io, io_all.at[me, place], own_sems.at[1]),
+        pltpu.make_async_copy(taps, taps_all.at[place], own_sems.at[2]),
+    ]
+    for copy in own:
+        copy.start()
+    io_copies = [
+        send(io, io_all.at[me, place], io_sems, k, other) for k, other in enumerate(col_peers)
+    ]
+    copies = [
+        send(taps, taps_all.at[place], tap_sems, k, other) for k, other in enumerate(col_peers)
+    ]
+    copies += [
+        send(pack, pack_all.at[me], row_sems, k, other) for k, other in enumerate(row_peers)
+    ]
+    own[1].wait()
+    for copy in io_copies:
+        copy.wait()
+    copies += [
+        send(io_all.at[me], io_all.at[me], row_sems, rows_n - 1 + k, other)
+        for k, other in enumerate(row_peers)
+    ]
+    own[0].wait()
+    own[2].wait()
+    for copy in copies:
+        copy.wait()
+
+
+def gather_weights(pack, io, taps, rows_n, cols_n):
+    shape = jax.ShapeDtypeStruct
+    return pl.pallas_call(
+        functools.partial(gather_kernel, rows_n, cols_n),
+        out_shape=(
+            shape((rows_n,) + pack.shape, BF16),
+            shape((rows_n, cols_n * io.shape[0], io.shape[1]), BF16),
+            shape((cols_n * io.shape[0], taps.shape[1]), BF16),
+        ),
+        in_specs=[ANY] * 3,
+        out_specs=(ANY,) * 3,
+        scratch_shapes=[
+            pltpu.SemaphoreType.DMA((2, 2 * (rows_n - 1))),
+            pltpu.SemaphoreType.DMA((2, cols_n - 1)),
+            pltpu.SemaphoreType.DMA((2, cols_n - 1)),
+            pltpu.SemaphoreType.DMA((3,)),
+        ],
+        compiler_params=pltpu.CompilerParams(collective_id=1, has_side_effects=True),
+        cost_estimate=pl.CostEstimate(flops=1, bytes_accessed=1, transcendentals=0),
+    )(pack, io, taps)
 
 
 def row_norm(values, scale_gain):
@@ -571,7 +985,6 @@
     per_device = max(1, local_experts // rows_n)
     split = max(1, rows_n // local_experts)
     part_width = hidden_width // split
-    slots = per_device * CAP
 
     def swap(values, k):
         if k == 0:
@@ -598,6 +1011,9 @@
             total = part if total is None else total + part
         return total
 
+    def after(value, *others):
+        return lax.optimization_barrier((value, *others))[0]
+
     micro = range(micro_count)
     own_rows = [layer_input[m].astype(F32) for m in micro]
     normed = [
@@ -605,30 +1021,31 @@
         for m in micro
     ]
 
-    io_gathered = lax.all_gather(
-        jnp.concatenate(
-            [state_io_proj.astype(F32), state_conv_kernel, state_conv_offset[None, :]], axis=0
-        ),
-        "col",
-        axis=1,
-        tiled=True,
+    own_taps = jnp.concatenate([state_conv_kernel, state_conv_offset[None, :]], axis=0).T
+    tap_parts = []
+    for _ in range(3):
+        tap_parts.append(own_taps.astype(BF16))
+        own_taps = own_taps - tap_parts[-1].astype(F32)
+    tap_parts = jnp.pad(jnp.concatenate(tap_parts, axis=1), ((0, 0), (0, LANES - 15)))
+    step_rows_t = jnp.pad(step_proj.T, ((0, HEAD_ROWS - heads), (0, 0)))
+    in_all, io_all, taps_all = gather_weights(
+        jnp.concatenate([gate_branch_proj.T, conv_in_proj.T, out_proj, step_rows_t], axis=0),
+        state_io_proj.T,
+        tap_parts,
+        rows_n,
+        cols_n,
     )
-    step_rows_t = jnp.pad(step_proj.T, ((0, HEAD_ROWS - heads), (0, 0)))
-    in_full = gather_width(
-        jnp.concatenate(
-            [gate_branch_proj.T, conv_in_proj.T, io_gathered[:depth].astype(BF16).T, step_rows_t],
-            axis=0,
-        )
-    )
-    out_full = gather_width(
-        jnp.concatenate([out_proj, shared_gate.T, shared_up.T, shared_down], axis=0)
-    )
-    wb, wc = in_full[:share], in_full[share : 2 * share]
-    wio = in_full[2 * share : 2 * share + 2 * NS]
-    ws = in_full[2 * share + 2 * NS :]
-    wo = out_full[:share]
-    shared_in = out_full[share : share + 2 * shared_width]
-    shared_out = out_full[share + 2 * shared_width :]
+
+    def join(parts, first, count):
+        return jnp.concatenate(
+            [parts[member, first : first + count] for member in range(rows_n)], axis=1
+        )
+
+    wb, wc, wo = [join(in_all, at * share, share) for at in range(3)]
+    ws = join(in_all, 3 * share, HEAD_ROWS)
+    wio = join(io_all, 0, 2 * NS)
+    taps_all = taps_all.astype(F32)
+    io_taps = jnp.pad(taps_all[:, :5] + taps_all[:, 5:10] + taps_all[:, 10:15], ((0, 0), (0, 3)))
     chan = jnp.concatenate(
         [
             conv_kernel.T,
@@ -639,185 +1056,321 @@
         ],
         axis=1,
     )
-    io_taps = jnp.pad(io_gathered[depth:].T, ((0, 0), (0, 3)))
     head_params = jnp.pad(
         jnp.stack([step_offset, jnp.exp(decay_log)], axis=1), ((0, HEAD_ROWS - heads), (0, 6))
     )
     weights = (wb, wc, wio, ws, wo, chan, io_taps, head_params)
 
-    gate_up = jnp.zeros((per_device, width, 2 * part_width), BF16)
-    down = jnp.zeros((per_device, part_width, width), BF16)
-    for k in range(rows_n):
-        first, hidden_at = unit_of(peer(k))
-        cut = (first, 0, hidden_at)
-        sizes = (per_device, depth, part_width)
-        up_part = jnp.concatenate(
-            [
-                lax.dynamic_slice(expert_gate, cut, sizes),
-                lax.dynamic_slice(expert_up, cut, sizes),
-            ],
-            axis=2,
-        )
-        down_part = lax.dynamic_slice(
-            expert_down, (first, hidden_at, 0), (per_device, part_width, depth)
-        )
-        at = peer(k) * depth
-        gate_up = lax.dynamic_update_slice(gate_up, swap(up_part, k), (0, at, 0))
-        down = lax.dynamic_update_slice(down, swap(down_part, k), (0, 0, at))
+    sizes = (per_device, depth, part_width)
+
+    def unit_parts(weight, transposed, moved=False):
+        parts = []
+        for k in range(rows_n):
+            first, hidden_at = unit_of(peer(k))
+            if transposed:
+                part = lax.dynamic_slice(
+                    weight, (first, hidden_at, 0), (per_device, part_width, depth)
+                )
+                part = jnp.swapaxes(part, 1, 2)
+            else:
+                part = lax.dynamic_slice(weight, (first, 0, hidden_at), sizes)
+            parts.append(swap(after(part, in_all), k) if moved else part)
+        return parts
+
+    gates = unit_parts(expert_gate, False)
+    ups = unit_parts(expert_up, False)
+    downs = unit_parts(expert_down, True, moved=True)
 
     place_j = lax.broadcasted_iota(jnp.int32, (length, length), 0)
     place_i = lax.broadcasted_iota(jnp.int32, (length, length), 1)
     upper = (place_j <= place_i).astype(BF16)
     expert_ids = col_index * local_experts + jnp.arange(local_experts, dtype=jnp.int32)
 
-    def dispatch(m):
+    def slots_of(m):
         hit = routes[m].T[None] == expert_ids[:, None, None]
         mask = jnp.any(hit, axis=1)
         gates = jnp.sum(jnp.where(hit, route_gates[m].T[None], 0.0), axis=1)
         rank = dot_plain(mask.astype(BF16), upper).astype(jnp.int32) - 1
-        slot = jnp.where(mask, rank, -1)
-        picks, slot_gates = [], []
-        for k in range(rows_n):
-            first, _ = unit_of(peer(k))
-            slot_k = lax.dynamic_slice(slot, (first, 0), (per_device, length))
-            gates_k = lax.dynamic_slice(gates, (first, 0), (per_device, length))
-            chosen = slot_k[:, None, :] == jnp.arange(CAP, dtype=jnp.int32)[None, :, None]
-            slot_gates.append(
-                jnp.sum(jnp.where(chosen, gates_k[:, None, :], 0.0), axis=2).reshape(slots, 1)
-            )
-            picks.append(chosen.astype(BF16).reshape(slots, length))
-        return picks, slot_gates
-
-    def stack_rows(parts):
-        return jnp.stack(
-            [part.reshape(per_device, CAP, width) for part in parts], axis=1
-        ).reshape(per_device, rows_n * CAP, width)
-
-    def send_back(rows):
-        rows = rows.astype(BF16).reshape(per_device, rows_n, CAP, width)
-        return [swap(rows[:, k].reshape(slots, width), k) for k in range(rows_n)]
-
-    outputs, input_grads = [], []
-    dense_grads, gate_up_grads, down_grads = [], [], []
-    all_sums, row_sums = [], []
+        slot = jnp.where(mask, rank, -(2**20))
+        firsts = [unit_of(peer(k))[0] for k in range(rows_n)]
+        take = lambda rows: jnp.concatenate(
+            [lax.dynamic_slice(rows, (first, 0), (per_device, length)) for first in firsts], axis=0
+        )
+        return take(slot), take(gates)
+
+    def swap_all(parts):
+        return [swap(part, k) for k, part in enumerate(parts)]
+
+    own_cots = []
     for m in micro:
         positions = col_index * own_count + jnp.arange(own_count)
         valid = (positions < seq_lengths[m, 0])[:, None]
-        own_cot = jnp.where(valid, out_grad[m], jnp.zeros_like(out_grad[m]))
-        cot = lax.all_gather(own_cot, "col", axis=0, tiled=True)
-        xn = normed[m]
-        y, squares, *saved = mixer_forward(xn, *weights, heads)
-        mean_square = lax.psum(jnp.sum(squares, axis=0), "col") / inner
-        inverse_rms = lax.rsqrt(mean_square + EPS)
-        y_own = lax.psum_scatter(y, "col", scatter_dimension=0, tiled=True).astype(F32)
-        own_rms = lax.dynamic_slice(inverse_rms, (col_index * own_count,), (own_count,))
-        residual = own_rows[m] + own_rms[:, None] * y_own
-        second = lax.all_gather(
-            row_norm(residual, second_gain).astype(BF16), "col", axis=0, tiled=True
-        )
-
-        picks, slot_gates = dispatch(m)
-        cot_rows = stack_rows(
+        own_cots.append(jnp.where(valid, out_grad[m], jnp.zeros_like(out_grad[m])))
+    slot_rows = [slots_of(m) for m in micro]
+    slot_cols = [(slot.T, gates.T) for slot, gates in slot_rows]
+
+    last = [None]
+
+    def step(function, *args):
+        if last[0] is not None:
+            args, _ = lax.optimization_barrier((args, last[0]))
+        out = function(*args)
+        last[0] = jax.tree.leaves(out)[0]
+        return out
+
+    state = [{} for _ in micro]
+
+    def mix(m, parts):
+        s = state[m]
+        (s["y_part"], s["squares"], *s["saved"]), received = step(
+            lambda xn, *parts: mixer_forward(parts, xn, *weights, heads), normed[m], *parts[1:]
+        )
+        return [parts[0], *received]
+
+    def sum_y(m, *others):
+        s = state[m]
+        s["y"] = lax.psum_scatter(
+            after(s["y_part"], *others), "col", scatter_dimension=0, tiled=True
+        )
+
+    def scale_of(m):
+        s = state[m]
+        total = step(lambda squares: lax.psum(jnp.sum(squares, axis=0), "col"), s["squares"])
+        s["rms"] = lax.rsqrt(total / inner + EPS)
+
+    def second_norm(m):
+        s = state[m]
+
+        def run(y_own, rms):
+            y_own = y_own.astype(F32)
+            own_rms = lax.dynamic_slice(rms, (col_index * own_count,), (own_count,))
+            residual = own_rows[m] + own_rms[:, None] * y_own
+            return row_norm(residual, second_gain).astype(BF16), residual, y_own
+
+        second, s["residual"], s["y_own"] = step(run, s["y"], s["rms"])
+        s["second"] = lax.all_gather(second, "col", axis=0, tiled=True)
+        if m:
+            s["cot"] = gather_cot(m, second)
+
+    def gather_cot(m, *others):
+        return lax.all_gather(after(own_cots[m], *others), "col", axis=0, tiled=True)
+
+    def exchange(m):
+        s = state[m]
+        slot, gates_of = slot_rows[m]
+        (
+            part,
+            out_rows,
+            s["shared_hidden"],
+            s["d_shared_gate"],
+            s["d_shared_up"],
+            *s["expert_saved"],
+        ) = step(
+            lambda second, cot, gate_parts, up_parts, down_parts: exchange_rows(
+                slot, gates_of, slot_cols[m][0], second, cot, shared_w, gate_parts, up_parts,
+                down_parts,
+            ),
+            s["second"],
+            s["cot"],
+            gates,
+            ups,
+            downs,
+        )
+        s["second_share"] = lax.psum_scatter(part, "col", scatter_dimension=0, tiled=True)
+        s["out_rows"] = swap_all([out_rows[k] for k in range(rows_n)])
+
+    def ahead_rows(m):
+        s = state[m]
+        slot_t, gates_t = slot_cols[m]
+        part = step(
+            lambda rows, left: combine_rows(slot_t, gates_t, rows, left, shared_out),
+            s["out_rows"],
+            s["shared_hidden"],
+        )
+        s["branch_share"] = lax.psum_scatter(part, "col", scatter_dimension=0, tiled=True)
+
+    def second_back(m):
+        s = state[m]
+
+        def run(share_in):
+            back, gain_grad = norm_adjoint(s["residual"], second_gain, share_in.astype(F32))
+            residual_grad = own_cots[m].astype(F32) + back
+            low = residual_grad.astype(BF16)
+            cross = jnp.sum(low.astype(F32) * s["y_own"], axis=1, keepdims=True)
+            parts = [low]
+            for _ in range(3):
+                parts.append(cross.astype(BF16))
+                cross = cross - parts[-1].astype(F32)
+            parts.append(jnp.zeros((own_count, LANES - 3), BF16))
+            return jnp.concatenate(parts, axis=1), residual_grad, gain_grad
+
+        low, s["residual_grad"], s["second_gain_grad"] = step(run, s["second_share"])
+        s["d_res"] = lax.all_gather(low, "col", axis=0, tiled=True)
+
+    def mix_back(m, parts):
+        s = state[m]
+        scale_rows = jnp.pad(
+            jnp.stack([s["rms"], jnp.full((length,), 1.0 / inner, F32)]), ((0, 6), (0, 0))
+        )
+        (first_part, *s["back"]), received = step(
+            lambda d_res, scales, *parts: mixer_backward(
+                parts, d_res, scales, normed[m], weights, s["saved"], heads
+            ),
+            s["d_res"],
+            scale_rows,
+            *parts[1:],
+        )
+        s["first_share"] = lax.psum_scatter(first_part, "col", scatter_dimension=0, tiled=True)
+        return [parts[0], *received]
+
+    def total_of(parts):
+        return jax.tree.map(lambda *terms: functools.reduce(jnp.add, terms), *parts)
+
+    def expert_grads(*saved):
+        def over_rows(left, right):
+            return jnp.einsum("ecd,ech->edh", left, right, preferred_element_type=F32)
+
+        totals = total_of(
             [
-                swap((dot_plain(picks[k], cot) * slot_gates[k]).astype(BF16), k)
+                (over_rows(tokens, d_pre), over_rows(cot, hidden))
+                for tokens, cot, hidden, d_pre in saved
+            ]
+        )
+        both, down = totals[0].astype(BF16), totals[1].astype(BF16)
+        return [
+            [
+                lax.dynamic_slice(full, (0, peer(k) * depth, at), (per_device, depth, part_width))
                 for k in range(rows_n)
             ]
-        )
-        token_rows = stack_rows(
-            [swap(dot_plain(picks[k], second).astype(BF16), k) for k in range(rows_n)]
-        )
-        pre = jnp.einsum("ecd,edh->ech", token_rows, gate_up, preferred_element_type=F32)
-        gate_pre, up_pre = pre[..., :part_width], pre[..., part_width:]
-        hidden = (jax.nn.silu(gate_pre) * up_pre).astype(BF16)
-        d_hidden = jnp.einsum("ecd,ehd->ech", cot_rows, down, preferred_element_type=F32)
-        d_pre = jnp.concatenate(
-            [
-                (d_hidden * up_pre * silu_slope(gate_pre)).astype(BF16),
-                (d_hidden * jax.nn.silu(gate_pre)).astype(BF16),
-            ],
-            axis=2,
-        )
-        d_rows = jnp.einsum("ech,edh->ecd", d_pre, gate_up, preferred_element_type=F32)
-        out_rows = jnp.einsum("ech,ehd->ecd", hidden, down, preferred_element_type=F32)
-        gate_up_grads.append(
-            jnp.einsum("ecd,ech->edh", token_rows, d_pre, preferred_element_type=F32)
-        )
-        down_grads.append(
-            jnp.einsum("ech,ecd->ehd", hidden, cot_rows, preferred_element_type=F32)
-        )
-
-        shared_pre = dot_last(second, shared_in)
-        shared_gate_pre = shared_pre[:, :shared_width]
-        shared_up_pre = shared_pre[:, shared_width:]
-        shared_hidden = (jax.nn.silu(shared_gate_pre) * shared_up_pre).astype(BF16)
-        d_shared = dot_last(cot, shared_out)
-        d_shared_pre = jnp.concatenate(
-            [
-                (d_shared * shared_up_pre * silu_slope(shared_gate_pre)).astype(BF16),
-                (d_shared * jax.nn.silu(shared_gate_pre)).astype(BF16),
-            ],
-            axis=1,
-        )
-
-        pick_all = jnp.concatenate(picks, axis=0)
-        back_rows = jnp.concatenate(send_back(d_rows), axis=0)
-        second_part = dot_first(pick_all, back_rows) + dot_plain(d_shared_pre, shared_in)
-        second_share = lax.psum_scatter(
-            second_part.astype(BF16), "col", scatter_dimension=0, tiled=True
-        ).astype(F32)
-        residual_back, second_gain_grad = norm_adjoint(residual, second_gain, second_share)
-        residual_grad = own_cot.astype(F32) + residual_back
-        residual_low = residual_grad.astype(BF16)
-        d_res = lax.all_gather(residual_low, "col", axis=0, tiled=True)
-        cross = lax.all_gather(
-            jnp.sum(residual_low.astype(F32) * y_own, axis=1), "col", axis=0, tiled=True
-        )
-        cube = inverse_rms * inverse_rms * inverse_rms * cross / inner
-        scale_rows = jnp.pad(jnp.stack([inverse_rms, cube]), ((0, 6), (0, 0)))
-        (
-            first_part,
-            gain_part,
-            mixed,
-            d_branch,
-            d_conv,
-            d_io,
-            d_step,
-            chan_grad,
-            io_grad,
-            head_grad,
-        ) = mixer_backward(d_res, scale_rows, xn, weights, saved, heads)
-        first_share = lax.psum_scatter(
-            first_part, "col", scatter_dimension=0, tiled=True
-        ).astype(F32)
-        rows_back, _ = norm_adjoint(own_rows[m], first_gain, first_share)
-        input_grads.append(residual_grad + rows_back)
-
-        out_back = jnp.concatenate(
-            [
-                (gate * rows.astype(F32)).astype(BF16)
-                for gate, rows in zip(slot_gates, send_back(out_rows))
-            ],
-            axis=0,
-        )
-        branch_part = dot_first(pick_all, out_back) + dot_plain(shared_hidden, shared_out)
-        branch_share = lax.psum_scatter(
-            branch_part.astype(BF16), "col", scatter_dimension=0, tiled=True
-        ).astype(F32)
-        outputs.append((residual + branch_share).astype(BF16))
-
-        dense_grads.append(
-            (
+            for full, at in ((both, 0), (both, part_width), (down, 0))
+        ]
+
+    def finish_output(m):
+        s = state[m]
+        s["output"] = step(
+            lambda share_in: (s["residual"] + share_in.astype(F32)).astype(BF16), s["branch_share"]
+        )
+
+    def finish_input(m):
+        s = state[m]
+
+        def run(share_in):
+            back, _ = norm_adjoint(own_rows[m], first_gain, share_in.astype(F32))
+            return s["residual_grad"] + back
+
+        s["input_grad"] = step(run, s["first_share"])
+
+    def dense_grads(m):
+        s = state[m]
+        _, mixed, d_branch, d_conv, d_io, d_step, *_ = s["back"]
+
+        def run(xn, d_res, mixed, d_branch, d_conv, d_io, d_step):
+            return (
+                dot_plain(d_io, xn),
                 dot_plain(d_branch, xn),
                 dot_plain(d_conv, xn),
-                dot_plain(d_io, xn),
+                dot_plain(mixed, d_res)[:, :width],
                 dot_plain(d_step, xn),
-                dot_plain(mixed, d_res),
-                dot_first(d_shared_pre, second),
-                dot_first(shared_hidden, cot),
             )
-        )
+
+        s["dense"] = step(run, normed[m], s["d_res"], mixed, d_branch, d_conv, d_io, d_step)
+
+    def shared_grads(m):
+        s = state[m]
+
+        def run(second, cot, hidden, d_gate, d_up):
+            return dot_first(d_gate, second), dot_first(d_up, second), dot_first(hidden, cot)
+
+        s["shared_grads"] = step(
+            run, s["second"], s["cot"], s["shared_hidden"], s["d_shared_gate"], s["d_shared_up"]
+        )
+
+    def place_expert_grads(gate_parts, up_parts, down_parts):
+        expert_gate_grad = jnp.zeros(expert_gate.shape, F32)
+        expert_up_grad = jnp.zeros(expert_up.shape, F32)
+        expert_down_grad = jnp.zeros(expert_down.shape, F32)
+        for k in range(rows_n):
+            first, hidden_at = unit_of(peer(k))
+            place = (first, 0, hidden_at)
+            expert_gate_grad = lax.dynamic_update_slice(
+                expert_gate_grad, gate_parts[k].astype(F32), place
+            )
+            expert_up_grad = lax.dynamic_update_slice(
+                expert_up_grad, up_parts[k].astype(F32), place
+            )
+            expert_down_grad = lax.dynamic_update_slice(
+                expert_down_grad,
+                jnp.swapaxes(down_parts[k].astype(F32), 1, 2),
+                (first, hidden_at, 0),
+            )
+        return expert_gate_grad, expert_up_grad, expert_down_grad
+
+    def arrive(parts):
+        return step(lambda *values: values, *parts)
+
+    first, second = 0, micro_count - 1
+    state[first]["cot"] = gather_cot(first, normed[second])
+    gates = mix(first, gates)
+    (state[first]["cot"],) = arrive([state[first]["cot"]])
+    sum_y(first)
+    ups = mix(second, ups)
+    scale_of(first)
+    second_norm(first)
+    sum_y(second)
+    downs = arrive(downs)
+    shared_full = step(
+        lambda *parts: gather_width(jnp.concatenate(parts, axis=0)),
+        shared_gate.T,
+        shared_up.T,
+        shared_down,
+    )
+    shared_w = (
+        shared_full[:shared_width],
+        shared_full[shared_width : 2 * shared_width],
+        shared_full[2 * shared_width :],
+    )
+    shared_out = shared_w[2]
+    scale_of(second)
+    second_norm(second)
+    exchange(first)
+    exchange(second)
+    second_back(first)
+    gate_grads, up_grads, down_grads = step(expert_grads, *[s["expert_saved"] for s in state])
+    second_back(second)
+    ahead_rows(first)
+    gate_grads = mix_back(first, gate_grads)
+    ahead_rows(second)
+    down_grads = swap_all(down_grads)
+    shared_grads(first)
+    shared_grads(second)
+    dense_grads(first)
+    finish_output(first)
+    up_grads = mix_back(second, up_grads)
+    dense_grads(second)
+    finish_input(first)
+    expert_gate_grad, expert_up_grad, expert_down_grad = step(
+        place_expert_grads, gate_grads, up_grads, down_grads
+    )
+    shared = step(
+        lambda *parts: add_shares(jnp.concatenate(parts, axis=0).astype(BF16)),
+        *total_of([s["shared_grads"] for s in state])
+    )
+    shared_in_grad, down_grad = shared[: 2 * shared_width], shared[2 * shared_width :]
+    finish_output(second)
+    io_sum, *dense = total_of([s["dense"] for s in state])
+    io_sum = lax.psum_scatter(io_sum.astype(BF16), "col", scatter_dimension=0, tiled=True)
+    dense = add_shares(jnp.concatenate(dense, axis=0).astype(BF16))
+    branch_grad, conv_grad = dense[:share], dense[share : 2 * share]
+    out_grad_sum, step_grad = dense[2 * share : 3 * share], dense[3 * share :]
+    all_sums, row_sums = [], []
+    for s in state:
+        gain_part, *_, chan_grad, io_grad, head_grad = s["back"]
         all_sums.append(
-            (jnp.sum(gain_part, axis=0) / first_gain, second_gain_grad, io_grad[:, :5].reshape(-1))
+            (
+                jnp.sum(gain_part, axis=0) / first_gain,
+                s["second_gain_grad"],
+                io_grad[:, :5].reshape(-1),
+            )
         )
         row_sums.append(
             (
@@ -827,43 +1380,14 @@
                 head_grad[:heads, 1],
             )
         )
-
-    def total_of(parts):
-        return jax.tree.map(lambda *terms: functools.reduce(jnp.add, terms), *parts)
-
-    gate_up_total = total_of(gate_up_grads).astype(BF16)
-    down_total = total_of(down_grads).astype(BF16)
-    expert_gate_grad = jnp.zeros(expert_gate.shape, F32)
-    expert_up_grad = jnp.zeros(expert_up.shape, F32)
-    expert_down_grad = jnp.zeros(expert_down.shape, F32)
-    for k in range(rows_n):
-        at = peer(k) * depth
-        first, hidden_at = unit_of(peer(k))
-        part = swap(
-            lax.dynamic_slice(gate_up_total, (0, at, 0), (per_device, depth, 2 * part_width)), k
-        ).astype(F32)
-        place = (first, 0, hidden_at)
-        expert_gate_grad = lax.dynamic_update_slice(expert_gate_grad, part[..., :part_width], place)
-        expert_up_grad = lax.dynamic_update_slice(expert_up_grad, part[..., part_width:], place)
-        part = swap(
-            lax.dynamic_slice(down_total, (0, 0, at), (per_device, part_width, depth)), k
-        ).astype(F32)
-        expert_down_grad = lax.dynamic_update_slice(expert_down_grad, part, (first, hidden_at, 0))
-
-    dense = add_shares(jnp.concatenate(total_of(dense_grads), axis=0).astype(BF16))
-    ends = []
-    at = 0
-    for rows in (share, share, 2 * NS, HEAD_ROWS, share, 2 * shared_width, shared_width):
-        ends.append(dense[at : at + rows])
-        at += rows
-    branch_grad, conv_grad, io_proj_part, step_grad, out_grad_sum, shared_in_grad, down_grad = ends
-    io_proj_grad = lax.psum_scatter(io_proj_part, "col", scatter_dimension=0, tiled=True)
-
     all_total = total_of(all_sums)
     row_total = total_of(row_sums)
-    sums = lax.psum(jnp.concatenate(all_total + row_total), "row")
+    small = jnp.concatenate(all_total + row_total)
+    sums = functools.reduce(jnp.add, [swap(small, k) for k in range(rows_n)])
     all_count = sum(part.shape[0] for part in all_total)
     all_values = lax.psum(sums[:all_count], "col")
+    io_proj_grad = add_shares(io_sum)
+    finish_input(second)
     first_gain_grad = all_values[:width]
     second_gain_grad = all_values[width : 2 * width]
     io_values = lax.dynamic_slice(
@@ -872,8 +1396,8 @@
     chan_values = sums[all_count : all_count + 6 * share].reshape(share, 6)
     head_values = sums[all_count + 6 * share :]
     return (
-        jnp.stack(outputs),
-        jnp.stack(input_grads),
+        jnp.stack([s["output"] for s in state]),
+        jnp.stack([s["input_grad"] for s in state]),
         first_gain_grad,
         branch_grad.T,
         conv_grad.T,

time: 1210 us -> 1030 us (0.85)
  Pallas kernels: 150 us -> 549 us
  waiting for transfers between devices: 479 us -> 150 us
  matrix products: 171 us -> 60.1 us
  blocking collectives: 145 us -> 54.4 us
  starting transfers between devices: 57.5 us -> 33.8 us
  local copies, waits for them, and re-layouts: 112 us -> 91.6 us
    pallas_call x0 -> x5, Pallas kernels: none -> 363 us  [the longest x2 288 us: exchange_rows(): pl.pallas_call(functools.partial(exchange_kernel, members), out_shape=(sh...]
    ppermute x45 -> x27, waiting for transfers between devices: 349 us -> 84.1 us  [swap(): return lax.ppermute(values, 'row', [(i, i ^ k) for i in range(rows_n)])]
    reduce_scatter x9, waiting for transfers between devices: 100 us -> 4.17 us  [the longest x2 4.1 us: exchange(): lax.psum_scatter(part, 'col', scatter_dimension=0, tiled=True)]
    dot_general x44 -> x18, matrix products: 102 us -> 35.8 us  [contract(): lax.dot_general(left_op, right_op, (((left_dim,), (right_dim,)), ((), ())...]
    psum x2, blocking collectives: 83.3 us -> 27.8 us  [scale_of(): lax.psum(jnp.sum(squares, axis=0), 'col')]
    dot_general x12 -> x4, matrix products: 69.3 us -> 24.3 us  [over_rows(): return jnp.einsum('ecd,ech->edh', left, right, preferred_element_type=F32)]
    all_gather x3 -> x0, blocking collectives: 36 us -> none  [the longest x2 18.4 us: local(): lax.all_gather(jnp.sum(residual_low.astype(F32) * y_own, axis=1), 'col',...]
    all_gather x2, waiting for transfers between devices: 0.02 us -> 35.7 us  [local(): lax.all_gather(row_norm(own_rows[m], first_gain).astype(BF16), 'col', axi...]
  transfers between devices with their start and end apart: 62 -> 44, of which waited for: 20 -> 10; matrix products, arithmetic and copies ran while one was open for 27% -> 20% of each run, Pallas kernels for 12% -> 54%
where the time goes in v2:
time: 1030 us; the launch traced here: 1020 us
  Pallas kernels  549 us (53%)
  waiting for transfers between devices  150 us (15%)
  local copies, waits for them, and re-layouts  91.6 us (9%)
  other arithmetic  68.1 us (7%)
  matrix products  60.1 us (6%)
  blocking collectives  54.4 us (5%)
  starting transfers between devices  33.8 us (3%)
  between operations  15.8 us (2%)
    pallas_call x2, Pallas kernels, exchange_rows(): pl.pallas_call(functools.partial(exchange_kernel, members), out_shape=(sh...  288 us
    pallas_call x2, Pallas kernels, mixer_backward(): pl.pallas_call(functools.partial(mixer_backward_kernel, heads), out_shape...  98 us
    pallas_call x2, Pallas kernels, mixer_forward(): pl.pallas_call(functools.partial(mixer_forward_kernel, heads), out_shape=...  87.2 us
    ppermute x27, waiting for transfers between devices, swap(): return lax.ppermute(values, 'row', [(i, i ^ k) for i in range(rows_n)])  84.1 us
    pallas_call x1, Pallas kernels, gather_weights(): pl.pallas_call(functools.partial(gather_kernel, rows_n, cols_n), out_shap...  52.3 us
    dot_general x18, matrix products, contract(): lax.dot_general(left_op, right_op, (((left_dim,), (right_dim,)), ((), ())...  35.8 us
    all_gather x2, waiting for transfers between devices, local(): lax.all_gather(row_norm(own_rows[m], first_gain).astype(BF16), 'col', axi...  35.7 us
    ppermute x27, starting transfers between devices, swap(): return lax.ppermute(values, 'row', [(i, i ^ k) for i in range(rows_n)])  31.8 us
  transfers between devices with their start and end apart: 44, of which 10 were waited for; matrix products, arithmetic and copies ran while one was open for 20% of the time, Pallas kernels for 54%

profile of v2, /device:TPU:0, one launch (start us, length us, event | category | flops | bytes accessed | tf_op | source)
XLA Modules:
  0.0 1022.4 jit_solution(9676942201325532149)
XLA Ops:
  8.8 2.3 fusion.49
  16.5 35.7 %all-gather.11.cloned.1.call-done.xn = bf16[1024,1536]{1,0:T(8,128)(2,1)} async-done(((bf16[128,1536]{1,0:T(8,128)(2,1)}), bf16[1024,1536]{1,0:T(8,128)(2,1)}) %all-gather.11.cloned.1.call-update) | async-done | bytes 3145744 | tf_op jit(solution)/shard_map/all_gather | solution.py:1020
  53.0 52.3 %shard_map.425 = (bf16[4,1168,384]{2,1,0:T(8,128)(2,1)}, bf16[4,256,384]{2,1,0:T(8,128)(2,1)}, bf16[256,128]{1,0:T(8,128)(2,1)}) custom-call(bf16[1168,384]{1,0:T(8,128)(2,1)} %fusion.32.pack, bf16[32,384]{1,0:T(8,128)(2,1)} %bitcast.251, bf16[32,128]{1,0:T(8,128)(2,1)} %fusion.65.taps), custom_call_target="tpu_custom_call" | custom-call | flops 1 | bytes 1 | tf_op jit(solution)/shard_map/pallas_call | solution.py:912
  108.7 3.8 constant_dynamic-slice_fusion.35
  117.3 44.1 %shard_map.426 = (bf16[1024,1536]{1,0:T(8,128)(2,1)}, f32[8,1024]{1,0:T(8,128)}, f32[384,1024]{1,0:T(8,128)}, f32[384,1024]{1,0:T(8,128)}, f32[256,1024]{1,0:T(8...) custom-call(bf16[1024,1536]{1,0:T(8,128)(2,1)} %all-gather.9.cloned., ...), custom_call_target="tpu_custom_call" | custom-call | flops 30000001024 | bytes 1048576 | tf_op jit(solution)/shard_map/pallas_call | solution.py:261
  161.5 3.6 constant_dynamic-slice_fusion.34
  165.1 43.1 %shard_map.427 = (bf16[1024,1536]{1,0:T(8,128)(2,1)}, f32[8,1024]{1,0:T(8,128)}, f32[384,1024]{1,0:T(8,128)}, f32[384,1024]{1,0:T(8,128)}, f32[256,1024]{1,0:T(8...) custom-call(bf16[1024,1536]{1,0:T(8,128)(2,1)} %all-gather.11.cloned, ...), custom_call_target="tpu_custom_call" | custom-call | flops 30000001024 | bytes 1048576 | tf_op jit(solution)/shard_map/pallas_call | solution.py:261
  209.0 14.2 %psum.21 = f32[1024]{0:T(1024)S(1)} all-reduce(f32[1024]{0:T(1024)S(1)} %reduce_sum.202), channel_id=1, replica_groups=mesh['row'=4,'col'=8] {'col'}, use_global_device_ids=true, to_apply=%region_4.5 | all-reduce | flops 1024 | bytes 8192 | tf_op jit(solution)/shard_map/psum | solution.py:1138
  226.9 3.1 constant_dynamic-slice_fusion.30
  230.1 2.3 copy.273
  235.1 2.4 collective-permute-start.2
  238.9 14.3 %collective-permute-done.refs_9_ = bf16[2,384,512]{2,1,0:T(8,128)(2,1)} collective-permute-done((bf16[2,384,512]{2,1,0:T(8,128)(2,1)}, bf16[2,384,512]{2,1,0:T(8,128)(2,1)}, u32[]{:S(2)}, u32[]{:S(2)}) %collective-permute-start) | collective-permute-done | bytes 786464 | tf_op jit(solution)/shard_map/ppermute | solution.py:992
  253.2 16.7 %collective-permute-done.1.refs_10_ = bf16[2,384,512]{2,1,0:T(8,128)(2,1)} collective-permute-done((bf16[2,384,512]{2,1,0:T(8,128)(2,1)}, bf16[2,384,512]{2,1,0:T(8,128)(2,1)}, u32[]{:S(2)}, u32[]{:S(2)}) %collective-permute-start.1) | collective-permute-done | bytes 786464 | tf_op jit(solution)/shard_map/ppermute | solution.py:992
  273.7 6.3 collective-permute-done.3
  280.1 5.2 collective-permute-done.4
  286.1 13.6 %psum.22 = f32[1024]{0:T(1024)S(1)} all-reduce(f32[1024]{0:T(1024)S(1)} %reduce_sum.205), channel_id=1, replica_groups=mesh['row'=4,'col'=8] {'col'}, use_global_device_ids=true, to_apply=%region_10.11 | all-reduce | flops 1024 | bytes 8192 | tf_op jit(solution)/shard_map/psum | solution.py:1138
  307.5 145.5 %shard_map.428 = (bf16[1024,1536]{1,0:T(8,128)(2,1)}, bf16[4,288,1536]{2,1,0:T(8,128)(2,1)}, bf16[1024,128]{1,0:T(8,128)(2,1)}, bf16[1024,128]{1,0:T(8,128)(2,1)...) custom-call(s32[8,1024]{1,0:T(8,128)} %copy-done.53, ...), custom_call_target="tpu_custom_call" | custom-call | flops 30000001024 | bytes 1048576 | tf_op jit(solution)/shard_map/pallas_call | solution.py:820
  455.4 142.3 %shard_map.429 = (bf16[1024,1536]{1,0:T(8,128)(2,1)}, bf16[4,288,1536]{2,1,0:T(8,128)(2,1)}, bf16[1024,128]{1,0:T(8,128)(2,1)}, bf16[1024,128]{1,0:T(8,128)(2,1)...) custom-call(s32[8,1024]{1,0:T(8,128)} %copy-done.54, ...), custom_call_target="tpu_custom_call" | custom-call | flops 30000001024 | bytes 1048576 | tf_op jit(solution)/shard_map/pallas_call | solution.py:820
  599.4 3.6 slice_bitcast_fusion.4
  611.2 10.5 %fusion.83 = f32[2,1536,1024]{2,1,0:T(8,128)} fusion(bf16[2,576,1536]{2,1,0:T(8,128)(2,1)} %get-tuple-element.295, bf16[2,576,1024]{2,1,0:T(8,128)(2,1)} %get-tuple-element.296), kind=kOutput, calls=%fused_computation.282 | convolution fusion | flops 3623878656 | bytes 18481152 | tf_op jit(solution)/shard_map/ecd,ech->edh/dot_general | solution.py:1231
  621.7 8.2 add_convert_fusion
  630.0 2.7 constant_dynamic-slice_fusion.14
  632.7 4.1 reduce-scatter.14.cloned.1.call-done
  641.1 11.6 %shard_map.430 = bf16[1024,1536]{1,0:T(8,128)(2,1)} custom-call(s32[1024,8]{1,0:T(8,128)} %bitcast.246, f32[1024,8]{1,0:T(8,128)} %bitcast.247, bf16[1024,128]{1,0:T(8,128)(2,1)} %get-tuple-element.342.extra_left, bf16[128,1536]{1,0:T(8,128)(2,1)} %get-tuple-element.624.down_sh.extra_right, bf16[288,1536]{1,0:T(8,128)(2,1)} %get-tuple-element.301.refs_0_, ...), custom_call_target="tpu_custom_call" | custom-call | flops 30000001024 | bytes 1048576 | tf_op jit(solution)/shard_map/pallas_call | solution.py:554
  654.4 23.6 %all-gather.21.cloned.1.call-done.d_res = bf16[1024,1664]{1,0:T(8,128)(2,1)} async-done(((bf16[128,1664]{1,0:T(8,128)(2,1)}), bf16[1024,1664]{1,0:T(8,128)(2,1)}) %all-gather.21.cloned.1.call-update) | async-done | bytes 3407888 | tf_op jit(solution)/shard_map/all_gather | solution.py:1208
  678.0 49.7 %shard_map.431 = (bf16[1024,1536]{1,0:T(8,128)(2,1)}, f32[8,1536]{1,0:T(8,128)}, bf16[384,1024]{1,0:T(8,128)(2,1)}, bf16[384,1024]{1,0:T(8,128)(2,1)}, bf16[384,...) custom-call(bf16[1024,1664]{1,0:T(8,128)(2,1)} %all-gather.21.cloned, ...), custom_call_target="tpu_custom_call" | custom-call | flops 30000001024 | bytes 1048576 | tf_op jit(solution)/shard_map/pallas_call | solution.py:514
  730.1 3.3 slice_bitcast_fusion
  736.8 2.7 fusion.88
  739.5 2.9 add_convert_fusion.1
  745.9 28.9 %collective-permute-done.10.refs_2_ = bf16[288,1536]{1,0:T(8,128)(2,1)S(1)} collective-permute-done((bf16[288,1536]{1,0:T(8,128)(2,1)S(1)}, bf16[288,1536]{1,0:T(8,128)(2,1)S(1)}, u32[]{:S(2)}, u32[]{:S(2)}) %collective-permute-start.10) | collective-permute-done | bytes 884768 | tf_op jit(solution)/shard_map/ppermute | solution.py:992
  777.2 11.8 %shard_map.432 = bf16[1024,1536]{1,0:T(8,128)(2,1)} custom-call(s32[1024,8]{1,0:T(8,128)} %bitcast.244, f32[1024,8]{1,0:T(8,128)} %bitcast.248, bf16[1024,128]{1,0:T(8,128)(2,1)} %get-tuple-element.344.extra_left, bf16[128,1536]{1,0:T(8,128)(2,1)} %get-tuple-element.624.down_sh.extra_right, bf16[288,1536]{1,0:T(8,128)(2,1)} %get-tuple-element.329.refs_0_, ...), custom_call_target="tpu_custom_call" | custom-call | flops 30000001024 | bytes 1048576 | tf_op jit(solution)/shard_map/pallas_call | solution.py:554
  789.0 2.7 fusion.84
  794.9 2.8 fusion.87
  797.9 2.5 convolution_add_fusion.3
  802.5 3.4 convolution_add_fusion.2
  808.1 2.8 fusion.89
  810.9 2.8 fusion.90
  815.7 48.3 %shard_map.433 = (bf16[1024,1536]{1,0:T(8,128)(2,1)}, f32[8,1536]{1,0:T(8,128)}, bf16[384,1024]{1,0:T(8,128)(2,1)}, bf16[384,1024]{1,0:T(8,128)(2,1)}, bf16[384,...) custom-call(bf16[1024,1664]{1,0:T(8,128)(2,1)} %all-gather.23.cloned, ...), custom_call_target="tpu_custom_call" | custom-call | flops 30000001024 | bytes 1048576 | tf_op jit(solution)/shard_map/pallas_call | solution.py:514
  885.5 3.9 add_convert_fusion.2
  889.5 4.4 fusion.9
  904.3 2.2 collective-permute-start.14
  909.8 26.6 %psum.23 = f32[4352]{0:T(1024)S(1)} all-reduce(f32[4352]{0:T(1024)S(1)} %slice.321), channel_id=1, replica_groups=mesh['row'=4,'col'=8] {'col'}, use_global_device_ids=true, to_apply=%region_32.33 | all-reduce | flops 4352 | bytes 34816 | tf_op jit(solution)/shard_map/psum | solution.py:1388
  941.2 2.5 fusion.53
  961.2 3.2 broadcast_in_dim.101
  968.9 3.5 broadcast.152.clone.1
  986.0 11.2 %collective-permute-done.23 = bf16[1168,384]{1,0:T(8,128)(2,1)} collective-permute-done((bf16[1168,384]{1,0:T(8,128)(2,1)S(1)}, bf16[1168,384]{1,0:T(8,128)(2,1)}, u32[]{:S(2)}, u32[]{:S(2)}) %collective-permute-start.23) | collective-permute-done | bytes 897056 | tf_op jit(solution)/shard_map/ppermute | solution.py:992
  997.2 2.4 convert_add_fusion
  1005.8 2.2 copy.264
  (505 shorter events, 165.1 us)
Async XLA Ops:
  7.3 45.0 %all-gather.11.cloned.1.call-start = ((), (), s32[]{:S(2)}) async-start(), calls=%async_computation.11 | async-start | bytes 3538944 | tf_op jit(solution)/shard_map/all_gather | solution.py:1020
  11.1 106.3 %all-gather.9.cloned.1.call-start = ((), (), s32[]{:S(2)}) async-start(), calls=%async_computation.9 | async-start | bytes 3538944 | tf_op jit(solution)/shard_map/all_gather | solution.py:1020
  11.9 153.2 %all-gather.13.cloned.1.call-start = ((), (), s32[]{:S(2)}) async-start(), calls=%async_computation.12 | async-start | bytes 3538944 | tf_op jit(solution)/shard_map/all_gather | solution.py:1156
  52.3 171.0 %reduce-scatter.10.cloned.1.call-start = ((), (), s32[]{:S(2)}) async-start(), calls=%async_computation.10 | async-start | bytes 3538944 | tf_op jit(solution)/shard_map/reduce_scatter | solution.py:1132
  161.5 138.3 %reduce-scatter.12.cloned.1.call-start = ((), (), s32[]{:S(2)}) async-start(), calls=%async_computation.14 | async-start | bytes 3538944 | tf_op jit(solution)/shard_map/reduce_scatter | solution.py:1132
  208.3 99.2 %all-gather.15.cloned.1.call-start = ((), (), s32[]{:S(2)}) async-start(), calls=%async_computation.13 | async-start | bytes 3538944 | tf_op jit(solution)/shard_map/all_gather | solution.py:1151
  223.3 384.6 %copy-start.67 = (f32[128]{0:T(128)}, f32[128]{0:T(128)S(1)}, u32[]{:S(2)}) copy-start(f32[128]{0:T(128)S(1)} %dynamic_slice.180) | copy-start | bytes 1540
  224.6 383.3 %copy-start.76 = (f32[128]{0:T(128)}, f32[128]{0:T(128)S(1)}, u32[]{:S(2)}) copy-start(f32[128]{0:T(128)S(1)} %add_rsqrt_fusion.3) | copy-start | bytes 1540
  226.7 228.6 %all-gather.19.cloned.1.call-start = ((), (), s32[]{:S(2)}) async-start(), calls=%async_computation.16 | async-start | bytes 3538944 | tf_op jit(solution)/shard_map/all_gather | solution.py:1156
  232.4 20.8 %collective-permute-start = (bf16[2,384,512]{2,1,0:T(8,128)(2,1)}, bf16[2,384,512]{2,1,0:T(8,128)(2,1)}, u32[]{:S(2)}, u32[]{:S(2)}) collective-permute-start(bf16[2,384,512]{2,1,0:T(8,128)(2,1)} %bitcast.240), channel_id=1, source_target_pairs={{0,8},{8,0},{16,24},{24,16},{1,9},{9,1},{17,25},{25,17},{2,10},{10... | collective-permute-start | bytes 2359304 | tf_op jit(solution)/shard_map/ppermute | solution.py:992
  234.0 35.9 %collective-permute-start.1 = (bf16[2,384,512]{2,1,0:T(8,128)(2,1)}, bf16[2,384,512]{2,1,0:T(8,128)(2,1)}, u32[]{:S(2)}, u32[]{:S(2)}) collective-permute-start(bf16[2,384,512]{2,1,0:T(8,128)(2,1)} %bitcast.241), channel_id=1, source_target_pairs={{0,16},{8,24},{16,0},{24,8},{1,17},{9,25},{17,1},{25,9},{2,18},{10... | collective-permute-start | bytes 2359304 | tf_op jit(solution)/shard_map/ppermute | solution.py:992
  235.1 34.8 %collective-permute-start.2 = (bf16[2,384,512]{2,1,0:T(8,128)(2,1)S(1)}, bf16[2,384,512]{2,1,0:T(8,128)(2,1)}, u32[]{:S(2)}, u32[]{:S(2)}) collective-permute-start(bf16[2,384,512]{2,1,0:T(8,128)(2,1)S(1)} %bitcast.242), channel_id=1, source_target_pairs={{0,24},{8,16},{16,8},{24,0},{1,25},{9,17},{17,9},{25,1},{2,26},{10... | collective-permute-start | bytes 2359304 | tf_op jit(solution)/shard_map/ppermute | solution.py:992
  270.0 10.0 collective-permute-start.3
  271.8 13.4 %collective-permute-start.4 = (bf16[384,384]{1,0:T(8,128)(2,1)S(1)}, bf16[384,384]{1,0:T(8,128)(2,1)S(1)}, u32[]{:S(2)}, u32[]{:S(2)}) collective-permute-start(bf16[384,384]{1,0:T(8,128)(2,1)S(1)} %constant_dynamic-update-slice_fusion.8), channel_id=1, source_target_pairs={{0,16},{8,24},{16,0},{24,8},{1,17},{9,25},{17,1},{25,9},{2,18},{10... | collective-permute-start | bytes 884744 | tf_op jit(solution)/shard_map/ppermute | solution.py:992
  272.1 13.2 %collective-permute-start.5 = (bf16[384,384]{1,0:T(8,128)(2,1)S(1)}, bf16[384,384]{1,0:T(8,128)(2,1)S(1)}, u32[]{:S(2)}, u32[]{:S(2)}) collective-permute-start(bf16[384,384]{1,0:T(8,128)(2,1)S(1)} %constant_dynamic-update-slice_fusion.8), channel_id=1, source_target_pairs={{0,24},{8,16},{16,8},{24,0},{1,25},{9,17},{17,9},{25,1},{2,26},{10... | collective-permute-start | bytes 884744 | tf_op jit(solution)/shard_map/ppermute | solution.py:992
  299.8 338.4 %copy-start.65 = (f32[128]{0:T(128)}, f32[128]{0:T(128)S(1)}, u32[]{:S(2)}) copy-start(f32[128]{0:T(128)S(1)} %dynamic_slice.195) | copy-start | bytes 1540
  301.2 337.1 %copy-start.74 = (f32[128]{0:T(128)}, f32[128]{0:T(128)S(1)}, u32[]{:S(2)}) copy-start(f32[128]{0:T(128)S(1)} %add_rsqrt_fusion.2) | copy-start | bytes 1540
  303.2 152.1 %all-gather.17.cloned.1.call-start = ((), (), s32[]{:S(2)}) async-start(), calls=%async_computation.15 | async-start | bytes 3538944 | tf_op jit(solution)/shard_map/all_gather | solution.py:1151
  304.0 302.5 %reduce-scatter.16.cloned.1.call-start = ((), (), s32[]{:S(2)}) async-start(), calls=%async_computation.18 | async-start | bytes 3538944 | tf_op jit(solution)/shard_map/reduce_scatter | solution.py:1179
  453.1 183.7 %reduce-scatter.14.cloned.1.call-start = ((), (), s32[]{:S(2)}) async-start(), calls=%async_computation.17 | async-start | bytes 3538944 | tf_op jit(solution)/shard_map/reduce_scatter | solution.py:1179
  597.7 80.3 %all-gather.21.cloned.1.call-start = ((), (), s32[]{:S(2)}) async-start(), calls=%async_computation.20 | async-start | bytes 3833856 | tf_op jit(solution)/shard_map/all_gather | solution.py:1208
  603.0 38.1 %collective-permute-start.6 = (bf16[288,1536]{1,0:T(8,128)(2,1)}, bf16[288,1536]{1,0:T(8,128)(2,1)}, u32[]{:S(2)}, u32[]{:S(2)}) collective-permute-start(bf16[288,1536]{1,0:T(8,128)(2,1)} %get-tuple-element.596), channel_id=1, source_target_pairs={{0,8},{8,0},{16,24},{24,16},{1,9},{9,1},{17,25},{25,17},{2,10},{10... | collective-permute-start | bytes 2654216 | tf_op jit(solution)/shard_map/ppermute | solution.py:992
  603.5 37.5 %collective-permute-start.7 = (bf16[288,1536]{1,0:T(8,128)(2,1)}, bf16[288,1536]{1,0:T(8,128)(2,1)}, u32[]{:S(2)}, u32[]{:S(2)}) collective-permute-start(bf16[288,1536]{1,0:T(8,128)(2,1)} %get-tuple-element.595), channel_id=1, source_target_pairs={{0,16},{8,24},{16,0},{24,8},{1,17},{9,25},{17,1},{25,9},{2,18},{10... | collective-permute-start | bytes 2654216 | tf_op jit(solution)/shard_map/ppermute | solution.py:992
  605.1 36.0 %collective-permute-start.8 = (bf16[288,1536]{1,0:T(8,128)(2,1)S(1)}, bf16[288,1536]{1,0:T(8,128)(2,1)}, u32[]{:S(2)}, u32[]{:S(2)}) collective-permute-start(bf16[288,1536]{1,0:T(8,128)(2,1)S(1)} %get-tuple-element.594), channel_id=1, source_target_pairs={{0,24},{8,16},{16,8},{24,0},{1,25},{9,17},{17,9},{25,1},{2,26},{10... | collective-permute-start | bytes 2654216 | tf_op jit(solution)/shard_map/ppermute | solution.py:992
  610.8 202.9 %reduce-scatter.18.cloned.1.call-start = ((), (), s32[]{:S(2)}) async-start(), calls=%async_computation.19 | async-start | bytes 3538944 | tf_op jit(solution)/shard_map/reduce_scatter | solution.py:1190
  652.8 162.9 %all-gather.23.cloned.1.call-start = ((), (), s32[]{:S(2)}) async-start(), calls=%async_computation.22 | async-start | bytes 3833856 | tf_op jit(solution)/shard_map/all_gather | solution.py:1208
  653.5 286.3 %reduce-scatter.22.cloned.1.call-start = ((), (), s32[]{:S(2)}) async-start(), calls=%async_computation.23 | async-start | bytes 3538944 | tf_op jit(solution)/shard_map/reduce_scatter | solution.py:1223
  727.7 253.7 %reduce-scatter.20.cloned.1.call-start = ((), (), s32[]{:S(2)}) async-start(), calls=%async_computation.21 | async-start | bytes 3538944 | tf_op jit(solution)/shard_map/reduce_scatter | solution.py:1190
  733.3 41.5 %collective-permute-start.10 = (bf16[288,1536]{1,0:T(8,128)(2,1)S(1)}, bf16[288,1536]{1,0:T(8,128)(2,1)S(1)}, u32[]{:S(2)}, u32[]{:S(2)}) collective-permute-start(bf16[288,1536]{1,0:T(8,128)(2,1)S(1)} %get-tuple-element.599), channel_id=1, source_target_pairs={{0,16},{8,24},{16,0},{24,8},{1,17},{9,25},{17,1},{25,9},{2,18},{10... | collective-permute-start | bytes 2654216 | tf_op jit(solution)/shard_map/ppermute | solution.py:992
  733.9 40.9 %collective-permute-start.11 = (bf16[288,1536]{1,0:T(8,128)(2,1)S(1)}, bf16[288,1536]{1,0:T(8,128)(2,1)S(1)}, u32[]{:S(2)}, u32[]{:S(2)}) collective-permute-start(bf16[288,1536]{1,0:T(8,128)(2,1)S(1)} %get-tuple-element.598), channel_id=1, source_target_pairs={{0,24},{8,16},{16,8},{24,0},{1,25},{9,17},{17,9},{25,1},{2,26},{10... | collective-permute-start | bytes 2654216 | tf_op jit(solution)/shard_map/ppermute | solution.py:992
  735.4 40.9 %collective-permute-start.9 = (bf16[288,1536]{1,0:T(8,128)(2,1)S(1)}, bf16[288,1536]{1,0:T(8,128)(2,1)S(1)}, u32[]{:S(2)}, u32[]{:S(2)}) collective-permute-start(bf16[288,1536]{1,0:T(8,128)(2,1)S(1)} %get-tuple-element.600), channel_id=1, source_target_pairs={{0,8},{8,0},{16,24},{24,16},{1,9},{9,1},{17,25},{25,17},{2,10},{10... | collective-permute-start | bytes 2654216 | tf_op jit(solution)/shard_map/ppermute | solution.py:992
  743.9 199.7 %collective-permute-start.12 = (bf16[2,384,512]{2,1,0:T(8,128)(2,1)}, bf16[2,384,512]{2,1,0:T(8,128)(2,1)}, u32[]{:S(2)}, u32[]{:S(2)}) collective-permute-start(bf16[2,384,512]{2,1,0:T(8,128)(2,1)} %get-tuple-element.604), channel_id=1, source_target_pairs={{0,8},{8,0},{16,24},{24,16},{1,9},{9,1},{17,25},{25,17},{2,10},{10... | collective-permute-start | bytes 2359304 | tf_op jit(solution)/shard_map/ppermute | solution.py:992
  744.5 199.2 %collective-permute-start.13 = (bf16[2,384,512]{2,1,0:T(8,128)(2,1)}, bf16[2,384,512]{2,1,0:T(8,128)(2,1)}, u32[]{:S(2)}, u32[]{:S(2)}) collective-permute-start(bf16[2,384,512]{2,1,0:T(8,128)(2,1)} %get-tuple-element.603), channel_id=1, source_target_pairs={{0,16},{8,24},{16,0},{24,8},{1,17},{9,25},{17,1},{25,9},{2,18},{10... | collective-permute-start | bytes 2359304 | tf_op jit(solution)/shard_map/ppermute | solution.py:992
  794.5 206.4 %reduce-scatter.26.cloned.1.call-start = ((), (), s32[]{:S(2)}) async-start(), calls=%async_computation.25 | async-start | bytes 884736 | tf_op jit(solution)/shard_map/reduce_scatter | solution.py:1361
  882.0 22.3 %collective-permute-start.18 = (f32[6674]{0:T(1024)}, f32[6674]{0:T(1024)}, u32[]{:S(2)}, u32[]{:S(2)}) collective-permute-start(f32[6674]{0:T(1024)} %concatenate.76), channel_id=1, source_target_pairs={{0,8},{8,0},{16,24},{24,16},{1,9},{9,1},{17,25},{25,17},{2,10},{10... | collective-permute-start | bytes 80096 | tf_op jit(solution)/shard_map/ppermute | solution.py:992
  883.2 23.4 %collective-permute-start.19 = (f32[6674]{0:T(1024)}, f32[6674]{0:T(1024)}, u32[]{:S(2)}, u32[]{:S(2)}) collective-permute-start(f32[6674]{0:T(1024)} %concatenate.76), channel_id=1, source_target_pairs={{0,16},{8,24},{16,0},{24,8},{1,17},{9,25},{17,1},{25,9},{2,18},{10... | collective-permute-start | bytes 80096 | tf_op jit(solution)/shard_map/ppermute | solution.py:992
  884.6 22.5 %collective-permute-start.20 = (f32[6674]{0:T(1024)}, f32[6674]{0:T(1024)}, u32[]{:S(2)}, u32[]{:S(2)}) collective-permute-start(f32[6674]{0:T(1024)} %concatenate.76), channel_id=1, source_target_pairs={{0,24},{8,16},{16,8},{24,0},{1,25},{9,17},{17,9},{25,1},{2,26},{10... | collective-permute-start | bytes 80096 | tf_op jit(solution)/shard_map/ppermute | solution.py:992
  889.4 122.1 %reduce-scatter.24.cloned.1.call-start = ((), (), s32[]{:S(2)}) async-start(), calls=%async_computation.24 | async-start | bytes 3538944 | tf_op jit(solution)/shard_map/reduce_scatter | solution.py:1223
  904.3 39.4 %collective-permute-start.14 = (bf16[2,384,512]{2,1,0:T(8,128)(2,1)}, bf16[2,384,512]{2,1,0:T(8,128)(2,1)}, u32[]{:S(2)}, u32[]{:S(2)}) collective-permute-start(bf16[2,384,512]{2,1,0:T(8,128)(2,1)} %get-tuple-element.602), channel_id=1, source_target_pairs={{0,24},{8,16},{16,8},{24,0},{1,25},{9,17},{17,9},{25,1},{2,26},{10... | collective-permute-start | bytes 2359304 | tf_op jit(solution)/shard_map/ppermute | solution.py:992
  906.5 79.4 %collective-permute-start.21 = (bf16[1168,384]{1,0:T(8,128)(2,1)}, bf16[1168,384]{1,0:T(8,128)(2,1)}, u32[]{:S(2)}, u32[]{:S(2)}) collective-permute-start(bf16[1168,384]{1,0:T(8,128)(2,1)} %get-tuple-element.575), channel_id=1, source_target_pairs={{0,8},{8,0},{16,24},{24,16},{1,9},{9,1},{17,25},{25,17},{2,10},{10... | collective-permute-start | bytes 2691080 | tf_op jit(solution)/shard_map/ppermute | solution.py:992
  907.1 78.9 %collective-permute-start.22 = (bf16[1168,384]{1,0:T(8,128)(2,1)}, bf16[1168,384]{1,0:T(8,128)(2,1)}, u32[]{:S(2)}, u32[]{:S(2)}) collective-permute-start(bf16[1168,384]{1,0:T(8,128)(2,1)} %get-tuple-element.577), channel_id=1, source_target_pairs={{0,16},{8,24},{16,0},{24,8},{1,17},{9,25},{17,1},{25,9},{2,18},{10... | collective-permute-start | bytes 2691080 | tf_op jit(solution)/shard_map/ppermute | solution.py:992
  957.6 21.5 %collective-permute-start.15 = (bf16[384,384]{1,0:T(8,128)(2,1)S(1)}, bf16[384,384]{1,0:T(8,128)(2,1)S(1)}, u32[]{:S(2)}, u32[]{:S(2)}) collective-permute-start(bf16[384,384]{1,0:T(8,128)(2,1)S(1)} %get-tuple-element.621), channel_id=1, source_target_pairs={{0,8},{8,0},{16,24},{24,16},{1,9},{9,1},{17,25},{25,17},{2,10},{10... | collective-permute-start | bytes 884744 | tf_op jit(solution)/shard_map/ppermute | solution.py:992
  959.0 22.3 %collective-permute-start.16 = (bf16[384,384]{1,0:T(8,128)(2,1)S(1)}, bf16[384,384]{1,0:T(8,128)(2,1)S(1)}, u32[]{:S(2)}, u32[]{:S(2)}) collective-permute-start(bf16[384,384]{1,0:T(8,128)(2,1)S(1)} %get-tuple-element.623), channel_id=1, source_target_pairs={{0,16},{8,24},{16,0},{24,8},{1,17},{9,25},{17,1},{25,9},{2,18},{10... | collective-permute-start | bytes 884744 | tf_op jit(solution)/shard_map/ppermute | solution.py:992
  960.4 20.9 %collective-permute-start.17 = (bf16[384,384]{1,0:T(8,128)(2,1)S(1)}, bf16[384,384]{1,0:T(8,128)(2,1)S(1)}, u32[]{:S(2)}, u32[]{:S(2)}) collective-permute-start(bf16[384,384]{1,0:T(8,128)(2,1)S(1)} %get-tuple-element.622), channel_id=1, source_target_pairs={{0,24},{8,16},{16,8},{24,0},{1,25},{9,17},{17,9},{25,1},{2,26},{10... | collective-permute-start | bytes 884744 | tf_op jit(solution)/shard_map/ppermute | solution.py:992
  979.1 18.1 %collective-permute-start.23 = (bf16[1168,384]{1,0:T(8,128)(2,1)S(1)}, bf16[1168,384]{1,0:T(8,128)(2,1)}, u32[]{:S(2)}, u32[]{:S(2)}) collective-permute-start(bf16[1168,384]{1,0:T(8,128)(2,1)S(1)} %copy-done.30), channel_id=1, source_target_pairs={{0,24},{8,16},{16,8},{24,0},{1,25},{9,17},{17,9},{25,1},{2,26},{10... | collective-permute-start | bytes 2691080 | tf_op jit(solution)/shard_map/ppermute | solution.py:992
  1001.6 8.5 collective-permute-start.24
  1003.0 7.1 collective-permute-start.25
  1004.4 5.7 collective-permute-start.26
  (109 other events, 1423.5 us)
Sparse Core Ops, SparseCore 0:
  11.2 40.9 all-gather.10
  54.4 37.1 all-gather.8
  93.3 37.1 all-gather.12
  161.6 38.6 reduce-scatter.9
  208.4 38.6 reduce-scatter.11
  249.2 37.3 all-gather.14
  303.3 35.1 all-gather.18
  340.7 37.1 all-gather.16
  453.2 37.7 reduce-scatter.15
  597.8 38.9 reduce-scatter.13
  638.5 39.4 all-gather.20
  680.7 39.1 reduce-scatter.17
  721.6 39.4 all-gather.22
  763.2 39.1 reduce-scatter.21
  804.6 39.4 reduce-scatter.19
  889.5 30.2 reduce-scatter.25
  922.1 38.8 reduce-scatter.23

commit v3 on v2

v3 whole, which is shorter than its diff:
```python
import functools

import jax
import jax.numpy as jnp
from jax import lax
from jax.experimental import pallas as pl
from jax.experimental.pallas import tpu as pltpu
from jax.sharding import PartitionSpec as P

NS = 128
BLOCK = 256
CAP = 144
EPS = 1e-05
HEAD_ROWS = 16
LANES = 128
F32 = jnp.float32
BF16 = jnp.bfloat16
VMEM = pl.BlockSpec(memory_space=pltpu.VMEM)
VMEM_LIMIT = 56 * 1024 * 1024
GROUP = 3
KERNEL_COST = pl.CostEstimate(flops=3 * 10**10, bytes_accessed=2**20, transcendentals=0)
ANY = pl.BlockSpec(memory_space=pl.ANY)
MESH = pl.DeviceIdType.MESH


def contract(left_op, right_op, left_dim, right_dim, precision=None):
    return lax.dot_general(
        left_op,
        right_op,
        (((left_dim,), (right_dim,)), ((), ())),
        preferred_element_type=F32,
        precision=precision,
    )


def dot_plain(left_op, right_op):
    return contract(left_op, right_op, 1, 0)


def dot_first(left_op, right_op):
    return contract(left_op, right_op, 0, 0)


def dot_last(left_op, right_op):
    return contract(left_op, right_op, 1, 1)


def silu_slope(values):
    logistic = jax.nn.sigmoid(values)
    return logistic * (1.0 + values * (1.0 - logistic))


def softplus(values):
    return jnp.maximum(values, 0.0) + jnp.log1p(jnp.exp(-jnp.abs(values)))


def shifts_back(current, before):
    joined = jnp.concatenate([before, current], axis=1)
    return [pltpu.roll(joined, step, 1)[:, LANES:] for step in (1, 2, 3)]


def load_block(ref, rows, block):
    cols = pl.ds(pl.multiple_of(block * BLOCK, BLOCK), BLOCK)
    current = ref[rows, cols]
    ahead = pl.multiple_of(jnp.maximum(block * BLOCK - LANES, 0), LANES)
    before = jnp.where(block > 0, ref[rows, pl.ds(ahead, LANES)], 0.0)
    return current, shifts_back(current, before)


def convolved(current, back, taps):
    return (
        taps[:, 4:5]
        + taps[:, 3:4] * current
        + taps[:, 2:3] * back[0]
        + taps[:, 1:2] * back[1]
        + taps[:, 0:1] * back[2]
    )


def conv_adjoint(adjoint, after, taps):
    joined = jnp.concatenate([adjoint, after], axis=1)
    width = joined.shape[1]
    total = taps[:, 3:4] * adjoint
    for step in (1, 2, 3):
        ahead = pltpu.roll(joined, width - step, 1)[:, :BLOCK]
        total = total + taps[:, 3 - step : 4 - step] * ahead
    return total


def lane_tile(columns):
    rows = columns[0].shape[0]
    lane = lax.broadcasted_iota(jnp.int32, (rows, LANES), 1)
    tile = jnp.zeros((rows, LANES), F32)
    for place, column in enumerate(columns):
        tile = jnp.where(lane == place, column, tile)
    return tile


def row_sum(values):
    return jnp.sum(values, axis=1, keepdims=True)


def decay_block(cum_row, cum_cols, head):
    lane = lax.broadcasted_iota(jnp.int32, cum_cols.shape, 1)
    cum_col = row_sum(jnp.where(lane == head, cum_cols, 0.0))
    place_j = lax.broadcasted_iota(jnp.int32, (BLOCK, BLOCK), 0)
    place_i = lax.broadcasted_iota(jnp.int32, (BLOCK, BLOCK), 1)
    return jnp.exp(jnp.where(place_j <= place_i, cum_row - cum_col, -1e30))


def step_rows(step_pre, head_params, step_s, cum_s, cum_t_s, blocks):
    step = softplus(step_pre + head_params[:, 0:1])
    step_s[...] = step
    log_decay = -(step * head_params[:, 1:2])
    place_j = lax.broadcasted_iota(jnp.int32, (BLOCK, BLOCK), 0)
    place_i = lax.broadcasted_iota(jnp.int32, (BLOCK, BLOCK), 1)
    upper = jnp.where(place_j <= place_i, 1.0, 0.0)
    for block in range(blocks):
        cols = slice(block * BLOCK, (block + 1) * BLOCK)
        cum = contract(log_decay[:, cols], upper, 1, 0, lax.Precision.HIGHEST)
        cum_s[:, cols] = cum
        cum_t_s[cols, :] = jnp.transpose(cum)


def score_blocks(io, scores_s, blocks):
    for block in range(blocks):
        cols = slice(block * BLOCK, (block + 1) * BLOCK)
        scores_s[block] = dot_first(io[:NS, cols], io[NS:, cols])


def block_cols(block):
    return pl.ds(pl.multiple_of(block * BLOCK, BLOCK), BLOCK)


def head_group(heads):
    return GROUP if heads % GROUP == 0 else 1


def greet(peers):
    barrier = pltpu.get_barrier_semaphore()
    for other in peers:
        pl.semaphore_signal(barrier, inc=1, device_id=other, device_id_type=MESH)
    pl.semaphore_wait(barrier, len(peers))


def row_partners(members):
    me = lax.axis_index("row")
    return [{"row": me ^ k} for k in range(1, members)]


def make_send(source, target, send_sem, recv_sem, other):
    return pltpu.make_async_remote_copy(
        src_ref=source,
        dst_ref=target,
        send_sem=send_sem,
        recv_sem=recv_sem,
        device_id=other,
        device_id_type=MESH,
    )


def send(*args):
    copy = make_send(*args)
    copy.start()
    return copy


def unit_of(member, per_device, split, part_width):
    if split == 1:
        return member * per_device, 0
    return (member * per_device) // split, pl.multiple_of((member % split) * part_width, LANES)


def unit_part(weight, member, per_device, split):
    part_width = weight.shape[2] // split
    first, hidden_at = unit_of(member, per_device, split, part_width)
    return weight.at[pl.ds(first, per_device), :, pl.ds(hidden_at, part_width)]


def send_stack(parts, stacked, sems):
    if not parts:
        return []
    me = lax.axis_index("row")
    copies = [pltpu.make_async_copy(parts[0], stacked.at[me], sems.at[0, 0])]
    copies[0].start()
    for k, other in enumerate(row_partners(len(parts)), 1):
        copies.append(send(parts[k], stacked.at[me], sems.at[0, k], sems.at[1, k], other))
    return copies


def mixer_forward_kernel(
    heads,
    cols_n,
    per_device,
    split,
    xn,
    wb,
    wc,
    wio,
    ws,
    wo,
    chan,
    io_taps,
    head_params,
    *refs,
):
    weight, *refs = refs
    count = len(refs) - 18
    y, squares, branch, conv, io_pre, io, step_pre, starts = refs[:8]
    received = refs[8 : 8 + count]
    step_s, cum_s, cum_t_s, scores_s, z_s, sems = refs[8 + count : 14 + count]
    squares_s, own_s, got_s, square_sems = refs[14 + count :]
    at = lax.axis_index("col")
    col_peers = [{"col": at ^ k} for k in range(1, cols_n)]
    row_peers = row_partners(count + 1)
    greet(row_peers + col_peers)
    copies = [
        send(
            unit_part(weight, lax.axis_index("row") ^ (k + 1), per_device, split),
            received[k],
            sems.at[0, k],
            sems.at[1, k],
            other,
        )
        for k, other in enumerate(row_peers)
    ]
    length = xn.shape[0]
    blocks = length // BLOCK
    size = wb.shape[0] // heads
    step_pre[...] = dot_last(ws[...], xn[...])
    step_rows(step_pre[...], head_params[...], step_s, cum_s, cum_t_s, blocks)

    def project(block, carry):
        cols = block_cols(block)
        rows = xn[cols, :]
        io_pre[:, cols] = dot_last(wio[...], rows)
        branch[:, cols] = dot_last(wb[...], rows)
        conv[:, cols] = dot_last(wc[...], rows)
        return carry

    lax.fori_loop(0, blocks, project, 0)

    def io_step(at, carry):
        rows = pl.ds(pl.multiple_of((at // blocks) * 64, 64), 64)
        block = at % blocks
        current, back = load_block(io_pre, rows, block)
        io[rows, block_cols(block)] = jax.nn.silu(
            convolved(current, back, io_taps[rows, :])
        ).astype(BF16)
        return carry

    lax.fori_loop(0, blocks * (2 * NS // 64), io_step, 0)
    score_blocks(io, scores_s, blocks)
    squares_s[...] = jnp.zeros_like(squares_s)

    group = head_group(heads)

    def head_step(first, carry):
        def block_steps(block, states):
            return tuple(
                block_step(first * group + at, block, state) for at, state in enumerate(states)
            )

        def block_step(head, block, state):
            rows = pl.ds(pl.multiple_of(head * size, size), size)
            params = chan[rows, :]
            cols = block_cols(block)
            current, back = load_block(conv, rows, block)
            x = jax.nn.silu(convolved(current, back, params))
            step_row = step_s[pl.ds(head, 1), cols]
            cum_row = cum_s[pl.ds(head, 1), cols]
            last = cum_row[:, BLOCK - 1 : BLOCK]
            mixing = (scores_s[block] * decay_block(cum_row, cum_t_s[cols, :], head)).astype(BF16)
            weighted = x * step_row
            starts[pl.ds(pl.multiple_of((head * blocks + block) * size, size), size), :] = state
            scanned = dot_plain(weighted.astype(BF16), mixing)
            scanned = scanned + dot_plain(state.astype(BF16), io[NS:, cols]) * jnp.exp(cum_row)
            scanned = scanned + params[:, 6:7] * x
            gated = scanned * jax.nn.silu(branch[rows, cols])
            squares_s[:, cols] += jnp.sum((gated * gated).reshape(size // 8, 8, BLOCK), axis=0)
            z_s[rows, cols] = (gated * params[:, 5:6]).astype(BF16)
            to_end = (weighted * jnp.exp(last - cum_row)).astype(BF16)
            return state * jnp.exp(last) + dot_last(to_end, io[:NS, cols])

        lax.fori_loop(0, blocks, block_steps, (jnp.zeros((size, NS), F32),) * group)
        return carry

    lax.fori_loop(0, heads // group, head_step, 0)
    own_s[...] = jnp.sum(squares_s[...], axis=0, keepdims=True)
    square_copies = [
        send(own_s, got_s.at[k], square_sems.at[0, k], square_sems.at[1, k], other)
        for k, other in enumerate(col_peers)
    ]

    def out_step(block, carry):
        cols = block_cols(block)
        y[cols, :] = dot_first(z_s[:, cols], wo[...]).astype(BF16)
        return carry

    lax.fori_loop(0, blocks, out_step, 0)
    for copy in square_copies:
        copy.wait()
    total = own_s[...]
    for k in range(cols_n - 1):
        total = total + got_s[k]
    squares[...] = total
    for copy in copies:
        copy.wait()


def mixer_forward(rows_n, cols_n, unit, weight, xn, wb, wc, wio, ws, wo, chan, io_taps, head_params, heads):
    length, width = xn.shape
    share = wb.shape[0]
    blocks = length // BLOCK
    size = share // heads
    shape = jax.ShapeDtypeStruct
    out = pl.pallas_call(
        functools.partial(mixer_forward_kernel, heads, cols_n, *unit),
        out_shape=(
            shape((length, width), BF16),
            shape((1, length), F32),
            shape((share, length), F32),
            shape((share, length), F32),
            shape((2 * NS, length), F32),
            shape((2 * NS, length), BF16),
            shape((HEAD_ROWS, length), F32),
            shape((heads * blocks * size, NS), F32),
        )
        + (shape((unit[0], weight.shape[1], weight.shape[2] // unit[1]), BF16),) * (rows_n - 1),
        in_specs=[VMEM] * 9 + [ANY],
        out_specs=(VMEM,) * 8 + (ANY,) * (rows_n - 1),
        scratch_shapes=[
            pltpu.VMEM((HEAD_ROWS, length), F32),
            pltpu.VMEM((HEAD_ROWS, length), F32),
            pltpu.VMEM((length, HEAD_ROWS), F32),
            pltpu.VMEM((blocks, BLOCK, BLOCK), F32),
            pltpu.VMEM((share, length), BF16),
            pltpu.SemaphoreType.DMA((2, rows_n - 1)),
            pltpu.VMEM((8, length), F32),
            pltpu.VMEM((1, length), F32),
            pltpu.VMEM((cols_n - 1, 1, length), F32),
            pltpu.SemaphoreType.DMA((2, cols_n - 1)),
        ],
        compiler_params=pltpu.CompilerParams(
            vmem_limit_bytes=VMEM_LIMIT, collective_id=2, has_side_effects=True
        ),
        cost_estimate=KERNEL_COST,
    )(xn, wb, wc, wio, ws, wo, chan, io_taps, head_params, weight)
    return out[:8], out[8:]


def mixer_backward_kernel(
    heads,
    members,
    moved_n,
    d_res,
    scale_rows,
    xn,
    wb,
    wc,
    wio,
    ws,
    wo,
    chan,
    io_taps,
    head_params,
    branch,
    conv,
    io_pre,
    io,
    step_pre,
    starts,
    *refs,
):
    refs = list(refs)
    parts, refs = refs[:members], refs[members:]
    moved, refs = refs[:moved_n], refs[moved_n:]
    first_part, gain_part, mixed, d_branch, d_conv, d_io, d_step = refs[:7]
    chan_grad_t, io_grad_t, head_grad = refs[7:10]
    stacked, arrived, refs = refs[10], refs[11 : 11 + moved_n], refs[11 + moved_n :]
    step_s, cum_s, cum_t_s, scores_s, d_scores_s, d_mixed_s, d_io_s = refs[:7]
    d_cum_s, d_size_s, adjoint_s, cube_s, sems, chan_grad, io_grad = refs[7:14]
    partners = row_partners(members)
    greet(partners)
    copies = [
        send(moved[k], arrived[k], refs[14].at[0, k], refs[14].at[1, k], partners[k])
        for k in range(moved_n)
    ]
    copies += send_stack(parts, stacked, sems)
    length, width = xn.shape
    blocks = length // BLOCK
    size = wb.shape[0] // heads
    step_rows(step_pre[...], head_params[...], step_s, cum_s, cum_t_s, blocks)
    score_blocks(io, scores_s, blocks)
    d_scores_s[...] = jnp.zeros_like(d_scores_s)
    d_io_s[...] = jnp.zeros_like(d_io_s)
    d_cum_s[...] = jnp.zeros_like(d_cum_s)
    d_size_s[...] = jnp.zeros_like(d_size_s)
    chan_grad[...] = jnp.zeros_like(chan_grad)
    io_grad[...] = jnp.zeros_like(io_grad)
    adjoint_s[:, :, length:] = jnp.zeros(adjoint_s.shape[:2] + (LANES,), F32)

    def project(block, carry):
        cols = block_cols(block)
        d_mixed_s[:, cols] = dot_last(wo[...], d_res[cols, :width])
        cross = jnp.transpose(d_res[cols, width:].astype(F32))
        cross = cross[0:1] + cross[1:2] + cross[2:3]
        rms = scale_rows[0:1, cols]
        cube_s[:, cols] = rms * rms * rms * cross * scale_rows[1:2, cols]
        return carry

    lax.fori_loop(0, blocks, project, 0)

    group = head_group(heads)

    def head_step(first, carry):
        def block_steps(reverse, d_states):
            return tuple(
                block_step(first * group + at, at, reverse, d_state)
                for at, d_state in enumerate(d_states)
            )

        def block_step(head, lane_set, reverse, d_state):
            rows = pl.ds(pl.multiple_of(head * size, size), size)
            params = chan[rows, :]
            block = blocks - 1 - reverse
            cols = block_cols(block)
            state = starts[pl.ds(pl.multiple_of((head * blocks + block) * size, size), size), :]
            state_low = state.astype(BF16)
            d_state_low = d_state.astype(BF16)
            write_rows = io[:NS, cols]
            read_rows = io[NS:, cols]
            step_row = step_s[pl.ds(head, 1), cols]
            cum_row = cum_s[pl.ds(head, 1), cols]
            last = cum_row[:, BLOCK - 1 : BLOCK]
            decays = decay_block(cum_row, cum_t_s[cols, :], head)
            mixing = (scores_s[block] * decays).astype(BF16)
            current, back = load_block(conv, rows, block)
            conv_act = convolved(current, back, params)
            logistic = jax.nn.sigmoid(conv_act)
            x = conv_act * logistic
            slope = logistic * (1.0 + conv_act * (1.0 - logistic))
            weighted = x * step_row
            weighted_low = weighted.astype(BF16)
            grown = jnp.exp(cum_row)
            within = dot_plain(weighted_low, mixing)
            carried = dot_plain(state_low, read_rows) * grown
            scanned = within + carried + params[:, 6:7] * x

            inverse_rms = scale_rows[0:1, cols]
            gate_in = branch[rows, cols]
            gate_logistic = jax.nn.sigmoid(gate_in)
            gate_out = gate_in * gate_logistic
            gated = scanned * gate_out
            d_mixed = d_mixed_s[rows, cols]
            gain = params[:, 5:6]
            mixed[rows, cols] = (gated * inverse_rms * gain).astype(BF16)
            d_gated = inverse_rms * (d_mixed * gain) - gated * cube_s[:, cols]
            d_gain = row_sum(d_mixed * gated * inverse_rms)
            d_scanned = d_gated * gate_out
            d_branch[rows, cols] = (
                d_gated * scanned * (gate_logistic * (1.0 + gate_in * (1.0 - gate_logistic)))
            ).astype(BF16)
            d_low = d_scanned.astype(BF16)
            d_skip = row_sum(d_scanned * x)

            d_within = dot_last(d_low, mixing)
            shrunk = jnp.exp(last - cum_row)
            d_fed = dot_plain(d_state_low, write_rows) * shrunk
            d_weighted = d_within + d_fed
            d_scores_s[block] += dot_first(weighted_low, d_low) * decays
            d_grown = (d_scanned * grown).astype(BF16)
            fed = (weighted * shrunk).astype(BF16)
            d_io_s[NS:, cols] += dot_first(state_low, d_grown)
            d_io_s[:NS, cols] += dot_first(d_state_low, fed)
            d_before = d_state * jnp.exp(last) + dot_last(d_grown, read_rows)

            fed_terms = weighted * d_fed
            d_cum = jnp.sum(
                d_low.astype(F32) * within
                - weighted_low.astype(F32) * d_within
                + d_scanned * carried
                - fed_terms,
                axis=0,
                keepdims=True,
            )
            at_end = jnp.sum(row_sum(fed_terms), axis=0, keepdims=True) + jnp.exp(last) * jnp.sum(
                row_sum(d_state * state), axis=0, keepdims=True
            )
            lane = lax.broadcasted_iota(jnp.int32, (1, BLOCK), 1)
            d_cum_s[pl.ds(head, 1), cols] = d_cum + jnp.where(lane == BLOCK - 1, at_end, 0.0)
            d_size_s[pl.ds(head, 1), cols] = jnp.sum(d_weighted * x, axis=0, keepdims=True)

            d_act = (d_weighted * step_row + params[:, 6:7] * d_scanned) * slope
            adjoint_s[lane_set, :, cols] = d_act
            after = adjoint_s[lane_set, :, pl.ds(pl.multiple_of((block + 1) * BLOCK, BLOCK), LANES)]
            d_conv[rows, cols] = conv_adjoint(d_act, after, params).astype(BF16)
            chan_grad[rows, :] += lane_tile(
                [
                    row_sum(d_act * back[2]),
                    row_sum(d_act * back[1]),
                    row_sum(d_act * back[0]),
                    row_sum(d_act * current),
                    row_sum(d_act),
                    d_gain,
                    d_skip,
                ]
            )
            return d_before

        lax.fori_loop(0, blocks, block_steps, (jnp.zeros((size, NS), F32),) * group)
        return carry

    lax.fori_loop(0, heads // group, head_step, 0)

    def scores_step(block, carry):
        cols = block_cols(block)
        d_scores = d_scores_s[block].astype(BF16)
        d_io_s[NS:, cols] += dot_plain(io[:NS, cols], d_scores)
        d_io_s[:NS, cols] += dot_last(io[NS:, cols], d_scores)
        return carry

    lax.fori_loop(0, blocks, scores_step, 0)

    def io_step(at, carry):
        rows = pl.ds(pl.multiple_of((at // blocks) * 64, 64), 64)
        block = blocks - 1 - at % blocks
        cols = block_cols(block)
        taps = io_taps[rows, :]
        current, back = load_block(io_pre, rows, block)
        d_act = d_io_s[rows, cols] * silu_slope(convolved(current, back, taps))
        adjoint_s[0, :64, cols] = d_act
        after = adjoint_s[0, :64, pl.ds(pl.multiple_of((block + 1) * BLOCK, BLOCK), LANES)]
        d_io[rows, cols] = conv_adjoint(d_act, after, taps).astype(BF16)
        io_grad[rows, :] += lane_tile(
            [
                row_sum(d_act * back[2]),
                row_sum(d_act * back[1]),
                row_sum(d_act * back[0]),
                row_sum(d_act * current),
                row_sum(d_act),
            ]
        )
        return carry

    lax.fori_loop(0, blocks * (2 * NS // 64), io_step, 0)

    place_j = lax.broadcasted_iota(jnp.int32, (BLOCK, BLOCK), 0)
    place_i = lax.broadcasted_iota(jnp.int32, (BLOCK, BLOCK), 1)
    lower = jnp.where(place_j >= place_i, 1.0, 0.0)
    rate = head_params[:, 1:2]
    decay_grad = jnp.zeros((HEAD_ROWS, 1), F32)
    offset_grad = jnp.zeros((HEAD_ROWS, 1), F32)
    for block in range(blocks):
        cols = slice(block * BLOCK, (block + 1) * BLOCK)
        d_log = contract(d_cum_s[:, cols], lower, 1, 0, lax.Precision.HIGHEST)
        decay_grad = decay_grad - row_sum(step_s[:, cols] * rate * d_log)
        d_size = d_size_s[:, cols] - rate * d_log
        d_pre = d_size * jax.nn.sigmoid(step_pre[:, cols] + head_params[:, 0:1])
        offset_grad = offset_grad + row_sum(d_pre)
        d_step[:, cols] = d_pre.astype(BF16)
    skip = jnp.sum(chan_grad[:, 6:7].reshape(heads, size, 1), axis=1)
    skip = jnp.concatenate([skip, jnp.zeros((HEAD_ROWS - heads, 1), F32)], axis=0)
    head_grad[...] = lane_tile([decay_grad, offset_grad, skip])
    gain_part[...] = jnp.zeros_like(gain_part)

    def first_step(block, carry):
        cols = block_cols(block)
        part = (
            dot_first(d_branch[:, cols], wb[...])
            + dot_first(d_conv[:, cols], wc[...])
            + dot_first(d_io[:, cols], wio[...])
            + dot_first(d_step[:, cols], ws[...])
        )
        first_part[cols, :] = part.astype(BF16)
        product = part * xn[cols, :].astype(F32)
        gain_part[...] += jnp.sum(product.reshape(BLOCK // 8, 8, -1), axis=0)
        return carry

    lax.fori_loop(0, blocks, first_step, 0)
    chan_grad_t[...] = jnp.transpose(chan_grad[...])[:8]
    io_grad_t[...] = jnp.transpose(io_grad[...])[:8]
    for copy in copies:
        copy.wait()


def mixer_backward(parts, moved, d_res, scale_rows, xn, weights, saved, heads):
    length, width = xn.shape
    share = weights[0].shape[0]
    blocks = length // BLOCK
    size = share // heads
    shape = jax.ShapeDtypeStruct
    out = pl.pallas_call(
        functools.partial(mixer_backward_kernel, heads, len(parts), len(moved)),
        out_shape=(
            shape((length, width), BF16),
            shape((8, width), F32),
            shape((share, length), BF16),
            shape((share, length), BF16),
            shape((share, length), BF16),
            shape((2 * NS, length), BF16),
            shape((HEAD_ROWS, length), BF16),
            shape((8, share), F32),
            shape((8, 2 * NS), F32),
            shape((HEAD_ROWS, LANES), F32),
        )
        + (shape((len(parts),) + parts[0].shape, BF16),)
        + tuple(shape(rows.shape, BF16) for rows in moved),
        in_specs=[VMEM] * 17 + [ANY] * (len(parts) + len(moved)),
        out_specs=(VMEM,) * 10 + (ANY,) * (1 + len(moved)),
        scratch_shapes=[
            pltpu.VMEM((HEAD_ROWS, length), F32),
            pltpu.VMEM((HEAD_ROWS, length), F32),
            pltpu.VMEM((length, HEAD_ROWS), F32),
            pltpu.VMEM((blocks, BLOCK, BLOCK), F32),
            pltpu.VMEM((blocks, BLOCK, BLOCK), F32),
            pltpu.VMEM((share, length), F32),
            pltpu.VMEM((2 * NS, length), F32),
            pltpu.VMEM((HEAD_ROWS, length), F32),
            pltpu.VMEM((HEAD_ROWS, length), F32),
            pltpu.VMEM((head_group(heads), size, length + LANES), F32),
            pltpu.VMEM((1, length), F32),
            pltpu.SemaphoreType.DMA((2, len(parts))),
            pltpu.VMEM((share, LANES), F32),
            pltpu.VMEM((2 * NS, LANES), F32),
        ]
        + [pltpu.SemaphoreType.DMA((2, len(moved)))] * bool(moved),
        compiler_params=pltpu.CompilerParams(
            vmem_limit_bytes=VMEM_LIMIT,
            collective_id=3 if moved else 8,
            has_side_effects=True,
        ),
        cost_estimate=KERNEL_COST,
    )(d_res, scale_rows, xn, *weights, *saved, *parts, *moved)
    return out[:10], out[10], out[11:]


def place_rows(slot_t, gates_t, placed):
    length, units = slot_t.shape

    def choose(block, carry):
        at = block_cols(block)
        slots = slot_t[at, :]
        for tile in range(units * CAP // LANES):
            low, high = tile * LANES // CAP, (tile * LANES + LANES - 1) // CAP
            lane = lax.broadcasted_iota(jnp.int32, (BLOCK, LANES), 1) + tile * LANES
            total = jnp.zeros((BLOCK, LANES), F32)
            for unit in range(low, high + 1):
                value = 1.0 if gates_t is None else gates_t[at, unit : unit + 1]
                total = jnp.where(lane == slots[:, unit : unit + 1] + unit * CAP, value, total)
            placed[at, tile * LANES : (tile + 1) * LANES] = total.astype(BF16)
        return carry

    lax.fori_loop(0, length // BLOCK, choose, 0)


def combine_kernel(members, with_parts, slot_t, gates_t, extra_left, extra_right, *refs):
    refs = list(refs)
    rows, refs = refs[:members], refs[members:]
    if with_parts:
        parts, out, stacked, chosen_s, rows_s, sems, part_sems = refs[:members], *refs[members:]
        greet(row_partners(members))
        copies = send_stack(parts, stacked, part_sems)
    else:
        out, chosen_s, rows_s, sems = refs
        copies = []
    part = rows_s.shape[0] // members
    loads = []
    for member in range(members):
        loads.append(
            pltpu.make_async_copy(
                rows[member], rows_s.at[pl.ds(member * part, part)], sems.at[member]
            )
        )
        loads[-1].start()
    place_rows(slot_t, gates_t, chosen_s)
    for copy in loads:
        copy.wait()

    def columns(at, carry):
        cols = block_cols(at)
        total = dot_plain(chosen_s[...], rows_s[:, cols])
        total = total + dot_plain(extra_left[...], extra_right[:, cols])
        out[:, cols] = total.astype(BF16)
        return carry

    lax.fori_loop(0, out.shape[1] // BLOCK, columns, 0)
    for copy in copies:
        copy.wait()


def combine_rows(slot_t, gates_t, rows, extra_left, extra_right, parts):
    length, units = slot_t.shape
    members = len(rows)
    width = rows[0].shape[1]
    shape = jax.ShapeDtypeStruct
    out = [shape((length, width), BF16)]
    scratch = [
        pltpu.VMEM((length, units * CAP), BF16),
        pltpu.VMEM((units * CAP, width), BF16),
        pltpu.SemaphoreType.DMA((members,)),
    ]
    params = {}
    if parts:
        out.append(shape((members,) + parts[0].shape, BF16))
        scratch.append(pltpu.SemaphoreType.DMA((2, members)))
        params = {"collective_id": 9, "has_side_effects": True}
    return pl.pallas_call(
        functools.partial(combine_kernel, members, bool(parts)),
        out_shape=tuple(out),
        in_specs=[VMEM] * 4 + [ANY] * (members + len(parts)),
        out_specs=(VMEM,) + (ANY,) * (len(out) - 1),
        scratch_shapes=scratch,
        compiler_params=pltpu.CompilerParams(vmem_limit_bytes=VMEM_LIMIT, **params),
        cost_estimate=KERNEL_COST,
    )(slot_t, gates_t, extra_left, extra_right, *rows, *parts)


def spread_start(
    members, weighted, slot, gates, source, received, outgoing, chosen_s, gate_s, row_sems, own_sems
):
    units, length = slot.shape
    width = source.shape[1]
    experts = units // members
    rows = experts * CAP
    partners = row_partners(members)

    def choose(unit, carry):
        at = pl.ds(pl.multiple_of(unit * CAP, CAP), CAP)
        place = lax.broadcasted_iota(jnp.int32, (CAP, length), 0)
        hit = place == slot[pl.ds(unit, 1), :]
        chosen_s[at, :] = jnp.where(hit, 1.0, 0.0).astype(BF16)
        if weighted:
            gate_s[at, :] = row_sum(jnp.where(hit, gates[pl.ds(unit, 1), :], 0.0))
        return carry

    lax.fori_loop(0, units, choose, 0)

    def pairs(part):
        out = []
        for expert in range(experts):
            for k, other in enumerate(partners):
                out.append(
                    make_send(
                        outgoing.at[pl.ds((k + 1) * rows + expert * CAP, CAP), part],
                        received.at[expert, pl.ds((k + 1) * CAP, CAP), part],
                        row_sems.at[0, k, expert],
                        row_sems.at[1, k, expert],
                        other,
                    )
                )
            out.append(
                pltpu.make_async_copy(
                    outgoing.at[pl.ds(expert * CAP, CAP), part],
                    received.at[expert, pl.ds(0, CAP), part],
                    own_sems.at[expert],
                )
            )
        return out

    def columns(at, carry):
        cols = block_cols(at)
        picked = dot_plain(chosen_s[...], source[:, cols])
        if weighted:
            picked = picked * gate_s[...]
        outgoing[:, cols] = picked.astype(BF16)
        for copy in pairs(cols):
            copy.start()
        return carry

    lax.fori_loop(0, width // BLOCK, columns, 0)
    return pairs(pl.ds(0, width))


def spread_kernel(members, weighted, before_n, slot, gates, source, *refs):
    if weighted:
        received, refs = refs[0], refs[1:]
    else:
        cot, gate_sh, up_sh, down_sh = refs[:4]
        before, refs = refs[4 : 4 + before_n], refs[4 + before_n :]
        received, hidden_sh, d_gate_sh, d_up_sh = refs[:4]
        grads, refs = refs[4:7], refs[7:]
    outgoing, chosen_s, gate_s, row_sems, own_sems = refs
    length, width = source.shape
    partners = row_partners(members)
    greet(partners)
    copies = spread_start(
        members, weighted, slot, gates, source, received, outgoing, chosen_s, gate_s, row_sems, own_sems
    )

    if not weighted:

        def shared_step(at, carry):
            at = block_cols(at)
            gate_pre = dot_last(source[at, :], gate_sh[...])
            up_pre = dot_last(source[at, :], up_sh[...])
            d_hidden = dot_last(cot[at, :], down_sh[...])
            logistic = jax.nn.sigmoid(gate_pre)
            active = gate_pre * logistic
            hidden_sh[at, :] = (active * up_pre).astype(BF16)
            slope = logistic * (1.0 + gate_pre * (1.0 - logistic))
            d_gate_sh[at, :] = (d_hidden * up_pre * slope).astype(BF16)
            d_up_sh[at, :] = (d_hidden * active).astype(BF16)
            return carry

        lax.fori_loop(0, length // BLOCK, shared_step, 0)

        def grad_step(at, carry):
            cols = block_cols(at)
            for at, (rows, right) in enumerate(
                ((source, d_gate_sh), (source, d_up_sh), (cot, hidden_sh))
            ):
                value = dot_first(rows[:, cols], right[...])
                if before:
                    value = value + before[at][cols, :]
                grads[at][cols, :] = value.astype(grads[at].dtype)
            return carry

        lax.fori_loop(0, width // BLOCK, grad_step, 0)
    for copy in copies:
        copy.wait()


def spread_scratch(members, units, length, width):
    experts = units // members
    return [
        pltpu.VMEM((units * CAP, width), BF16),
        pltpu.VMEM((units * CAP, length), BF16),
        pltpu.VMEM((units * CAP, 1), F32),
        pltpu.SemaphoreType.DMA((2, members - 1, experts)),
        pltpu.SemaphoreType.DMA((experts,)),
    ]


def spread_rows(members, slot, gates, source, cot=None, shared_w=(), before=(), grad_type=F32):
    units, length = slot.shape
    width = source.shape[1]
    experts = units // members
    weighted = cot is None
    shape = jax.ShapeDtypeStruct
    out = [shape((experts, members * CAP, width), BF16)]
    out += [shape((length, weight.shape[0]), BF16) for weight in shared_w]
    out += [shape(weight.shape[::-1], grad_type) for weight in shared_w]
    extra = () if weighted else (cot, *shared_w, *before)
    return pl.pallas_call(
        functools.partial(spread_kernel, members, weighted, len(before)),
        out_shape=tuple(out),
        in_specs=[VMEM] * (3 + len(extra)),
        out_specs=(ANY,) + (VMEM,) * (2 * len(shared_w)),
        scratch_shapes=spread_scratch(members, units, length, width),
        compiler_params=pltpu.CompilerParams(
            vmem_limit_bytes=VMEM_LIMIT,
            collective_id=4 if weighted else 11 if before else 5,
            has_side_effects=True,
        ),
        cost_estimate=KERNEL_COST,
    )(slot, gates, source, *extra)


def expert_kernel(
    members, split, following, slot_t, token_s, cot_s, d_gate_sh, d_up_sh, gate_sh, up_sh, *refs
):
    refs = list(refs)
    if following:
        slot, gates, source = refs[:3]
        received, picked_s, chosen_s, gate_s, spread_sems, own_sems = refs[-6:]
        refs = refs[3:-6]
    else:
        grads, grad_outs, grad_got, grad_sems = refs[:3], refs[-7:-4], refs[-4:-1], refs[-1]
        refs = refs[3:-7]
    shards = [refs[at * members : (at + 1) * members] for at in range(3)]
    part, out_rows, hidden_s, d_pre_s, outgoing, back_s, weights, places_s, row_sems, weight_sems = (
        refs[3 * members :]
    )
    experts, _, width = token_s.shape
    rows = experts * CAP
    hidden_width = weights.shape[3]
    depth = width // members
    chunk = min(BLOCK, hidden_width)
    me = lax.axis_index("row")
    partners = row_partners(members)
    weight_copies = []
    for which in range(3):
        for member in range(members):
            place = pl.ds(pl.multiple_of((me ^ member) * depth, depth), depth)
            shard = shards[which][member]
            if member == 0 and which < 2:
                shard = unit_part(shard, me, experts, split)
            weight_copies.append(
                pltpu.make_async_copy(
                    shard,
                    weights.at[which, :, place],
                    weight_sems.at[which, member],
                )
            )
            weight_copies[-1].start()
    greet(partners)
    spread = []
    if following:
        spread = spread_start(
            members,
            True,
            slot,
            gates,
            source,
            received,
            picked_s,
            chosen_s,
            gate_s,
            spread_sems,
            own_sems,
        )
    grad_copies = []
    if not following:
        for which in range(3):
            for k, other in enumerate(partners):
                place = pl.ds(pl.multiple_of((me ^ (k + 1)) * depth, depth), depth)
                grad_copies.append(
                    send(
                        grads[which].at[place],
                        grad_got[which].at[k],
                        grad_sems.at[0, which, k],
                        grad_sems.at[1, which, k],
                        other,
                    )
                )
    for copy in weight_copies:
        copy.wait()
    copies = []
    for expert in range(experts):

        def hidden_step(at, carry):
            cols = pl.ds(pl.multiple_of(at * chunk, chunk), chunk)
            up_cols = pl.ds(pl.multiple_of(hidden_width + at * chunk, chunk), chunk)
            gate_pre = dot_plain(token_s[expert], weights[0, expert, :, cols])
            up_pre = dot_plain(token_s[expert], weights[1, expert, :, cols])
            d_hidden = dot_plain(cot_s[expert], weights[2, expert, :, cols])
            logistic = jax.nn.sigmoid(gate_pre)
            active = gate_pre * logistic
            hidden_s[expert, :, cols] = (active * up_pre).astype(BF16)
            slope = logistic * (1.0 + gate_pre * (1.0 - logistic))
            d_pre_s[expert, :, cols] = (d_hidden * up_pre * slope).astype(BF16)
            d_pre_s[expert, :, up_cols] = (d_hidden * active).astype(BF16)
            return carry

        lax.fori_loop(0, hidden_width // chunk, hidden_step, 0)

        def back_step(at, carry):
            cols = block_cols(at)
            back = dot_last(d_pre_s[expert, :, :hidden_width], weights[0, expert, cols, :])
            back = back + dot_last(d_pre_s[expert, :, hidden_width:], weights[1, expert, cols, :])
            back = back.astype(BF16)
            back_s[expert * CAP : (expert + 1) * CAP, cols] = back[:CAP]
            for k in range(members - 1):
                outgoing[k * rows + expert * CAP : k * rows + (expert + 1) * CAP, cols] = back[
                    (k + 1) * CAP : (k + 2) * CAP
                ]
            for copy in returns(cols):
                copy.start()
            return carry

        def returns(cols, expert=expert):
            return [
                make_send(
                    outgoing.at[pl.ds(k * rows + expert * CAP, CAP), cols],
                    back_s.at[pl.ds((k + 1) * rows + expert * CAP, CAP), cols],
                    row_sems.at[0, k, expert],
                    row_sems.at[1, k, expert],
                    other,
                )
                for k, other in enumerate(partners)
            ]

        lax.fori_loop(0, width // BLOCK, back_step, 0)
        copies += returns(pl.ds(0, width))

    for expert in range(experts):

        def ahead_step(at, carry):
            cols = block_cols(at)
            ahead = dot_last(hidden_s[expert], weights[2, expert, cols, :]).astype(BF16)
            for member in range(members):
                out_rows[member][expert * CAP : (expert + 1) * CAP, cols] = ahead[
                    member * CAP : (member + 1) * CAP
                ]
            return carry

        lax.fori_loop(0, width // BLOCK, ahead_step, 0)

    place_rows(slot_t, None, places_s)
    for copy in copies:
        copy.wait()

    def columns(at, carry):
        cols = block_cols(at)
        total = dot_plain(places_s[...], back_s[:, cols])
        total = total + dot_plain(d_gate_sh[...], gate_sh[:, cols])
        total = total + dot_plain(d_up_sh[...], up_sh[:, cols])
        part[:, cols] = total.astype(BF16)
        return carry

    lax.fori_loop(0, width // BLOCK, columns, 0)
    for copy in spread + grad_copies:
        copy.wait()
    if not following:
        own = pl.ds(pl.multiple_of(me * depth, depth), depth)
        for which in range(3):
            value = grads[which][own, :].astype(F32)
            for k in range(members - 1):
                value = value + grad_got[which][k].astype(F32)
            grad_outs[which][...] = value


def expert_rows(
    following, grads, slot_t, tokens, cots, d_gate_sh, d_up_sh, shared_w, gate_parts, up_parts, down_parts
):
    members = len(gate_parts)
    length, units = slot_t.shape
    experts, stacked, width = tokens.shape
    rows = experts * CAP
    hidden_width = gate_parts[1].shape[2]
    split = gate_parts[0].shape[2] // hidden_width
    shape = jax.ShapeDtypeStruct
    extra = 3
    firsts = 7 + extra + 3 * members
    outs_n = 3 + members + (1 if following else 3)
    depth = width // members

    def kernel(*refs):
        ins, outs, scratch = refs[:firsts], refs[firsts : firsts + outs_n], refs[firsts + outs_n :]
        more = outs[3 + members :]
        outs, tail, scratch = outs[: 3 + members], (*more, *scratch[6:]), scratch[:6]
        expert_kernel(
            members, split, bool(following), *ins, outs[0], outs[1 : 1 + members], *outs[1 + members :],
            *scratch, *tail,
        )

    out_shape = [shape((length, width), BF16)] + [shape((rows, width), BF16)] * members
    out_shape += [
        shape((experts, stacked, hidden_width), BF16),
        shape((experts, stacked, 2 * hidden_width), BF16),
    ]
    out_specs = [VMEM] * (3 + members)
    scratch = [
        pltpu.VMEM(((members - 1) * rows, width), BF16),
        pltpu.VMEM((members * rows, width), BF16),
        pltpu.VMEM((3, experts, width, hidden_width), BF16),
        pltpu.VMEM((length, units * CAP), BF16),
        pltpu.SemaphoreType.DMA((2, members - 1, experts)),
        pltpu.SemaphoreType.DMA((3, members)),
    ]
    if following:
        out_shape.append(shape((experts, stacked, width), BF16))
        out_specs.append(ANY)
        scratch += spread_scratch(members, units, length, width)
    else:
        for grad in grads:
            out_shape.append(shape((depth, grad.shape[1]), F32))
            out_specs.append(VMEM)
            scratch.append(pltpu.VMEM((members - 1, depth, grad.shape[1]), BF16))
        scratch.append(pltpu.SemaphoreType.DMA((2, 3, members - 1)))
    out = pl.pallas_call(
        kernel,
        out_shape=tuple(out_shape),
        in_specs=[VMEM] * (7 + extra) + [ANY] * (3 * members),
        out_specs=tuple(out_specs),
        scratch_shapes=scratch,
        compiler_params=pltpu.CompilerParams(
            vmem_limit_bytes=VMEM_LIMIT,
            collective_id=6 if following else 10,
            has_side_effects=True,
        ),
        cost_estimate=KERNEL_COST,
    )(
        slot_t,
        tokens,
        cots,
        d_gate_sh,
        d_up_sh,
        *shared_w[:2],
        *(following or grads),
        *gate_parts,
        *up_parts,
        *down_parts,
    )
    return out[0], out[1 : 1 + members], out[1 + members : 3 + members], out[3 + members :]


def tail_kernel(rows_n, cols_n, micro_n, first_gain, *refs):
    refs = list(refs)
    sets = [refs[at * 12 : (at + 1) * 12] for at in range(micro_n)]
    refs = refs[micro_n * 12 :]
    outs, small_outs, refs = refs[:5], refs[5:9], refs[9:]
    totals, got, refs = refs[:4], refs[4:9], refs[9:]
    io_s, io_got, io_t_s, small_s, small_got, few_got, row_sems, col_sems = (
        refs[0], refs[1], refs[2], refs[3:7], refs[7:11], refs[11:13], refs[13], refs[14]
    )
    me, at = lax.axis_index("row"), lax.axis_index("col")
    width = sets[0][0].shape[1]
    depth = width // rows_n
    io_rows = io_got.shape[1]
    row_peers = row_partners(rows_n)
    col_peers = [{"col": at ^ k} for k in range(1, cols_n)]
    greet(row_peers + col_peers)
    row_copies, small_copies = [], []

    def to_row(which, k, source, target, other):
        return send(source, target, row_sems.at[0, which, k], row_sems.at[1, which, k], other)

    def to_col(which, k, source, target, other):
        return send(source, target, col_sems.at[0, which, k], col_sems.at[1, which, k], other)

    def total_of(place):
        return functools.reduce(jnp.add, [one[place][...] for one in sets])

    gain = jnp.sum(total_of(7), axis=0, keepdims=True) / first_gain[...]
    small_s[0][...] = jnp.concatenate([gain, total_of(8)], axis=0)
    for which, place in ((1, 10), (2, 9), (3, 11)):
        small_s[which][...] = total_of(place)
    for which in range(4):
        for k, other in enumerate(row_peers):
            small_copies.append(
                to_row(which, k, small_s[which], small_got[which].at[k], other)
            )

    def io_step(block, carry):
        cols = block_cols(block)
        io_s[:, cols] = functools.reduce(
            jnp.add, [dot_plain(one[6][...], one[0][:, cols]) for one in sets]
        ).astype(BF16)
        return carry

    lax.fori_loop(0, width // BLOCK, io_step, 0)
    io_copies = []
    for k, other in enumerate(col_peers):
        place = pl.ds(pl.multiple_of((at ^ (k + 1)) * io_rows, io_rows), io_rows)
        io_copies.append(to_col(0, k, io_s.at[place], io_got.at[k], other))
    def grads_at(cols):
        rows_t = [jnp.transpose(one[0][:, cols]) for one in sets]
        d_res_t = [jnp.transpose(one[1][:, cols]) for one in sets]
        for which, left in enumerate((2, 3, 4, 5)):
            right_t = d_res_t if left == 4 else rows_t
            totals[which][cols, :] = functools.reduce(
                jnp.add, [dot_last(right, one[left][...]) for right, one in zip(right_t, sets)]
            ).astype(BF16)

    def send_grads(k):
        place = pl.ds(pl.multiple_of((me ^ k) * depth, depth), depth)
        for which in range(4):
            row_copies.append(
                to_row(
                    4 + which, k - 1, totals[which].at[place], got[which].at[k - 1], row_peers[k - 1]
                )
            )

    if depth % LANES == 0:
        for k in [*range(1, rows_n), 0]:
            grads_at(pl.ds(pl.multiple_of((me ^ k) * depth, depth), depth))
            if k:
                send_grads(k)
    else:

        def grad_step(block, carry):
            grads_at(block_cols(block))
            return carry

        lax.fori_loop(0, width // BLOCK, grad_step, 0)
        for k in range(1, rows_n):
            send_grads(k)
    for copy in small_copies:
        copy.wait()
    for which in range(4):
        value = small_s[which][...]
        for k in range(rows_n - 1):
            value = value + small_got[which][k]
        small_s[which][...] = value
    few_copies = [
        to_col(1 + which, k, small_s[which], few_got[which].at[k], other)
        for which in range(2)
        for k, other in enumerate(col_peers)
    ]
    for copy in io_copies:
        copy.wait()
    io_total = io_s[pl.ds(pl.multiple_of(at * io_rows, io_rows), io_rows), :].astype(F32)
    for k in range(cols_n - 1):
        io_total = io_total + io_got[k].astype(F32)
    io_t_s[...] = jnp.transpose(io_total).astype(BF16)
    for k, other in enumerate(row_peers):
        place = pl.ds(pl.multiple_of((me ^ (k + 1)) * depth, depth), depth)
        row_copies.append(to_row(8, k, io_t_s.at[place], got[4].at[k], other))
    for copy in few_copies:
        copy.wait()
    for which in range(4):
        value = small_s[which][...]
        if which < 2:
            for k in range(cols_n - 1):
                value = value + few_got[which][k]
        small_outs[which][...] = value
    own = pl.ds(pl.multiple_of(me * depth, depth), depth)
    for copy in row_copies:
        copy.wait()
    for which, total in enumerate([*totals, io_t_s]):
        value = total[own, :].astype(F32)
        for k in range(rows_n - 1):
            value = value + got[which][k].astype(F32)
        outs[which][...] = value


def tail_sums(rows_n, cols_n, first_gain, sets):
    width = sets[0][0].shape[1]
    depth = width // rows_n
    io_full = sets[0][6].shape[0]
    io_rows = io_full // cols_n
    shares = [left.shape[0] for left in sets[0][2:6]]
    shape = jax.ShapeDtypeStruct
    vmem = lambda *dims: pltpu.VMEM(dims, BF16)
    small = [(2, width), sets[0][10].shape, sets[0][9].shape, sets[0][11].shape]
    small_f32 = lambda lead, dims: pltpu.VMEM(lead + dims, F32)
    return pl.pallas_call(
        functools.partial(tail_kernel, rows_n, cols_n, len(sets)),
        out_shape=tuple(shape((depth, share), F32) for share in shares + [io_rows])
        + tuple(shape(dims, F32) for dims in small),
        in_specs=[VMEM] * (1 + 12 * len(sets)),
        out_specs=(VMEM,) * 9,
        scratch_shapes=[vmem(width, share) for share in shares]
        + [vmem(rows_n - 1, depth, share) for share in shares + [io_rows]]
        + [vmem(io_full, width), vmem(cols_n - 1, io_rows, width), vmem(width, io_rows)]
        + [small_f32((), dims) for dims in small]
        + [small_f32((rows_n - 1,), dims) for dims in small]
        + [small_f32((cols_n - 1,), dims) for dims in small[:2]]
        + [
            pltpu.SemaphoreType.DMA((2, 9, rows_n - 1)),
            pltpu.SemaphoreType.DMA((2, 3, cols_n - 1)),
        ],
        compiler_params=pltpu.CompilerParams(
            vmem_limit_bytes=VMEM_LIMIT, collective_id=7, has_side_effects=True
        ),
        cost_estimate=KERNEL_COST,
    )(first_gain, *[ref for one in sets for ref in one])


def gather_kernel(
    rows_n,
    cols_n,
    pack,
    io,
    taps,
    first,
    pack_all,
    io_all,
    taps_all,
    first_all,
    row_sems,
    io_sems,
    tap_sems,
    own_sems,
    first_sems,
):
    me, at = lax.axis_index("row"), lax.axis_index("col")
    io_rows = io.shape[0]
    place = pl.ds(pl.multiple_of(at * io_rows, io_rows), io_rows)
    row_peers = [{"row": me ^ k} for k in range(1, rows_n)]
    col_peers = [{"col": at ^ k} for k in range(1, cols_n)]
    barrier = pltpu.get_barrier_semaphore()
    for other in row_peers + col_peers:
        pl.semaphore_signal(barrier, inc=1, device_id=other, device_id_type=MESH)
    pl.semaphore_wait(barrier, rows_n + cols_n - 2)

    def send_one(source, target, sems, k, other):
        return send(source, target, sems.at[0, k], sems.at[1, k], other)

    own = [
        pltpu.make_async_copy(pack, pack_all.at[me], own_sems.at[0]),
        pltpu.make_async_copy(io, io_all.at[me, place], own_sems.at[1]),
        pltpu.make_async_copy(taps, taps_all.at[place], own_sems.at[2]),
        pltpu.make_async_copy(first, first_all.at[at], own_sems.at[3]),
    ]
    for copy in own:
        copy.start()

    def send_first(which, k, source, owner, other):
        return make_send(
            source,
            first_all.at[owner],
            first_sems.at[0, which, k],
            first_sems.at[1, which, k],
            other,
        )

    far = [
        send_first(0, k, first, at, {"col": at ^ (2 * k)}) for k in range(1, cols_n // 2)
    ]
    near = [send_first(1, 0, first, at, {"col": at ^ 1})]
    for copy in far + near:
        copy.start()
    io_copies = [
        send_one(io, io_all.at[me, place], io_sems, k, other) for k, other in enumerate(col_peers)
    ]
    copies = [
        send_one(taps, taps_all.at[place], tap_sems, k, other)
        for k, other in enumerate(col_peers)
    ]
    copies += [
        send_one(pack, pack_all.at[me], row_sems, k, other) for k, other in enumerate(row_peers)
    ]
    own[1].wait()
    for copy in io_copies:
        copy.wait()
    copies += [
        send_one(io_all.at[me], io_all.at[me], row_sems, rows_n - 1 + k, other)
        for k, other in enumerate(row_peers)
    ]
    for k, copy in enumerate(far, 1):
        copy.wait()
        owner = at ^ (2 * k)
        near.append(send_first(1, k, first_all.at[owner], owner, {"col": at ^ 1}))
        near[-1].start()
    own[0].wait()
    own[2].wait()
    own[3].wait()
    for copy in near + copies:
        copy.wait()


def gather_weights(pack, io, taps, first, rows_n, cols_n):
    shape = jax.ShapeDtypeStruct
    return pl.pallas_call(
        functools.partial(gather_kernel, rows_n, cols_n),
        out_shape=(
            shape((rows_n,) + pack.shape, BF16),
            shape((rows_n, cols_n * io.shape[0], io.shape[1]), BF16),
            shape((cols_n * io.shape[0], taps.shape[1]), BF16),
            shape((cols_n,) + first.shape, BF16),
        ),
        in_specs=[ANY] * 4,
        out_specs=(ANY,) * 4,
        scratch_shapes=[
            pltpu.SemaphoreType.DMA((2, 2 * (rows_n - 1))),
            pltpu.SemaphoreType.DMA((2, cols_n - 1)),
            pltpu.SemaphoreType.DMA((2, cols_n - 1)),
            pltpu.SemaphoreType.DMA((4,)),
            pltpu.SemaphoreType.DMA((2, 2, cols_n // 2)),
        ],
        compiler_params=pltpu.CompilerParams(collective_id=1, has_side_effects=True),
        cost_estimate=pl.CostEstimate(flops=1, bytes_accessed=1, transcendentals=0),
    )(pack, io, taps, first)


def row_norm(values, scale_gain):
    return values * lax.rsqrt(jnp.mean(values * values, axis=1, keepdims=True) + EPS) * scale_gain


def norm_adjoint(values, scale_gain, cotangent):
    inverse = lax.rsqrt(jnp.mean(values * values, axis=1, keepdims=True) + EPS)
    unit = values * inverse
    scaled = cotangent * scale_gain
    back = inverse * (scaled - unit * jnp.mean(scaled * unit, axis=1, keepdims=True))
    return back, jnp.sum(cotangent * unit, axis=0, keepdims=True)


def local(
    layer_input,
    out_grad,
    seq_lengths,
    routes,
    route_gates,
    first_gain,
    gate_branch_proj,
    conv_in_proj,
    state_io_proj,
    step_proj,
    conv_kernel,
    conv_offset,
    state_conv_kernel,
    state_conv_offset,
    decay_log,
    step_offset,
    skip_scale,
    mixer_gain,
    out_proj,
    second_gain,
    expert_gate,
    expert_up,
    expert_down,
    shared_gate,
    shared_up,
    shared_down,
):
    rows_n = lax.axis_size("row")
    cols_n = lax.axis_size("col")
    row_index = lax.axis_index("row")
    col_index = lax.axis_index("col")
    micro_count, own_count, width = layer_input.shape
    length = own_count * cols_n
    local_experts, depth, hidden_width = expert_gate.shape
    share = conv_kernel.shape[1]
    heads = decay_log.shape[0]
    size = share // heads
    inner = share * cols_n
    io_width = state_conv_kernel.shape[1]
    shared_width = shared_gate.shape[1]
    per_device = max(1, local_experts // rows_n)
    split = max(1, rows_n // local_experts)
    part_width = hidden_width // split

    def swap(values, k):
        if k == 0:
            return values
        return lax.ppermute(values, "row", [(i, i ^ k) for i in range(rows_n)])

    def peer(k):
        return row_index ^ k

    def unit_at(member):
        return (member * per_device) // split, (member % split) * part_width

    def gather_width(pack):
        full = jnp.zeros((pack.shape[0], width), pack.dtype)
        for k in range(rows_n):
            full = lax.dynamic_update_slice(full, swap(pack, k), (0, peer(k) * depth))
        return full

    def after(value, *others):
        return lax.optimization_barrier((value, *others))[0]

    micro = range(micro_count)
    own_rows = [layer_input[m].astype(F32) for m in micro]
    first_rows = [row_norm(own_rows[m], first_gain).astype(BF16) for m in micro]

    own_taps = jnp.concatenate([state_conv_kernel, state_conv_offset[None, :]], axis=0).T
    tap_parts = []
    for _ in range(3):
        tap_parts.append(own_taps.astype(BF16))
        own_taps = own_taps - tap_parts[-1].astype(F32)
    tap_parts = jnp.pad(jnp.concatenate(tap_parts, axis=1), ((0, 0), (0, LANES - 15)))
    step_rows_t = jnp.pad(step_proj.T, ((0, HEAD_ROWS - heads), (0, 0)))
    in_all, io_all, taps_all, first_all = gather_weights(
        jnp.concatenate([gate_branch_proj.T, conv_in_proj.T, out_proj, step_rows_t], axis=0),
        state_io_proj.T,
        tap_parts,
        first_rows[0],
        rows_n,
        cols_n,
    )

    normed = [first_all.reshape(length, width)] + [
        lax.all_gather(after(rows, in_all), "col", axis=0, tiled=True) for rows in first_rows[1:]
    ]

    def join(parts, first, count):
        return jnp.concatenate(
            [parts[member, first : first + count] for member in range(rows_n)], axis=1
        )

    wb, wc, wo = [join(in_all, at * share, share) for at in range(3)]
    ws = join(in_all, 3 * share, HEAD_ROWS)
    wio = join(io_all, 0, 2 * NS)
    taps_all = taps_all.astype(F32)
    io_taps = jnp.pad(taps_all[:, :5] + taps_all[:, 5:10] + taps_all[:, 10:15], ((0, 0), (0, 3)))
    chan = jnp.concatenate(
        [
            conv_kernel.T,
            conv_offset[:, None],
            mixer_gain[:, None],
            jnp.repeat(skip_scale, size)[:, None],
            jnp.zeros((share, 1), F32),
        ],
        axis=1,
    )
    head_params = jnp.pad(
        jnp.stack([step_offset, jnp.exp(decay_log)], axis=1), ((0, HEAD_ROWS - heads), (0, 6))
    )
    weights = (wb, wc, wio, ws, wo, chan, io_taps, head_params)

    downs = []
    for k in range(rows_n):
        first, hidden_at = unit_at(peer(k))
        part = lax.dynamic_slice(
            expert_down, (first, hidden_at, 0), (per_device, part_width, depth)
        )
        downs.append(swap(after(jnp.swapaxes(part, 1, 2), in_all), k))

    place_j = lax.broadcasted_iota(jnp.int32, (length, length), 0)
    place_i = lax.broadcasted_iota(jnp.int32, (length, length), 1)
    upper = (place_j <= place_i).astype(BF16)
    expert_ids = col_index * local_experts + jnp.arange(local_experts, dtype=jnp.int32)

    def slots_of(m):
        hit = routes[m].T[None] == expert_ids[:, None, None]
        mask = jnp.any(hit, axis=1)
        gates = jnp.sum(jnp.where(hit, route_gates[m].T[None], 0.0), axis=1)
        rank = dot_plain(mask.astype(BF16), upper).astype(jnp.int32) - 1
        slot = jnp.where(mask, rank, -(2**20))
        firsts = [unit_at(peer(k))[0] for k in range(rows_n)]
        take = lambda rows: jnp.concatenate(
            [lax.dynamic_slice(rows, (first, 0), (per_device, length)) for first in firsts], axis=0
        )
        return take(slot), take(gates)

    def swap_all(parts):
        return [swap(part, k) for k, part in enumerate(parts)]

    own_cots = []
    for m in micro:
        positions = col_index * own_count + jnp.arange(own_count)
        valid = (positions < seq_lengths[m, 0])[:, None]
        own_cots.append(jnp.where(valid, out_grad[m], jnp.zeros_like(out_grad[m])))
    slot_rows = [slots_of(m) for m in micro]
    slot_cols = [(slot.T, gates.T) for slot, gates in slot_rows]

    last = [None]

    def step(function, *args):
        if last[0] is not None:
            args, _ = lax.optimization_barrier((args, last[0]))
        out = function(*args)
        last[0] = jax.tree.leaves(out)[0]
        return out

    state = [{} for _ in micro]

    def mix(m, weight):
        s = state[m]
        (s["y_part"], s["squares"], *s["saved"]), received = step(
            lambda xn: mixer_forward(
                rows_n, cols_n, (per_device, split), weight, xn, *weights, heads
            ),
            normed[m],
        )
        return [weight, *received]

    def sum_y(m, *others):
        s = state[m]
        s["y"] = lax.psum_scatter(
            after(s["y_part"], *others), "col", scatter_dimension=0, tiled=True
        )

    def scale_of(m):
        s = state[m]
        s["rms"] = lax.rsqrt(s["squares"][0] / inner + EPS)

    def second_norm(m):
        s = state[m]

        def run(y_own, rms):
            y_own = y_own.astype(F32)
            own_rms = lax.dynamic_slice(rms, (col_index * own_count,), (own_count,))
            residual = own_rows[m] + own_rms[:, None] * y_own
            return row_norm(residual, second_gain).astype(BF16), residual, y_own

        second, s["residual"], s["y_own"] = step(run, s["y"], s["rms"])
        s["second"] = lax.all_gather(second, "col", axis=0, tiled=True)
        s["second_own"] = second

    def gather_cot(m, *others):
        return lax.all_gather(after(own_cots[m], *others), "col", axis=0, tiled=True)

    def spread_cot(m):
        s = state[m]
        slot, gates_of = slot_rows[m]
        (s["cot_rows"],) = step(
            lambda cot: spread_rows(rows_n, slot, gates_of, cot), s["cot"]
        )

    def spread_tokens(m):
        s = state[m]
        slot, gates_of = slot_rows[m]
        (
            s["token_rows"],
            s["shared_hidden"],
            s["d_shared_gate"],
            s["d_shared_up"],
            *s["shared_grads"],
        ) = step(
            lambda second, cot, before: spread_rows(
                rows_n,
                slot,
                gates_of,
                second,
                cot,
                shared_w,
                before,
                BF16 if m == micro_count - 1 else F32,
            ),
            s["second"],
            s["cot"],
            state[m - 1]["shared_grads"] if m else (),
        )

    def experts(m):
        s = state[m]
        later = state[m + 1] if m + 1 < micro_count else None
        part, out_rows, saved, spread = step(
            lambda cot, grads, *args: expert_rows(
                () if later is None else (*slot_rows[m + 1], cot), grads, slot_cols[m][0], *args
            ),
            s["cot"] if later is None else later["cot"],
            s["shared_grads"],
            s["token_rows"],
            s["cot_rows"],
            s["d_shared_gate"],
            s["d_shared_up"],
            shared_w,
            gates,
            ups,
            downs,
        )
        s["expert_saved"] = [s["token_rows"], s["cot_rows"], *saved]
        if later is None:
            s["shared_totals"] = spread
        else:
            (later["cot_rows"],) = spread
        s["second_share"] = lax.psum_scatter(part, "col", scatter_dimension=0, tiled=True)
        s["out_rows"] = list(out_rows) if later is None else swap_all(out_rows)

    def ahead_rows(m, parts=()):
        s = state[m]
        slot_t, gates_t = slot_cols[m]
        part, *stacked = step(
            lambda rows, left, parts: combine_rows(
                slot_t, gates_t, rows, left, shared_out, parts
            ),
            s["out_rows"],
            s["shared_hidden"],
            parts,
        )
        s["branch_share"] = lax.psum_scatter(part, "col", scatter_dimension=0, tiled=True)
        return stacked

    def second_back(m):
        s = state[m]

        def run(share_in):
            back, gain_grad = norm_adjoint(s["residual"], second_gain, share_in.astype(F32))
            residual_grad = own_cots[m].astype(F32) + back
            low = residual_grad.astype(BF16)
            cross = jnp.sum(low.astype(F32) * s["y_own"], axis=1, keepdims=True)
            parts = [low]
            for _ in range(3):
                parts.append(cross.astype(BF16))
                cross = cross - parts[-1].astype(F32)
            parts.append(jnp.zeros((own_count, LANES - 3), BF16))
            return jnp.concatenate(parts, axis=1), residual_grad, gain_grad

        low, s["residual_grad"], s["second_gain_grad"] = step(run, s["second_share"])
        s["low"] = low
        s["d_res"] = lax.all_gather(low, "col", axis=0, tiled=True)

    def mix_back(m, parts, moved=()):
        s = state[m]
        scale_rows = jnp.pad(
            jnp.stack([s["rms"], jnp.full((length,), 1.0 / inner, F32)]), ((0, 6), (0, 0))
        )
        (first_part, *s["back"]), stacked, arrived = step(
            lambda d_res, scales, parts, moved: mixer_backward(
                parts, moved, d_res, scales, normed[m], weights, s["saved"], heads
            ),
            s["d_res"],
            scale_rows,
            parts,
            moved,
        )
        s["first_part"] = first_part
        return stacked, arrived

    def total_of(parts):
        return jax.tree.map(lambda *terms: functools.reduce(jnp.add, terms), *parts)

    def expert_grads(*saved):
        def over_rows(left, right):
            return jnp.einsum("ecd,ech->edh", left, right, preferred_element_type=F32)

        totals = total_of(
            [
                (over_rows(tokens, d_pre), over_rows(cot, hidden))
                for tokens, cot, hidden, d_pre in saved
            ]
        )
        both, down = totals[0].astype(BF16), totals[1].astype(BF16)
        return [
            [
                lax.dynamic_slice(full, (0, peer(k) * depth, at), (per_device, depth, part_width))
                for k in range(rows_n)
            ]
            for full, at in ((both, 0), (both, part_width), (down, 0))
        ]

    def sum_first(m, *others):
        s = state[m]
        s["first_share"] = lax.psum_scatter(
            after(s["first_part"], *others), "col", scatter_dimension=0, tiled=True
        )

    def finish_output(m):
        s = state[m]
        s["output"] = step(
            lambda share_in: (s["residual"] + share_in.astype(F32)).astype(BF16), s["branch_share"]
        )

    def finish_input(m):
        s = state[m]

        def run(share_in):
            back, _ = norm_adjoint(own_rows[m], first_gain, share_in.astype(F32))
            return s["residual_grad"] + back

        s["input_grad"] = step(run, s["first_share"])

    def whole_experts(stacked):
        stacked = stacked.reshape(local_experts, split, depth, part_width)
        return jnp.swapaxes(stacked, 1, 2).reshape(local_experts, depth, hidden_width)

    def arrive(parts):
        return step(lambda *values: values, *parts)

    first, second = 0, micro_count - 1
    state[first]["cot"] = gather_cot(first, in_all)
    gates = mix(first, expert_gate)
    (normed[second],) = arrive([normed[second]])
    sum_y(first)
    scale_of(first)
    state[second]["cot"] = gather_cot(second, state[first]["squares"])
    ups = mix(second, expert_up)
    downs = arrive(downs)
    (state[first]["cot"],) = arrive([state[first]["cot"]])
    scale_of(second)
    second_norm(first)
    sum_y(second, state[first]["second_own"])
    spread_cot(first)
    shared_full = step(
        lambda *parts: gather_width(jnp.concatenate(parts, axis=0)),
        shared_gate.T,
        shared_up.T,
        shared_down,
    )
    shared_w = (
        shared_full[:shared_width],
        shared_full[shared_width : 2 * shared_width],
        shared_full[2 * shared_width :],
    )
    shared_out = shared_w[2]
    spread_tokens(first)
    second_norm(second)
    experts(first)
    spread_tokens(second)
    second_back(first)
    experts(second)
    (state[first]["d_res"],) = arrive([state[first]["d_res"]])
    shared_totals = state[second]["shared_totals"]
    gate_grads, up_grads, down_grads = step(expert_grads, *[s["expert_saved"] for s in state])
    state[first]["out_rows"] = arrive(state[first]["out_rows"])
    second_back(second)
    ahead_rows(first)
    rows = state[second]["out_rows"]
    gate_grads, arrived = mix_back(first, gate_grads, rows[1:])
    state[second]["out_rows"] = [rows[0], *arrived]
    (state[second]["d_res"],) = arrive([state[second]["d_res"]])
    sum_first(first, state[second]["low"])
    (down_grads,) = ahead_rows(second, down_grads)
    finish_output(first)
    up_grads, _ = mix_back(second, up_grads)
    sum_first(second)
    finish_input(first)
    finish_output(second)
    sets = []
    for m in micro:
        s = state[m]
        gain_part, mixed, d_branch, d_conv, d_io, d_step, chan_grad, io_grad, head_grad = s["back"]
        sets.append(
            [
                normed[m],
                s["d_res"],
                d_branch,
                d_conv,
                mixed,
                d_step,
                d_io,
                gain_part,
                s["second_gain_grad"],
                chan_grad,
                io_grad,
                head_grad,
            ]
        )
    branch_grad, conv_grad, out_grad_sum, step_grad, io_proj_grad, gains, io_sums, chans, by_head = (
        step(lambda sets: tail_sums(rows_n, cols_n, first_gain[None, :], sets), sets)
    )
    finish_input(second)
    io_values = lax.dynamic_slice(io_sums, (0, col_index * io_width), (5, io_width))
    return (
        jnp.stack([s["output"] for s in state]),
        jnp.stack([s["input_grad"] for s in state]),
        gains[0],
        branch_grad,
        conv_grad,
        io_proj_grad,
        step_grad[:, :heads],
        chans[:4],
        chans[4],
        io_values[:4],
        io_values[4],
        by_head[:heads, 0],
        by_head[:heads, 1],
        by_head[:heads, 2],
        chans[5],
        out_grad_sum.T,
        gains[1],
        whole_experts(gate_grads).astype(F32),
        whole_experts(up_grads).astype(F32),
        jnp.swapaxes(whole_experts(down_grads).astype(F32), 1, 2),
        shared_totals[0],
        shared_totals[1],
        shared_totals[2].T,
    )


def solution(mesh):
    both = P(None, ("row", "col"), None)
    placed = (
        both,
        both,
        P(None, "row"),
        P(None, "row", None),
        P(None, "row", None),
        P(),
        P("row", "col"),
        P("row", "col"),
        P("row", "col"),
        P("row", "col"),
        P(None, "col"),
        P("col"),
        P(None, "col"),
        P("col"),
        P("col"),
        P("col"),
        P("col"),
        P("col"),
        P("col", "row"),
        P(),
        P("col", "row", None),
        P("col", "row", None),
        P("col", None, "row"),
        P("row", "col"),
        P("row", "col"),
        P("col", "row"),
    )
    return jax.shard_map(
        local,
        mesh=mesh,
        in_specs=placed,
        out_specs=(both, both, P()) + placed[6:19] + (P(),) + placed[20:],
        check_vma=False,
    )
```

time: 1030 us -> 931 us (0.904)
  Pallas kernels: 549 us -> 729 us
  waiting for transfers between devices: 150 us -> 29 us
  blocking collectives: 54.4 us -> 0 us
  local copies, waits for them, and re-layouts: 91.6 us -> 57.2 us
  matrix products: 60.1 us -> 27.3 us
  starting transfers between devices: 33.8 us -> 12.5 us
  other arithmetic: 68.1 us -> 54.8 us
    pallas_call x8 -> x12, Pallas kernels: 496 us -> 671 us  [the longest x2 165 us: expert_rows(): pl.pallas_call(kernel, out_shape=tuple(out_shape), in_specs=[VMEM] * (7 +...]
    ppermute x27 -> x9, waiting for transfers between devices: 84.1 us -> 23.9 us  [swap(): return lax.ppermute(values, 'row', [(i, i ^ k) for i in range(rows_n)])]
    psum x3 -> x0, blocking collectives: 54.4 us -> none  [the longest x2 27.8 us: scale_of(): lax.psum(jnp.sum(squares, axis=0), 'col')]
    all_gather x2 -> x1, waiting for transfers between devices: 35.7 us -> 0.02 us  [local(): lax.all_gather(after(rows, in_all), 'col', axis=0, tiled=True)]
    dot_general x18 -> x2, matrix products: 35.8 us -> 0.63 us  [contract(): lax.dot_general(left_op, right_op, (((left_dim,), (right_dim,)), ((), ())...]
    all_gather x2, waiting for transfers between devices: 23.6 us -> 0.01 us  [second_back(): s['d_res'] = lax.all_gather(low, 'col', axis=0, tiled=True)]
    ppermute x27 -> x9, starting transfers between devices: 31.8 us -> 10.7 us  [swap(): return lax.ppermute(values, 'row', [(i, i ^ k) for i in range(rows_n)])]
    add x9 -> x0, other arithmetic: 11.3 us -> none  [the longest x6 7.94 us: total_of(): return jax.tree.map(lambda *terms: functools.reduce(jnp.add, terms), *parts)]
  transfers between devices with their start and end apart: 44 -> 24, of which waited for: 10 -> 5; matrix products, arithmetic and copies ran while one was open for 20% -> 12% of each run, Pallas kernels for 54% -> 73%
where the time goes in v3:
time: 931 us; the launch traced here: 925 us
  Pallas kernels  729 us (78%)
  local copies, waits for them, and re-layouts  57.2 us (6%)
  other arithmetic  54.8 us (6%)
  waiting for transfers between devices  29 us (3%)
  matrix products  27.3 us (3%)
  between operations  15.7 us (2%)
  starting transfers between devices  12.5 us (1%)
    pallas_call x2, Pallas kernels, expert_rows(): pl.pallas_call(kernel, out_shape=tuple(out_shape), in_specs=[VMEM] * (7 +...  165 us
    pallas_call x3, Pallas kernels, spread_rows(): pl.pallas_call(functools.partial(spread_kernel, members, weighted, len(be...  136 us
    pallas_call x2, Pallas kernels, mixer_backward(): pl.pallas_call(functools.partial(mixer_backward_kernel, heads, len(parts)...  130 us
    pallas_call x2, Pallas kernels, mixer_forward(): pl.pallas_call(functools.partial(mixer_forward_kernel, heads, cols_n, *un...  115 us
    pallas_call x1, Pallas kernels, tail_sums(): pl.pallas_call(functools.partial(tail_kernel, rows_n, cols_n, len(sets)),...  75.4 us
    pallas_call x1, Pallas kernels, gather_weights(): pl.pallas_call(functools.partial(gather_kernel, rows_n, cols_n), out_shap...  57.8 us
    pallas_call x2, Pallas kernels, combine_rows(): pl.pallas_call(functools.partial(combine_kernel, members, bool(parts)), o...  48.9 us
    dot_general x4, matrix products, over_rows(): return jnp.einsum('ecd,ech->edh', left, right, preferred_element_type=F32)  26.6 us
  transfers between devices with their start and end apart: 24, of which 5 were waited for; matrix products, arithmetic and copies ran while one was open for 12% of the time, Pallas kernels for 73%

profile of v3, /device:TPU:0, one launch (start us, length us, event | category | flops | bytes accessed | tf_op | source)
XLA Modules:
  0.0 925.1 jit_solution(13866460587314352923)
XLA Ops:
  12.6 1.9 fusion.30
  15.6 57.8 %shard_map.425 = (bf16[4,1168,384]{2,1,0:T(8,128)(2,1)}, bf16[4,256,384]{2,1,0:T(8,128)(2,1)}, bf16[256,128]{1,0:T(8,128)(2,1)}, bf16[8,128,1536]{2,1,0:T(8,128)(2,1)}) custom-call(bf16[1168,384]{1,0:T(8,128)(2,1)} %fusion.19.pack, bf16[32,384]{1,0:T(8,128)(2,1)} %bitcast.201, bf16[32,128]{1,0:T(8,128)(2,1)} %fusion.51.taps, ...), custom_call_target="tpu_custom_call" | custom-call | flops 1 | bytes 1 | tf_op jit(solution)/shard_map/pallas_call | solution.py:1327
  79.1 1.4 slice_bitcast_fusion.19
  86.0 44.5 %shard_map.426 = (bf16[1024,1536]{1,0:T(8,128)(2,1)}, f32[1,1024]{1,0:T(1,128)}, f32[384,1024]{1,0:T(8,128)}, f32[384,1024]{1,0:T(8,128)}, f32[256,1024]{1,0:T(8...) custom-call(bf16[1024,1536]{1,0:T(8,128)(2,1)} %bitcast.210, ...), custom_call_target="tpu_custom_call" | custom-call | flops 30000001024 | bytes 1048576 | tf_op jit(solution)/shard_map/pallas_call | solution.py:317
  130.8 3.2 constant_dynamic-slice_fusion.29
  133.9 2.3 copy.217
  136.3 1.6 collective-permute-start.1
  142.5 70.7 %shard_map.427 = (bf16[1024,1536]{1,0:T(8,128)(2,1)}, f32[1,1024]{1,0:T(1,128)}, f32[384,1024]{1,0:T(8,128)}, f32[384,1024]{1,0:T(8,128)}, f32[256,1024]{1,0:T(8...) custom-call(bf16[1024,1536]{1,0:T(8,128)(2,1)} %all-gather.10.cloned, ...), custom_call_target="tpu_custom_call" | custom-call | flops 30000001024 | bytes 1048576 | tf_op jit(solution)/shard_map/pallas_call | solution.py:317
  214.7 2.0 multiply_convert_fusion.1
  220.4 44.2 %shard_map.428.refs_2_ = bf16[2,576,1536]{2,1,0:T(8,128)(2,1)} custom-call(s32[8,1024]{1,0:T(8,128)} %pad_add_fusion.slot, f32[8,1024]{1,0:T(8,128)} %pad_maximum_fusion.7.gates, bf16[1024,1536]{1,0:T(8,128)(2,1)} %all-gather.8.cloned.1.call-done.source.refs_0_), custom_call_target="tpu_custom_call" | custom-call | flops 30000001024 | bytes 1048576 | tf_op jit(solution)/shard_map/pallas_call | solution.py:845
  265.4 1.5 collective-permute-start.3
  266.8 1.5 collective-permute-start.5
  268.5 5.8 collective-permute-done.3
  274.7 3.7 collective-permute-done.5
  279.6 44.3 %shard_map.429 = (bf16[2,576,1536]{2,1,0:T(8,128)(2,1)}, bf16[1024,128]{1,0:T(8,128)(2,1)}, bf16[1024,128]{1,0:T(8,128)(2,1)}, bf16[1024,128]{1,0:T(8,128)(2,1)}...) custom-call(s32[8,1024]{1,0:T(8,128)} %pad_add_fusion.slot, f32[8,1024]{1,0:T(8,128)} %pad_maximum_fusion.7.gates, ...), custom_call_target="tpu_custom_call" | custom-call | flops 30000001024 | bytes 1048576 | tf_op jit(solution)/shard_map/pallas_call | solution.py:845
  325.3 2.0 multiply_convert_fusion
  330.3 3.7 all-gather.12.cloned.1.call-done.refs_9_.refs_0_
  334.0 97.1 %shard_map.430 = (bf16[1024,1536]{1,0:T(8,128)(2,1)}, bf16[288,1536]{1,0:T(8,128)(2,1)}, bf16[288,1536]{1,0:T(8,128)(2,1)}, bf16[288,1536]{1,0:T(8,128)(2,1)}, b...) custom-call(s32[1024,8]{1,0:T(8,128)} %bitcast.191, ...), custom_call_target="tpu_custom_call" | custom-call | flops 30000001024 | bytes 1048576 | tf_op jit(solution)/shard_map/pallas_call | solution.py:1062
  431.2 47.9 %shard_map.431 = (bf16[2,576,1536]{2,1,0:T(8,128)(2,1)}, bf16[1024,128]{1,0:T(8,128)(2,1)}, bf16[1024,128]{1,0:T(8,128)(2,1)}, bf16[1024,128]{1,0:T(8,128)(2,1)}...) custom-call(s32[8,1024]{1,0:T(8,128)} %pad_add_fusion.1.refs_7_.slot, ...), custom_call_target="tpu_custom_call" | custom-call | flops 30000001024 | bytes 1048576 | tf_op jit(solution)/shard_map/pallas_call | solution.py:845
  479.2 2.0 fusion.28
  481.2 1.5 fusion.26
  485.5 67.6 %shard_map.432 = (bf16[1024,1536]{1,0:T(8,128)(2,1)}, bf16[288,1536]{1,0:T(8,128)(2,1)}, bf16[288,1536]{1,0:T(8,128)(2,1)}, bf16[288,1536]{1,0:T(8,128)(2,1)}, b...) custom-call(s32[1024,8]{1,0:T(8,128)} %bitcast.193, ...), custom_call_target="tpu_custom_call" | custom-call | flops 30000001024 | bytes 1048576 | tf_op jit(solution)/shard_map/pallas_call | solution.py:1062
  553.2 1.5 collective-permute-start.6
  554.7 1.5 collective-permute-start.7
  556.8 10.7 %fusion.64 = f32[2,1536,1024]{2,1,0:T(8,128)} fusion(bf16[2,576,1536]{2,1,0:T(8,128)(2,1)} %get-tuple-element.370.refs_1_, bf16[2,576,1024]{2,1,0:T(8,128)(2,1)} %get-tuple-element.371), kind=kOutput, calls=%fused_computation.209 | convolution fusion | flops 3623878656 | bytes 18481152 | tf_op jit(solution)/shard_map/ecd,ech->edh/dot_general | solution.py:1671
  567.5 8.2 add_convert_fusion
  575.7 2.8 constant_dynamic-slice_fusion.1
  578.5 14.1 %collective-permute-done.7.refs_2_ = bf16[288,1536]{1,0:T(8,128)(2,1)} collective-permute-done((bf16[288,1536]{1,0:T(8,128)(2,1)}, bf16[288,1536]{1,0:T(8,128)(2,1)}, u32[]{:S(2)}, u32[]{:S(2)}) %collective-permute-start.7) | collective-permute-done | bytes 884768 | tf_op jit(solution)/shard_map/ppermute | solution.py:1409
  592.6 1.4 fusion.29
  594.0 1.5 fusion.27
  598.1 11.6 %shard_map.433 = bf16[1024,1536]{1,0:T(8,128)(2,1)} custom-call(s32[1024,8]{1,0:T(8,128)} %bitcast.192, f32[1024,8]{1,0:T(8,128)} %bitcast.196, bf16[1024,128]{1,0:T(8,128)(2,1)} %get-tuple-element.380.extra_left, bf16[128,1536]{1,0:T(8,128)(2,1)} %get-tuple-element.667.refs_3_.extra_right, bf16[288,1536]{1,0:T(8,128)(2,1)} %get-tuple-element.381.refs_0_, ...), custom_call_target="tpu_custom_call" | custom-call | flops 30000001024 | bytes 1048576 | tf_op jit(solution)/shard_map/pallas_call | solution.py:708
  611.1 81.4 %shard_map.434 = (bf16[1024,1536]{1,0:T(8,128)(2,1)}, f32[8,1536]{1,0:T(8,128)}, bf16[384,1024]{1,0:T(8,128)(2,1)}, bf16[384,1024]{1,0:T(8,128)(2,1)}, bf16[384,...) custom-call(bf16[1024,1664]{1,0:T(8,128)(2,1)} %all-gather.18.cloned, ...), custom_call_target="tpu_custom_call" | custom-call | flops 30000001024 | bytes 1048576 | tf_op jit(solution)/shard_map/pallas_call | solution.py:593
  694.2 4.8 fusion.65
  699.1 2.9 add_convert_fusion.1
  702.0 1.7 constant_dynamic-slice_fusion.5
  703.7 37.2 %shard_map.435 = (bf16[1024,1536]{1,0:T(8,128)(2,1)}, bf16[4,2,384,512]{3,2,1,0:T(8,128)(2,1)}) custom-call(s32[1024,8]{1,0:T(8,128)} %bitcast.194, f32[1024,8]{1,0:T(8,128)} %bitcast.195, bf16[1024,128]{1,0:T(8,128)(2,1)} %get-tuple-element.414.extra_left, bf16[128,1536]{1,0:T(8,128)(2,1)} %get-tuple-element.667.refs_3_.extra_right, ...), custom_call_target="tpu_custom_call" | custom-call | flops 30000001024 | bytes 1048576 | tf_op jit(solution)/shard_map/pallas_call | solution.py:708
  745.5 48.9 %shard_map.436 = (bf16[1024,1536]{1,0:T(8,128)(2,1)}, f32[8,1536]{1,0:T(8,128)}, bf16[384,1024]{1,0:T(8,128)(2,1)}, bf16[384,1024]{1,0:T(8,128)(2,1)}, bf16[384,...) custom-call(bf16[1024,1664]{1,0:T(8,128)(2,1)} %all-gather.20.cloned, ...), custom_call_target="tpu_custom_call" | custom-call | flops 30000001024 | bytes 1048576 | tf_op jit(solution)/shard_map/pallas_call | solution.py:593
  794.5 5.6 bitcast_convert_fusion.2
  800.7 3.8 bitcast_convert_fusion
  804.5 6.6 copy.210
  812.4 5.6 bitcast_convert_fusion.1
  820.3 75.4 %shard_map.437 = (f32[384,384]{1,0:T(8,128)}, f32[384,384]{1,0:T(8,128)}, f32[384,384]{1,0:T(8,128)}, f32[384,16]{1,0:T(8,128)}, f32[384,32]{1,0:T(8,128)}, /*in...) custom-call(f32[1,1536]{1,0:T(1,128)} %broadcast_in_dim.107.first_gain, ...), custom_call_target="tpu_custom_call" | custom-call | flops 30000001024 | bytes 1048576 | tf_op jit(solution)/shard_map/pallas_call | solution.py:1219
  899.0 1.6 copy.212
  900.7 1.7 copy.211
  902.3 2.1 copy.213
  904.4 1.5 slice_reduce_fusion.2
  907.3 1.4 slice_reduce_fusion
  912.2 1.7 fusion.35
  (308 shorter events, 64.0 us)
Async XLA Ops:
  7.2 135.3 %all-gather.10.cloned.1.call-start = ((), (), s32[]{:S(2)}) async-start(), calls=%async_computation.10 | async-start | bytes 3538944 | tf_op jit(solution)/shard_map/all_gather | solution.py:1447
  12.6 60.9 %copy-start.56 = (s32[2,1]{0,1:T(1,128)S(1)}, s32[2,1]{0,1:T(1,128)}, u32[]{:S(2)}) copy-start(s32[2,1]{0,1:T(1,128)} %param.28) | copy-start | bytes 28
  12.6 62.8 %copy-start.15 = (bf16[2,128,1536]{2,1,0:T(8,128)(2,1)S(1)}, bf16[2,128,1536]{2,1,0:T(8,128)(2,1)}, u32[]{:S(2)}) copy-start(bf16[2,128,1536]{2,1,0:T(8,128)(2,1)} %param.27) | copy-start | bytes 2359300
  14.5 62.0 %copy-start.54 = (f32[384]{0:T(512)S(1)}, f32[384]{0:T(512)}, u32[]{:S(2)}) copy-start(f32[384]{0:T(512)} %param.37) | copy-start | bytes 4612
  14.5 62.0 %copy-start.55 = (f32[384]{0:T(512)S(1)}, f32[384]{0:T(512)}, u32[]{:S(2)}) copy-start(f32[384]{0:T(512)} %param.43) | copy-start | bytes 4612
  14.5 62.0 %copy-start.63 = (f32[6]{0:T(128)S(1)}, f32[6]{0:T(128)}, u32[]{:S(2)}) copy-start(f32[6]{0:T(128)} %param.40) | copy-start | bytes 76
  14.5 62.1 %copy-start.61 = (f32[6]{0:T(128)S(1)}, f32[6]{0:T(128)}, u32[]{:S(2)}) copy-start(f32[6]{0:T(128)} %param.41) | copy-start | bytes 76
  14.5 62.2 %copy-start.60 = (f32[6]{0:T(128)S(1)}, f32[6]{0:T(128)}, u32[]{:S(2)}) copy-start(f32[6]{0:T(128)} %param.42) | copy-start | bytes 76
  14.5 62.9 %copy-start.50 = (f32[4,384]{1,0:T(4,128)S(1)}, f32[4,384]{1,0:T(4,128)}, u32[]{:S(2)}) copy-start(f32[4,384]{1,0:T(4,128)} %param.36) | copy-start | bytes 18436
  73.4 139.9 %all-gather.8.cloned.1.call-start = ((), (), s32[]{:S(2)}) async-start(), calls=%async_computation.9 | async-start | bytes 3538944 | tf_op jit(solution)/shard_map/all_gather | solution.py:1556
  76.4 136.9 %reduce-scatter.9.cloned.1.call-start = ((), (), s32[]{:S(2)}) async-start(), calls=%async_computation.8 | async-start | bytes 3538944 | tf_op jit(solution)/shard_map/reduce_scatter | solution.py:1534
  130.5 149.0 %all-gather.14.cloned.1.call-start = ((), (), s32[]{:S(2)}) async-start(), calls=%async_computation.12 | async-start | bytes 3538944 | tf_op jit(solution)/shard_map/all_gather | solution.py:1552
  136.3 77.0 %collective-permute-start.1 = (bf16[2,384,512]{2,1,0:T(8,128)(2,1)}, bf16[2,384,512]{2,1,0:T(8,128)(2,1)}, u32[]{:S(2)}, u32[]{:S(2)}) collective-permute-start(bf16[2,384,512]{2,1,0:T(8,128)(2,1)} %bitcast.187), channel_id=1, source_target_pairs={{0,16},{8,24},{16,0},{24,8},{1,17},{9,25},{17,1},{25,9},{2,18},{10... | collective-permute-start | bytes 2359304 | tf_op jit(solution)/shard_map/ppermute | solution.py:1409
  139.0 74.2 %collective-permute-start.2 = (bf16[2,384,512]{2,1,0:T(8,128)(2,1)}, bf16[2,384,512]{2,1,0:T(8,128)(2,1)}, u32[]{:S(2)}, u32[]{:S(2)}) collective-permute-start(bf16[2,384,512]{2,1,0:T(8,128)(2,1)} %bitcast.188), channel_id=1, source_target_pairs={{0,24},{8,16},{16,8},{24,0},{1,25},{9,17},{17,9},{25,1},{2,26},{10... | collective-permute-start | bytes 2359304 | tf_op jit(solution)/shard_map/ppermute | solution.py:1409
  140.7 72.6 %collective-permute-start = (bf16[2,384,512]{2,1,0:T(8,128)(2,1)S(1)}, bf16[2,384,512]{2,1,0:T(8,128)(2,1)}, u32[]{:S(2)}, u32[]{:S(2)}) collective-permute-start(bf16[2,384,512]{2,1,0:T(8,128)(2,1)S(1)} %bitcast.189), channel_id=1, source_target_pairs={{0,8},{8,0},{16,24},{24,16},{1,9},{9,1},{17,25},{25,17},{2,10},{10... | collective-permute-start | bytes 2359304 | tf_op jit(solution)/shard_map/ppermute | solution.py:1409
  142.5 70.8 %copy-start.39 = (f32[1,1024]{1,0:T(1,128)}, f32[1,1024]{1,0:T(1,128)S(1)}, u32[]{:S(2)}) copy-start(f32[1,1024]{1,0:T(1,128)S(1)} %add_rsqrt_fusion.1) | copy-start | bytes 12292
  142.5 72.2 %copy-start.18 = (f32[1536]{0:T(1024)S(1)}, f32[1536]{0:T(1024)}, u32[]{:S(2)}) copy-start(f32[1536]{0:T(1024)} %param.45) | copy-start | bytes 18436
  213.4 267.8 %copy-start.36 = (f32[128]{0:T(128)}, f32[128]{0:T(128)S(1)}, u32[]{:S(2)}) copy-start(f32[128]{0:T(128)S(1)} %dynamic_slice.113) | copy-start | bytes 1540
  214.7 266.5 %copy-start.44 = (f32[128]{0:T(128)}, f32[128]{0:T(128)S(1)}, u32[]{:S(2)}) copy-start(f32[128]{0:T(128)S(1)} %add_rsqrt_fusion.3) | copy-start | bytes 1540
  216.9 107.1 %reduce-scatter.11.cloned.1.call-start = ((), (), s32[]{:S(2)}) async-start(), calls=%async_computation.13 | async-start | bytes 3538944 | tf_op jit(solution)/shard_map/reduce_scatter | solution.py:1534
  217.4 116.5 %all-gather.12.cloned.1.call-start = ((), (), s32[]{:S(2)}) async-start(), calls=%async_computation.11 | async-start | bytes 3538944 | tf_op jit(solution)/shard_map/all_gather | solution.py:1556
  218.0 213.2 %all-gather.16.cloned.1.call-start = ((), (), s32[]{:S(2)}) async-start(), calls=%async_computation.14 | async-start | bytes 3538944 | tf_op jit(solution)/shard_map/all_gather | solution.py:1552
  220.4 44.3 %copy-start.31 = (bf16[128,384]{1,0:T(8,128)(2,1)S(1)}, bf16[128,384]{1,0:T(8,128)(2,1)}, u32[]{:S(2)}) copy-start(bf16[128,384]{1,0:T(8,128)(2,1)} %param.51) | copy-start | bytes 294916
  220.4 46.4 %copy-start.52 = (f32[1,1024]{1,0:T(1,128)S(1)}, f32[1,1024]{1,0:T(1,128)}, u32[]{:S(2)}) copy-start(f32[1,1024]{1,0:T(1,128)} %get-tuple-element.303) | copy-start | bytes 12292
  264.7 9.9 %collective-permute-start.4 = (bf16[384,384]{1,0:T(8,128)(2,1)S(1)}, bf16[384,384]{1,0:T(8,128)(2,1)S(1)}, u32[]{:S(2)}, u32[]{:S(2)}) collective-permute-start(bf16[384,384]{1,0:T(8,128)(2,1)S(1)} %constant_dynamic-update-slice_fusion.4), channel_id=1, source_target_pairs={{0,16},{8,24},{16,0},{24,8},{1,17},{9,25},{17,1},{25,9},{2,18},{10... | collective-permute-start | bytes 884744 | tf_op jit(solution)/shard_map/ppermute | solution.py:1409
  265.4 9.0 collective-permute-start.3
  266.8 57.1 %copy-start.41 = (f32[1,1024]{1,0:T(1,128)}, f32[1,1024]{1,0:T(1,128)S(1)}, u32[]{:S(2)}) copy-start(f32[1,1024]{1,0:T(1,128)S(1)} %add_rsqrt_fusion) | copy-start | bytes 12292
  266.8 11.6 %collective-permute-start.5 = (bf16[384,384]{1,0:T(8,128)(2,1)S(1)}, bf16[384,384]{1,0:T(8,128)(2,1)S(1)}, u32[]{:S(2)}, u32[]{:S(2)}) collective-permute-start(bf16[384,384]{1,0:T(8,128)(2,1)S(1)} %constant_dynamic-update-slice_fusion.4), channel_id=1, source_target_pairs={{0,24},{8,16},{16,8},{24,0},{1,25},{9,17},{17,9},{25,1},{2,26},{10... | collective-permute-start | bytes 884744 | tf_op jit(solution)/shard_map/ppermute | solution.py:1409
  324.0 270.0 %copy-start.38 = (f32[128]{0:T(128)}, f32[128]{0:T(128)S(1)}, u32[]{:S(2)}) copy-start(f32[128]{0:T(128)S(1)} %dynamic_slice.122) | copy-start | bytes 1540
  325.3 268.7 %copy-start.46 = (f32[128]{0:T(128)}, f32[128]{0:T(128)S(1)}, u32[]{:S(2)}) copy-start(f32[128]{0:T(128)S(1)} %add_rsqrt_fusion.2) | copy-start | bytes 1540
  327.4 151.8 %reduce-scatter.13.cloned.1.call-start = ((), (), s32[]{:S(2)}) async-start(), calls=%async_computation.15 | async-start | bytes 3538944 | tf_op jit(solution)/shard_map/reduce_scatter | solution.py:1613
  431.1 48.1 %copy-start.1 = (bf16[128,1536]{1,0:T(8,128)(2,1)S(1)}, bf16[128,1536]{1,0:T(8,128)(2,1)}, u32[]{:S(2)}) copy-start(bf16[128,1536]{1,0:T(8,128)(2,1)} %reduce-scatter.9.cloned.1.call-done) | copy-start | bytes 1179652
  431.1 50.1 %copy-start.7 = (bf16[128,1536]{1,0:T(8,128)(2,1)S(1)}, bf16[128,1536]{1,0:T(8,128)(2,1)}, u32[]{:S(2)}) copy-start(bf16[128,1536]{1,0:T(8,128)(2,1)} %get-tuple-element.267) | copy-start | bytes 1179652
  431.1 125.6 %all-gather.18.cloned.1.call-start = ((), (), s32[]{:S(2)}) async-start(), calls=%async_computation.16 | async-start | bytes 3833856 | tf_op jit(solution)/shard_map/all_gather | solution.py:1647
  484.1 108.5 %reduce-scatter.15.cloned.1.call-start = ((), (), s32[]{:S(2)}) async-start(), calls=%async_computation.17 | async-start | bytes 3538944 | tf_op jit(solution)/shard_map/reduce_scatter | solution.py:1613
  553.1 150.6 %all-gather.20.cloned.1.call-start = ((), (), s32[]{:S(2)}) async-start(), calls=%async_computation.19 | async-start | bytes 3833856 | tf_op jit(solution)/shard_map/all_gather | solution.py:1647
  553.2 25.3 %collective-permute-start.6 = (bf16[288,1536]{1,0:T(8,128)(2,1)}, bf16[288,1536]{1,0:T(8,128)(2,1)}, u32[]{:S(2)}, u32[]{:S(2)}) collective-permute-start(bf16[288,1536]{1,0:T(8,128)(2,1)} %get-tuple-element.326), channel_id=1, source_target_pairs={{0,8},{8,0},{16,24},{24,16},{1,9},{9,1},{17,25},{25,17},{2,10},{10... | collective-permute-start | bytes 2654216 | tf_op jit(solution)/shard_map/ppermute | solution.py:1409
  554.7 37.9 %collective-permute-start.7 = (bf16[288,1536]{1,0:T(8,128)(2,1)}, bf16[288,1536]{1,0:T(8,128)(2,1)}, u32[]{:S(2)}, u32[]{:S(2)}) collective-permute-start(bf16[288,1536]{1,0:T(8,128)(2,1)} %get-tuple-element.327), channel_id=1, source_target_pairs={{0,16},{8,24},{16,0},{24,8},{1,17},{9,25},{17,1},{25,9},{2,18},{10... | collective-permute-start | bytes 2654216 | tf_op jit(solution)/shard_map/ppermute | solution.py:1409
  556.2 36.4 %collective-permute-start.8 = (bf16[288,1536]{1,0:T(8,128)(2,1)S(1)}, bf16[288,1536]{1,0:T(8,128)(2,1)}, u32[]{:S(2)}, u32[]{:S(2)}) collective-permute-start(bf16[288,1536]{1,0:T(8,128)(2,1)S(1)} %copy-done.62), channel_id=1, source_target_pairs={{0,24},{8,16},{16,8},{24,0},{1,25},{9,17},{17,9},{25,1},{2,26},{10... | collective-permute-start | bytes 2654216 | tf_op jit(solution)/shard_map/ppermute | solution.py:1409
  575.7 16.9 %copy-start.3 = (bf16[128,1536]{1,0:T(8,128)(2,1)S(1)}, bf16[128,1536]{1,0:T(8,128)(2,1)}, u32[]{:S(2)}) copy-start(bf16[128,1536]{1,0:T(8,128)(2,1)} %reduce-scatter.11.cloned.1.call-done) | copy-start | bytes 1179652
  575.7 18.3 %copy-start.5 = (bf16[128,1536]{1,0:T(8,128)(2,1)S(1)}, bf16[128,1536]{1,0:T(8,128)(2,1)}, u32[]{:S(2)}) copy-start(bf16[128,1536]{1,0:T(8,128)(2,1)} %get-tuple-element.280) | copy-start | bytes 1179652
  594.0 15.7 %copy-start.59 = (f32[128]{0:T(128)}, f32[128]{0:T(128)S(1)}, u32[]{:S(2)}) copy-start(f32[128]{0:T(128)S(1)} %broadcast_multiply_fusion.2) | copy-start | bytes 1540
  596.9 147.4 %reduce-scatter.17.cloned.1.call-start = ((), (), s32[]{:S(2)}) async-start(), calls=%async_computation.18 | async-start | bytes 3538944 | tf_op jit(solution)/shard_map/reduce_scatter | solution.py:1627
  609.8 201.3 %reduce-scatter.21.cloned.1.call-start = ((), (), s32[]{:S(2)}) async-start(), calls=%async_computation.21 | async-start | bytes 3538944 | tf_op jit(solution)/shard_map/reduce_scatter | solution.py:1690
  692.5 126.2 %reduce-scatter.19.cloned.1.call-start = ((), (), s32[]{:S(2)}) async-start(), calls=%async_computation.20 | async-start | bytes 3538944 | tf_op jit(solution)/shard_map/reduce_scatter | solution.py:1627
  741.0 169.9 %reduce-scatter.23.cloned.1.call-start = ((), (), s32[]{:S(2)}) async-start(), calls=%async_computation.22 | async-start | bytes 3538944 | tf_op jit(solution)/shard_map/reduce_scatter | solution.py:1690
  895.7 16.5 %copy-start.6 = (bf16[128,1536]{1,0:T(8,128)(2,1)S(1)}, bf16[128,1536]{1,0:T(8,128)(2,1)}, u32[]{:S(2)}) copy-start(bf16[128,1536]{1,0:T(8,128)(2,1)} %get-tuple-element.280) | copy-start | bytes 1179652
  895.7 16.5 %copy-start.11 = (bf16[128,1536]{1,0:T(8,128)(2,1)S(1)}, bf16[128,1536]{1,0:T(8,128)(2,1)}, u32[]{:S(2)}) copy-start(bf16[128,1536]{1,0:T(8,128)(2,1)} %reduce-scatter.15.cloned.1.call-done) | copy-start | bytes 1179652
  (45 other events, 183.5 us)
Sparse Core Ops, SparseCore 0:
  73.5 36.3 all-gather.9
  111.5 37.1 all-gather.7
  151.0 39.7 reduce-scatter.8
  216.9 36.7 all-gather.13
  255.8 39.1 reduce-scatter.10
  296.6 37.3 all-gather.11
  336.2 37.1 all-gather.15
  431.2 39.1 reduce-scatter.12
  484.2 39.2 all-gather.17
  553.3 39.1 reduce-scatter.14
  597.0 39.3 all-gather.19
  639.2 39.1 reduce-scatter.16
  692.6 41.7 reduce-scatter.20
  741.1 45.4 reduce-scatter.18
  794.6 44.4 reduce-scatter.22

commit v4 on v3

--- a/solution.py
+++ b/solution.py
@@ -1090,10 +1090,12 @@
     refs = list(refs)
     sets = [refs[at * 12 : (at + 1) * 12] for at in range(micro_n)]
     refs = refs[micro_n * 12 :]
-    outs, small_outs, refs = refs[:5], refs[5:9], refs[9:]
-    totals, got, refs = refs[:4], refs[4:9], refs[9:]
-    io_s, io_got, io_t_s, small_s, small_got, few_got, row_sems, col_sems = (
-        refs[0], refs[1], refs[2], refs[3:7], refs[7:11], refs[11:13], refs[13], refs[14]
+    pieces, refs = refs[:rows_n], refs[rows_n:]
+    outs, small_outs, refs = refs[:2], refs[2:6], refs[6:]
+    totals, got, refs = refs[:5], refs[5:7], refs[7:]
+    rows_t, refs = refs[:micro_n], refs[micro_n:]
+    io_s, io_got, small_s, small_got, few_got, row_sems, col_sems = (
+        refs[0], refs[1], refs[2:6], refs[6:10], refs[10:12], refs[12], refs[13]
     )
     me, at = lax.axis_index("row"), lax.axis_index("col")
     width = sets[0][0].shape[1]
@@ -1123,50 +1125,41 @@
                 to_row(which, k, small_s[which], small_got[which].at[k], other)
             )
 
-    def io_step(block, carry):
+    def total_at(which, cols, rights, left):
+        totals[which][cols, :] = functools.reduce(
+            jnp.add, [dot_last(right, one[left][...]) for right, one in zip(rights, sets)]
+        ).astype(BF16)
+
+    def early_step(block, carry):
         cols = block_cols(block)
-        io_s[:, cols] = functools.reduce(
-            jnp.add, [dot_plain(one[6][...], one[0][:, cols]) for one in sets]
-        ).astype(BF16)
+        rights = [jnp.transpose(one[0][:, cols]) for one in sets]
+        for kept, right in zip(rows_t, rights):
+            kept[cols, :] = right
+        total_at(3, cols, rights, 5)
+        total_at(4, cols, rights, 6)
         return carry
 
-    lax.fori_loop(0, width // BLOCK, io_step, 0)
-    io_copies = []
-    for k, other in enumerate(col_peers):
-        place = pl.ds(pl.multiple_of((at ^ (k + 1)) * io_rows, io_rows), io_rows)
-        io_copies.append(to_col(0, k, io_s.at[place], io_got.at[k], other))
-    def grads_at(cols):
-        rows_t = [jnp.transpose(one[0][:, cols]) for one in sets]
-        d_res_t = [jnp.transpose(one[1][:, cols]) for one in sets]
-        for which, left in enumerate((2, 3, 4, 5)):
-            right_t = d_res_t if left == 4 else rows_t
-            totals[which][cols, :] = functools.reduce(
-                jnp.add, [dot_last(right, one[left][...]) for right, one in zip(right_t, sets)]
-            ).astype(BF16)
-
-    def send_grads(k):
+    lax.fori_loop(0, width // BLOCK, early_step, 0)
+    for k, other in enumerate(row_peers):
+        place = pl.ds(pl.multiple_of((me ^ (k + 1)) * depth, depth), depth)
+        for which in range(2):
+            row_copies.append(
+                to_row(4 + which, k, totals[3 + which].at[place], got[which].at[k], other)
+            )
+
+    def late_step(block, carry):
+        cols = block_cols(block)
+        rights = [kept[cols, :] for kept in rows_t]
+        total_at(0, cols, rights, 2)
+        total_at(1, cols, rights, 3)
+        total_at(2, cols, [jnp.transpose(one[1][:, cols]) for one in sets], 4)
+        return carry
+
+    lax.fori_loop(0, width // BLOCK, late_step, 0)
+    for k in range(rows_n):
         place = pl.ds(pl.multiple_of((me ^ k) * depth, depth), depth)
-        for which in range(4):
-            row_copies.append(
-                to_row(
-                    4 + which, k - 1, totals[which].at[place], got[which].at[k - 1], row_peers[k - 1]
-                )
-            )
-
-    if depth % LANES == 0:
-        for k in [*range(1, rows_n), 0]:
-            grads_at(pl.ds(pl.multiple_of((me ^ k) * depth, depth), depth))
-            if k:
-                send_grads(k)
-    else:
-
-        def grad_step(block, carry):
-            grads_at(block_cols(block))
-            return carry
-
-        lax.fori_loop(0, width // BLOCK, grad_step, 0)
-        for k in range(1, rows_n):
-            send_grads(k)
+        for which in range(3):
+            pieces[k][which] = totals[which][place, :]
     for copy in small_copies:
         copy.wait()
     for which in range(4):
@@ -1179,15 +1172,21 @@
         for which in range(2)
         for k, other in enumerate(col_peers)
     ]
-    for copy in io_copies:
+    own = pl.ds(pl.multiple_of(me * depth, depth), depth)
+    for copy in row_copies:
         copy.wait()
-    io_total = io_s[pl.ds(pl.multiple_of(at * io_rows, io_rows), io_rows), :].astype(F32)
-    for k in range(cols_n - 1):
-        io_total = io_total + io_got[k].astype(F32)
-    io_t_s[...] = jnp.transpose(io_total).astype(BF16)
-    for k, other in enumerate(row_peers):
-        place = pl.ds(pl.multiple_of((me ^ (k + 1)) * depth, depth), depth)
-        row_copies.append(to_row(8, k, io_t_s.at[place], got[4].at[k], other))
+    sums = []
+    for which in range(2):
+        value = totals[3 + which][own, :].astype(F32)
+        for k in range(rows_n - 1):
+            value = value + got[which][k].astype(F32)
+        sums.append(value)
+    outs[0][...] = sums[0]
+    io_s[...] = jnp.transpose(sums[1]).astype(BF16)
+    io_copies = []
+    for k, other in enumerate(col_peers):
+        place = pl.ds(pl.multiple_of((at ^ (k + 1)) * io_rows, io_rows), io_rows)
+        io_copies.append(to_col(0, k, io_s.at[place], io_got.at[k], other))
     for copy in few_copies:
         copy.wait()
     for which in range(4):
@@ -1196,14 +1195,12 @@
             for k in range(cols_n - 1):
                 value = value + few_got[which][k]
         small_outs[which][...] = value
-    own = pl.ds(pl.multiple_of(me * depth, depth), depth)
-    for copy in row_copies:
+    for copy in io_copies:
         copy.wait()
-    for which, total in enumerate([*totals, io_t_s]):
-        value = total[own, :].astype(F32)
-        for k in range(rows_n - 1):
-            value = value + got[which][k].astype(F32)
-        outs[which][...] = value
+    value = io_s[pl.ds(pl.multiple_of(at * io_rows, io_rows), io_rows), :].astype(F32)
+    for k in range(cols_n - 1):
+        value = value + io_got[k].astype(F32)
+    outs[1][...] = jnp.transpose(value)
 
 
 def tail_sums(rows_n, cols_n, first_gain, sets):
@@ -1218,18 +1215,20 @@
     small_f32 = lambda lead, dims: pltpu.VMEM(lead + dims, F32)
     return pl.pallas_call(
         functools.partial(tail_kernel, rows_n, cols_n, len(sets)),
-        out_shape=tuple(shape((depth, share), F32) for share in shares + [io_rows])
+        out_shape=(shape((3, depth, shares[0]), BF16),) * rows_n
+        + (shape((depth, shares[3]), F32), shape((depth, io_rows), F32))
         + tuple(shape(dims, F32) for dims in small),
         in_specs=[VMEM] * (1 + 12 * len(sets)),
-        out_specs=(VMEM,) * 9,
-        scratch_shapes=[vmem(width, share) for share in shares]
-        + [vmem(rows_n - 1, depth, share) for share in shares + [io_rows]]
-        + [vmem(io_full, width), vmem(cols_n - 1, io_rows, width), vmem(width, io_rows)]
+        out_specs=(VMEM,) * (rows_n + 6),
+        scratch_shapes=[vmem(width, share) for share in shares + [io_full]]
+        + [vmem(rows_n - 1, depth, share) for share in (shares[3], io_full)]
+        + [vmem(width, sets[0][0].shape[0])] * len(sets)
+        + [vmem(io_full, depth), vmem(cols_n - 1, io_rows, depth)]
         + [small_f32((), dims) for dims in small]
         + [small_f32((rows_n - 1,), dims) for dims in small]
         + [small_f32((cols_n - 1,), dims) for dims in small[:2]]
         + [
-            pltpu.SemaphoreType.DMA((2, 9, rows_n - 1)),
+            pltpu.SemaphoreType.DMA((2, 6, rows_n - 1)),
             pltpu.SemaphoreType.DMA((2, 3, cols_n - 1)),
         ],
         compiler_params=pltpu.CompilerParams(
@@ -1782,9 +1781,15 @@
                 head_grad,
             ]
         )
-    branch_grad, conv_grad, out_grad_sum, step_grad, io_proj_grad, gains, io_sums, chans, by_head = (
-        step(lambda sets: tail_sums(rows_n, cols_n, first_gain[None, :], sets), sets)
+    *pieces, step_grad, io_proj_grad, gains, io_sums, chans, by_head = step(
+        lambda sets: tail_sums(rows_n, cols_n, first_gain[None, :], sets), sets
     )
+    pieces = swap_all(pieces)
+    gate_grads, up_grads, down_grads = arrive([gate_grads, up_grads, down_grads])
+    branch_grad, conv_grad, out_grad_sum = [
+        functools.reduce(jnp.add, [piece[which].astype(F32) for piece in pieces])
+        for which in range(3)
+    ]
     finish_input(second)
     io_values = lax.dynamic_slice(io_sums, (0, col_index * io_width), (5, io_width))
     return (

time: 931 us -> 913 us (0.981)
  Pallas kernels: 729 us -> 699 us
    pallas_call x1, Pallas kernels: 75.4 us -> 46.4 us  [tail_sums(): pl.pallas_call(functools.partial(tail_kernel, rows_n, cols_n, len(sets)),...]
    ppermute x9 -> x12, waiting for transfers between devices: 23.9 us -> 33.1 us  [swap(): return lax.ppermute(values, 'row', [(i, i ^ k) for i in range(rows_n)])]
    unnamed x156 -> x150, local copies, waits for them, and re-layouts: 19.7 us -> 15.8 us
  transfers between devices with their start and end apart: 24 -> 27, of which waited for: 5 -> 6; matrix products, arithmetic and copies ran while one was open for 12% -> 12% of each run, Pallas kernels for 73% -> 71%
where the time goes in v4:
time: 913 us; the launch traced here: 907 us
  Pallas kernels  699 us (77%)
  other arithmetic  58.9 us (6%)
  local copies, waits for them, and re-layouts  51.1 us (6%)
  waiting for transfers between devices  38.1 us (4%)
  matrix products  27.6 us (3%)
  starting transfers between devices  16.4 us (2%)
  between operations  15.4 us (2%)
    pallas_call x2, Pallas kernels, expert_rows(): pl.pallas_call(kernel, out_shape=tuple(out_shape), in_specs=[VMEM] * (7 +...  165 us
    pallas_call x3, Pallas kernels, spread_rows(): pl.pallas_call(functools.partial(spread_kernel, members, weighted, len(be...  136 us
    pallas_call x2, Pallas kernels, mixer_backward(): pl.pallas_call(functools.partial(mixer_backward_kernel, heads, len(parts)...  130 us
    pallas_call x2, Pallas kernels, mixer_forward(): pl.pallas_call(functools.partial(mixer_forward_kernel, heads, cols_n, *un...  115 us
    pallas_call x1, Pallas kernels, gather_weights(): pl.pallas_call(functools.partial(gather_kernel, rows_n, cols_n), out_shap...  57.8 us
    pallas_call x2, Pallas kernels, combine_rows(): pl.pallas_call(functools.partial(combine_kernel, members, bool(parts)), o...  48.7 us
    pallas_call x1, Pallas kernels, tail_sums(): pl.pallas_call(functools.partial(tail_kernel, rows_n, cols_n, len(sets)),...  46.4 us
    ppermute x12, waiting for transfers between devices, swap(): return lax.ppermute(values, 'row', [(i, i ^ k) for i in range(rows_n)])  33.1 us
  transfers between devices with their start and end apart: 27, of which 6 were waited for; matrix products, arithmetic and copies ran while one was open for 12% of the time, Pallas kernels for 71%

profile of v4, /device:TPU:0, one launch (start us, length us, event | category | flops | bytes accessed | tf_op | source)
XLA Modules:
  0.0 906.9 jit_solution(15014681676623565029)
XLA Ops:
  12.6 1.9 fusion.30
  15.6 57.8 %shard_map.425 = (bf16[4,1168,384]{2,1,0:T(8,128)(2,1)}, bf16[4,256,384]{2,1,0:T(8,128)(2,1)}, bf16[256,128]{1,0:T(8,128)(2,1)}, bf16[8,128,1536]{2,1,0:T(8,128)(2,1)}) custom-call(bf16[1168,384]{1,0:T(8,128)(2,1)} %fusion.19.pack, bf16[32,384]{1,0:T(8,128)(2,1)} %bitcast.207, bf16[32,128]{1,0:T(8,128)(2,1)} %fusion.51.taps, ...), custom_call_target="tpu_custom_call" | custom-call | flops 1 | bytes 1 | tf_op jit(solution)/shard_map/pallas_call | solution.py:1326
  79.1 1.4 slice_bitcast_fusion.19
  86.0 44.5 %shard_map.426 = (bf16[1024,1536]{1,0:T(8,128)(2,1)}, f32[1,1024]{1,0:T(1,128)}, f32[384,1024]{1,0:T(8,128)}, f32[384,1024]{1,0:T(8,128)}, f32[256,1024]{1,0:T(8...) custom-call(bf16[1024,1536]{1,0:T(8,128)(2,1)} %bitcast.216, ...), custom_call_target="tpu_custom_call" | custom-call | flops 30000001024 | bytes 1048576 | tf_op jit(solution)/shard_map/pallas_call | solution.py:317
  130.8 3.2 constant_dynamic-slice_fusion.29
  134.0 2.3 copy.217
  136.3 1.6 collective-permute-start.1
  142.6 70.7 %shard_map.427 = (bf16[1024,1536]{1,0:T(8,128)(2,1)}, f32[1,1024]{1,0:T(1,128)}, f32[384,1024]{1,0:T(8,128)}, f32[384,1024]{1,0:T(8,128)}, f32[256,1024]{1,0:T(8...) custom-call(bf16[1024,1536]{1,0:T(8,128)(2,1)} %all-gather.10.cloned, ...), custom_call_target="tpu_custom_call" | custom-call | flops 30000001024 | bytes 1048576 | tf_op jit(solution)/shard_map/pallas_call | solution.py:317
  214.8 2.0 multiply_convert_fusion.1
  220.5 44.2 %shard_map.428.refs_2_ = bf16[2,576,1536]{2,1,0:T(8,128)(2,1)} custom-call(s32[8,1024]{1,0:T(8,128)} %pad_add_fusion.slot, f32[8,1024]{1,0:T(8,128)} %pad_maximum_fusion.7.gates, bf16[1024,1536]{1,0:T(8,128)(2,1)} %all-gather.8.cloned.1.call-done.source.refs_0_), custom_call_target="tpu_custom_call" | custom-call | flops 30000001024 | bytes 1048576 | tf_op jit(solution)/shard_map/pallas_call | solution.py:845
  265.4 1.4 collective-permute-start.3
  266.9 1.6 collective-permute-start.5
  268.6 5.8 collective-permute-done.3
  274.8 3.7 collective-permute-done.5
  279.6 44.3 %shard_map.429 = (bf16[2,576,1536]{2,1,0:T(8,128)(2,1)}, bf16[1024,128]{1,0:T(8,128)(2,1)}, bf16[1024,128]{1,0:T(8,128)(2,1)}, bf16[1024,128]{1,0:T(8,128)(2,1)}...) custom-call(s32[8,1024]{1,0:T(8,128)} %pad_add_fusion.slot, f32[8,1024]{1,0:T(8,128)} %pad_maximum_fusion.7.gates, ...), custom_call_target="tpu_custom_call" | custom-call | flops 30000001024 | bytes 1048576 | tf_op jit(solution)/shard_map/pallas_call | solution.py:845
  325.3 2.1 multiply_convert_fusion
  330.6 3.5 all-gather.12.cloned.1.call-done.refs_9_.refs_0_
  334.1 97.1 %shard_map.430 = (bf16[1024,1536]{1,0:T(8,128)(2,1)}, bf16[288,1536]{1,0:T(8,128)(2,1)}, bf16[288,1536]{1,0:T(8,128)(2,1)}, bf16[288,1536]{1,0:T(8,128)(2,1)}, b...) custom-call(s32[1024,8]{1,0:T(8,128)} %bitcast.197, ...), custom_call_target="tpu_custom_call" | custom-call | flops 30000001024 | bytes 1048576 | tf_op jit(solution)/shard_map/pallas_call | solution.py:1062
  431.3 48.0 %shard_map.431 = (bf16[2,576,1536]{2,1,0:T(8,128)(2,1)}, bf16[1024,128]{1,0:T(8,128)(2,1)}, bf16[1024,128]{1,0:T(8,128)(2,1)}, bf16[1024,128]{1,0:T(8,128)(2,1)}...) custom-call(s32[8,1024]{1,0:T(8,128)} %pad_add_fusion.1.refs_7_.slot, ...), custom_call_target="tpu_custom_call" | custom-call | flops 30000001024 | bytes 1048576 | tf_op jit(solution)/shard_map/pallas_call | solution.py:845
  479.3 2.0 fusion.28
  481.3 1.5 fusion.26
  485.4 67.6 %shard_map.432 = (bf16[1024,1536]{1,0:T(8,128)(2,1)}, bf16[288,1536]{1,0:T(8,128)(2,1)}, bf16[288,1536]{1,0:T(8,128)(2,1)}, bf16[288,1536]{1,0:T(8,128)(2,1)}, b...) custom-call(s32[1024,8]{1,0:T(8,128)} %bitcast.199, ...), custom_call_target="tpu_custom_call" | custom-call | flops 30000001024 | bytes 1048576 | tf_op jit(solution)/shard_map/pallas_call | solution.py:1062
  553.0 1.5 collective-permute-start.6
  554.5 1.5 collective-permute-start.7
  556.6 10.7 %fusion.64 = f32[2,1536,1024]{2,1,0:T(8,128)} fusion(bf16[2,576,1536]{2,1,0:T(8,128)(2,1)} %get-tuple-element.374.refs_1_, bf16[2,576,1024]{2,1,0:T(8,128)(2,1)} %get-tuple-element.375), kind=kOutput, calls=%fused_computation.212 | convolution fusion | flops 3623878656 | bytes 18481152 | tf_op jit(solution)/shard_map/ecd,ech->edh/dot_general | solution.py:1670
  567.3 8.2 add_convert_fusion
  575.5 2.8 constant_dynamic-slice_fusion.1
  578.3 14.1 %collective-permute-done.7.refs_2_ = bf16[288,1536]{1,0:T(8,128)(2,1)} collective-permute-done((bf16[288,1536]{1,0:T(8,128)(2,1)}, bf16[288,1536]{1,0:T(8,128)(2,1)}, u32[]{:S(2)}, u32[]{:S(2)}) %collective-permute-start.7) | collective-permute-done | bytes 884768 | tf_op jit(solution)/shard_map/ppermute | solution.py:1408
  592.4 1.4 fusion.29
  593.9 1.5 fusion.27
  598.0 11.6 %shard_map.433 = bf16[1024,1536]{1,0:T(8,128)(2,1)} custom-call(s32[1024,8]{1,0:T(8,128)} %bitcast.198, f32[1024,8]{1,0:T(8,128)} %bitcast.202, bf16[1024,128]{1,0:T(8,128)(2,1)} %get-tuple-element.384.extra_left, bf16[128,1536]{1,0:T(8,128)(2,1)} %get-tuple-element.678.refs_3_.extra_right, bf16[288,1536]{1,0:T(8,128)(2,1)} %get-tuple-element.385.refs_0_, ...), custom_call_target="tpu_custom_call" | custom-call | flops 30000001024 | bytes 1048576 | tf_op jit(solution)/shard_map/pallas_call | solution.py:708
  610.9 81.4 %shard_map.434 = (bf16[1024,1536]{1,0:T(8,128)(2,1)}, f32[8,1536]{1,0:T(8,128)}, bf16[384,1024]{1,0:T(8,128)(2,1)}, bf16[384,1024]{1,0:T(8,128)(2,1)}, bf16[384,...) custom-call(bf16[1024,1664]{1,0:T(8,128)(2,1)} %all-gather.18.cloned, ...), custom_call_target="tpu_custom_call" | custom-call | flops 30000001024 | bytes 1048576 | tf_op jit(solution)/shard_map/pallas_call | solution.py:593
  694.1 5.1 fusion.65
  699.2 2.9 add_convert_fusion.1
  702.2 1.7 constant_dynamic-slice_fusion.5
  703.9 37.0 %shard_map.435 = (bf16[1024,1536]{1,0:T(8,128)(2,1)}, bf16[4,2,384,512]{3,2,1,0:T(8,128)(2,1)}) custom-call(s32[1024,8]{1,0:T(8,128)} %bitcast.200, f32[1024,8]{1,0:T(8,128)} %bitcast.201, bf16[1024,128]{1,0:T(8,128)(2,1)} %get-tuple-element.418.extra_left, bf16[128,1536]{1,0:T(8,128)(2,1)} %get-tuple-element.678.refs_3_.extra_right, ...), custom_call_target="tpu_custom_call" | custom-call | flops 30000001024 | bytes 1048576 | tf_op jit(solution)/shard_map/pallas_call | solution.py:708
  746.1 49.0 %shard_map.436 = (bf16[1024,1536]{1,0:T(8,128)(2,1)}, f32[8,1536]{1,0:T(8,128)}, bf16[384,1024]{1,0:T(8,128)(2,1)}, bf16[384,1024]{1,0:T(8,128)(2,1)}, bf16[384,...) custom-call(bf16[1024,1664]{1,0:T(8,128)(2,1)} %all-gather.20.cloned, ...), custom_call_target="tpu_custom_call" | custom-call | flops 30000001024 | bytes 1048576 | tf_op jit(solution)/shard_map/pallas_call | solution.py:593
  796.6 1.6 fusion.40
  799.5 46.4 %shard_map.437 = (bf16[3,384,384]{2,1,0:T(8,128)(2,1)}, bf16[3,384,384]{2,1,0:T(8,128)(2,1)}, bf16[3,384,384]{2,1,0:T(8,128)(2,1)}, bf16[3,384,384]{2,1,0:T(8,12...) custom-call(f32[1,1536]{1,0:T(1,128)} %broadcast_in_dim.107.first_ga, ...), custom_call_target="tpu_custom_call" | custom-call | flops 30000001024 | bytes 1048576 | tf_op jit(solution)/shard_map/pallas_call | solution.py:1216
  848.5 1.6 copy.212
  850.1 1.7 copy.211
  855.3 5.5 bitcast_convert_fusion
  860.8 6.7 copy.210
  871.7 5.6 bitcast_convert_fusion.1
  877.4 3.8 bitcast_convert_fusion.2
  882.5 1.7 fusion.35
  885.4 9.3 %collective-permute-done.10 = bf16[3,384,384]{2,1,0:T(8,128)(2,1)} collective-permute-done((bf16[3,384,384]{2,1,0:T(8,128)(2,1)}, bf16[3,384,384]{2,1,0:T(8,128)(2,1)}, u32[]{:S(2)}, u32[]{:S(2)}) %collective-permute-start.10) | collective-permute-done | bytes 884768 | tf_op jit(solution)/shard_map/ppermute | solution.py:1408
  894.7 3.1 add_bitcast_fusion
  (309 shorter events, 66.3 us)
Async XLA Ops:
  7.2 135.4 %all-gather.10.cloned.1.call-start = ((), (), s32[]{:S(2)}) async-start(), calls=%async_computation.10 | async-start | bytes 3538944 | tf_op jit(solution)/shard_map/all_gather | solution.py:1446
  12.6 60.9 %copy-start.55 = (s32[2,1]{0,1:T(1,128)S(1)}, s32[2,1]{0,1:T(1,128)}, u32[]{:S(2)}) copy-start(s32[2,1]{0,1:T(1,128)} %param.28) | copy-start | bytes 28
  12.6 62.8 %copy-start.14 = (bf16[2,128,1536]{2,1,0:T(8,128)(2,1)S(1)}, bf16[2,128,1536]{2,1,0:T(8,128)(2,1)}, u32[]{:S(2)}) copy-start(bf16[2,128,1536]{2,1,0:T(8,128)(2,1)} %param.27) | copy-start | bytes 2359300
  14.5 62.0 %copy-start.53 = (f32[384]{0:T(512)S(1)}, f32[384]{0:T(512)}, u32[]{:S(2)}) copy-start(f32[384]{0:T(512)} %param.37) | copy-start | bytes 4612
  14.5 62.0 %copy-start.54 = (f32[384]{0:T(512)S(1)}, f32[384]{0:T(512)}, u32[]{:S(2)}) copy-start(f32[384]{0:T(512)} %param.43) | copy-start | bytes 4612
  14.5 62.0 %copy-start.62 = (f32[6]{0:T(128)S(1)}, f32[6]{0:T(128)}, u32[]{:S(2)}) copy-start(f32[6]{0:T(128)} %param.40) | copy-start | bytes 76
  14.5 62.0 %copy-start.60 = (f32[6]{0:T(128)S(1)}, f32[6]{0:T(128)}, u32[]{:S(2)}) copy-start(f32[6]{0:T(128)} %param.41) | copy-start | bytes 76
  14.5 62.1 %copy-start.59 = (f32[6]{0:T(128)S(1)}, f32[6]{0:T(128)}, u32[]{:S(2)}) copy-start(f32[6]{0:T(128)} %param.42) | copy-start | bytes 76
  14.5 62.9 %copy-start.49 = (f32[4,384]{1,0:T(4,128)S(1)}, f32[4,384]{1,0:T(4,128)}, u32[]{:S(2)}) copy-start(f32[4,384]{1,0:T(4,128)} %param.36) | copy-start | bytes 18436
  73.4 139.9 %all-gather.8.cloned.1.call-start = ((), (), s32[]{:S(2)}) async-start(), calls=%async_computation.9 | async-start | bytes 3538944 | tf_op jit(solution)/shard_map/all_gather | solution.py:1555
  76.4 136.9 %reduce-scatter.9.cloned.1.call-start = ((), (), s32[]{:S(2)}) async-start(), calls=%async_computation.8 | async-start | bytes 3538944 | tf_op jit(solution)/shard_map/reduce_scatter | solution.py:1533
  130.5 149.1 %all-gather.14.cloned.1.call-start = ((), (), s32[]{:S(2)}) async-start(), calls=%async_computation.12 | async-start | bytes 3538944 | tf_op jit(solution)/shard_map/all_gather | solution.py:1551
  136.3 77.0 %collective-permute-start.1 = (bf16[2,384,512]{2,1,0:T(8,128)(2,1)}, bf16[2,384,512]{2,1,0:T(8,128)(2,1)}, u32[]{:S(2)}, u32[]{:S(2)}) collective-permute-start(bf16[2,384,512]{2,1,0:T(8,128)(2,1)} %bitcast.194), channel_id=1, source_target_pairs={{0,16},{8,24},{16,0},{24,8},{1,17},{9,25},{17,1},{25,9},{2,18},{10... | collective-permute-start | bytes 2359304 | tf_op jit(solution)/shard_map/ppermute | solution.py:1408
  139.1 74.2 %collective-permute-start.2 = (bf16[2,384,512]{2,1,0:T(8,128)(2,1)}, bf16[2,384,512]{2,1,0:T(8,128)(2,1)}, u32[]{:S(2)}, u32[]{:S(2)}) collective-permute-start(bf16[2,384,512]{2,1,0:T(8,128)(2,1)} %bitcast.195), channel_id=1, source_target_pairs={{0,24},{8,16},{16,8},{24,0},{1,25},{9,17},{17,9},{25,1},{2,26},{10... | collective-permute-start | bytes 2359304 | tf_op jit(solution)/shard_map/ppermute | solution.py:1408
  140.7 72.6 %collective-permute-start = (bf16[2,384,512]{2,1,0:T(8,128)(2,1)S(1)}, bf16[2,384,512]{2,1,0:T(8,128)(2,1)}, u32[]{:S(2)}, u32[]{:S(2)}) collective-permute-start(bf16[2,384,512]{2,1,0:T(8,128)(2,1)S(1)} %bitcast.196), channel_id=1, source_target_pairs={{0,8},{8,0},{16,24},{24,16},{1,9},{9,1},{17,25},{25,17},{2,10},{10... | collective-permute-start | bytes 2359304 | tf_op jit(solution)/shard_map/ppermute | solution.py:1408
  142.6 70.8 %copy-start.37 = (f32[1,1024]{1,0:T(1,128)}, f32[1,1024]{1,0:T(1,128)S(1)}, u32[]{:S(2)}) copy-start(f32[1,1024]{1,0:T(1,128)S(1)} %add_rsqrt_fusion.1) | copy-start | bytes 12292
  142.6 72.2 %copy-start.15 = (f32[1536]{0:T(1024)S(1)}, f32[1536]{0:T(1024)}, u32[]{:S(2)}) copy-start(f32[1536]{0:T(1024)} %param.45) | copy-start | bytes 18436
  213.5 267.8 %copy-start.33 = (f32[128]{0:T(128)}, f32[128]{0:T(128)S(1)}, u32[]{:S(2)}) copy-start(f32[128]{0:T(128)S(1)} %dynamic_slice.113) | copy-start | bytes 1540
  214.8 266.5 %copy-start.42 = (f32[128]{0:T(128)}, f32[128]{0:T(128)S(1)}, u32[]{:S(2)}) copy-start(f32[128]{0:T(128)S(1)} %add_rsqrt_fusion.3) | copy-start | bytes 1540
  216.9 106.9 %reduce-scatter.11.cloned.1.call-start = ((), (), s32[]{:S(2)}) async-start(), calls=%async_computation.13 | async-start | bytes 3538944 | tf_op jit(solution)/shard_map/reduce_scatter | solution.py:1533
  217.5 116.6 %all-gather.12.cloned.1.call-start = ((), (), s32[]{:S(2)}) async-start(), calls=%async_computation.11 | async-start | bytes 3538944 | tf_op jit(solution)/shard_map/all_gather | solution.py:1555
  218.1 213.2 %all-gather.16.cloned.1.call-start = ((), (), s32[]{:S(2)}) async-start(), calls=%async_computation.14 | async-start | bytes 3538944 | tf_op jit(solution)/shard_map/all_gather | solution.py:1551
  220.5 44.3 %copy-start.27 = (bf16[128,384]{1,0:T(8,128)(2,1)S(1)}, bf16[128,384]{1,0:T(8,128)(2,1)}, u32[]{:S(2)}) copy-start(bf16[128,384]{1,0:T(8,128)(2,1)} %param.51) | copy-start | bytes 294916
  220.5 46.3 %copy-start.51 = (f32[1,1024]{1,0:T(1,128)S(1)}, f32[1,1024]{1,0:T(1,128)}, u32[]{:S(2)}) copy-start(f32[1,1024]{1,0:T(1,128)} %get-tuple-element.307) | copy-start | bytes 12292
  264.8 9.9 %collective-permute-start.4 = (bf16[384,384]{1,0:T(8,128)(2,1)S(1)}, bf16[384,384]{1,0:T(8,128)(2,1)S(1)}, u32[]{:S(2)}, u32[]{:S(2)}) collective-permute-start(bf16[384,384]{1,0:T(8,128)(2,1)S(1)} %constant_dynamic-update-slice_fusion.4), channel_id=1, source_target_pairs={{0,16},{8,24},{16,0},{24,8},{1,17},{9,25},{17,1},{25,9},{2,18},{10... | collective-permute-start | bytes 884744 | tf_op jit(solution)/shard_map/ppermute | solution.py:1408
  265.4 9.0 collective-permute-start.3
  266.9 57.0 %copy-start.39 = (f32[1,1024]{1,0:T(1,128)}, f32[1,1024]{1,0:T(1,128)S(1)}, u32[]{:S(2)}) copy-start(f32[1,1024]{1,0:T(1,128)S(1)} %add_rsqrt_fusion) | copy-start | bytes 12292
  266.9 11.6 %collective-permute-start.5 = (bf16[384,384]{1,0:T(8,128)(2,1)S(1)}, bf16[384,384]{1,0:T(8,128)(2,1)S(1)}, u32[]{:S(2)}, u32[]{:S(2)}) collective-permute-start(bf16[384,384]{1,0:T(8,128)(2,1)S(1)} %constant_dynamic-update-slice_fusion.4), channel_id=1, source_target_pairs={{0,24},{8,16},{16,8},{24,0},{1,25},{9,17},{17,9},{25,1},{2,26},{10... | collective-permute-start | bytes 884744 | tf_op jit(solution)/shard_map/ppermute | solution.py:1408
  324.0 269.9 %copy-start.35 = (f32[128]{0:T(128)}, f32[128]{0:T(128)S(1)}, u32[]{:S(2)}) copy-start(f32[128]{0:T(128)S(1)} %dynamic_slice.122) | copy-start | bytes 1540
  325.3 268.6 %copy-start.43 = (f32[128]{0:T(128)}, f32[128]{0:T(128)S(1)}, u32[]{:S(2)}) copy-start(f32[128]{0:T(128)S(1)} %add_rsqrt_fusion.2) | copy-start | bytes 1540
  327.4 151.9 %reduce-scatter.13.cloned.1.call-start = ((), (), s32[]{:S(2)}) async-start(), calls=%async_computation.15 | async-start | bytes 3538944 | tf_op jit(solution)/shard_map/reduce_scatter | solution.py:1612
  431.2 48.1 %copy-start.1 = (bf16[128,1536]{1,0:T(8,128)(2,1)S(1)}, bf16[128,1536]{1,0:T(8,128)(2,1)}, u32[]{:S(2)}) copy-start(bf16[128,1536]{1,0:T(8,128)(2,1)} %reduce-scatter.9.cloned.1.call-done) | copy-start | bytes 1179652
  431.2 50.1 %copy-start.6 = (bf16[128,1536]{1,0:T(8,128)(2,1)S(1)}, bf16[128,1536]{1,0:T(8,128)(2,1)}, u32[]{:S(2)}) copy-start(bf16[128,1536]{1,0:T(8,128)(2,1)} %get-tuple-element.271) | copy-start | bytes 1179652
  431.2 125.4 %all-gather.18.cloned.1.call-start = ((), (), s32[]{:S(2)}) async-start(), calls=%async_computation.16 | async-start | bytes 3833856 | tf_op jit(solution)/shard_map/all_gather | solution.py:1646
  484.1 108.2 %reduce-scatter.15.cloned.1.call-start = ((), (), s32[]{:S(2)}) async-start(), calls=%async_computation.17 | async-start | bytes 3538944 | tf_op jit(solution)/shard_map/reduce_scatter | solution.py:1612
  553.0 150.9 %all-gather.20.cloned.1.call-start = ((), (), s32[]{:S(2)}) async-start(), calls=%async_computation.19 | async-start | bytes 3833856 | tf_op jit(solution)/shard_map/all_gather | solution.py:1646
  553.0 25.3 %collective-permute-start.6 = (bf16[288,1536]{1,0:T(8,128)(2,1)}, bf16[288,1536]{1,0:T(8,128)(2,1)}, u32[]{:S(2)}, u32[]{:S(2)}) collective-permute-start(bf16[288,1536]{1,0:T(8,128)(2,1)} %get-tuple-element.330), channel_id=1, source_target_pairs={{0,8},{8,0},{16,24},{24,16},{1,9},{9,1},{17,25},{25,17},{2,10},{10... | collective-permute-start | bytes 2654216 | tf_op jit(solution)/shard_map/ppermute | solution.py:1408
  554.5 37.9 %collective-permute-start.7 = (bf16[288,1536]{1,0:T(8,128)(2,1)}, bf16[288,1536]{1,0:T(8,128)(2,1)}, u32[]{:S(2)}, u32[]{:S(2)}) collective-permute-start(bf16[288,1536]{1,0:T(8,128)(2,1)} %get-tuple-element.331), channel_id=1, source_target_pairs={{0,16},{8,24},{16,0},{24,8},{1,17},{9,25},{17,1},{25,9},{2,18},{10... | collective-permute-start | bytes 2654216 | tf_op jit(solution)/shard_map/ppermute | solution.py:1408
  556.0 36.4 %collective-permute-start.8 = (bf16[288,1536]{1,0:T(8,128)(2,1)S(1)}, bf16[288,1536]{1,0:T(8,128)(2,1)}, u32[]{:S(2)}, u32[]{:S(2)}) collective-permute-start(bf16[288,1536]{1,0:T(8,128)(2,1)S(1)} %copy-done.61), channel_id=1, source_target_pairs={{0,24},{8,16},{16,8},{24,0},{1,25},{9,17},{17,9},{25,1},{2,26},{10... | collective-permute-start | bytes 2654216 | tf_op jit(solution)/shard_map/ppermute | solution.py:1408
  575.5 18.3 %copy-start.4 = (bf16[128,1536]{1,0:T(8,128)(2,1)S(1)}, bf16[128,1536]{1,0:T(8,128)(2,1)}, u32[]{:S(2)}) copy-start(bf16[128,1536]{1,0:T(8,128)(2,1)} %get-tuple-element.284) | copy-start | bytes 1179652
  596.7 148.1 %reduce-scatter.17.cloned.1.call-start = ((), (), s32[]{:S(2)}) async-start(), calls=%async_computation.18 | async-start | bytes 3538944 | tf_op jit(solution)/shard_map/reduce_scatter | solution.py:1626
  609.6 185.5 %reduce-scatter.21.cloned.1.call-start = ((), (), s32[]{:S(2)}) async-start(), calls=%async_computation.21 | async-start | bytes 3538944 | tf_op jit(solution)/shard_map/reduce_scatter | solution.py:1689
  692.3 105.9 %reduce-scatter.19.cloned.1.call-start = ((), (), s32[]{:S(2)}) async-start(), calls=%async_computation.20 | async-start | bytes 3538944 | tf_op jit(solution)/shard_map/reduce_scatter | solution.py:1626
  741.0 140.1 %reduce-scatter.23.cloned.1.call-start = ((), (), s32[]{:S(2)}) async-start(), calls=%async_computation.22 | async-start | bytes 3538944 | tf_op jit(solution)/shard_map/reduce_scatter | solution.py:1689
  746.1 49.1 %copy-start.48 = (f32[128]{0:T(128)S(1)}, f32[128]{0:T(128)}, u32[]{:S(2)}) copy-start(f32[128]{0:T(128)} %copy-done.47) | copy-start | bytes 1540
  851.8 33.6 %collective-permute-start.9 = (bf16[3,384,384]{2,1,0:T(8,128)(2,1)}, bf16[3,384,384]{2,1,0:T(8,128)(2,1)}, u32[]{:S(2)}, u32[]{:S(2)}) collective-permute-start(bf16[3,384,384]{2,1,0:T(8,128)(2,1)} %get-tuple-element.494), channel_id=1, source_target_pairs={{0,8},{8,0},{16,24},{24,16},{1,9},{9,1},{17,25},{25,17},{2,10},{10... | collective-permute-start | bytes 2654216 | tf_op jit(solution)/shard_map/ppermute | solution.py:1408
  853.2 41.5 %collective-permute-start.10 = (bf16[3,384,384]{2,1,0:T(8,128)(2,1)}, bf16[3,384,384]{2,1,0:T(8,128)(2,1)}, u32[]{:S(2)}, u32[]{:S(2)}) collective-permute-start(bf16[3,384,384]{2,1,0:T(8,128)(2,1)} %get-tuple-element.495), channel_id=1, source_target_pairs={{0,16},{8,24},{16,0},{24,8},{1,17},{9,25},{17,1},{25,9},{2,18},{10... | collective-permute-start | bytes 2654216 | tf_op jit(solution)/shard_map/ppermute | solution.py:1408
  854.2 40.6 %collective-permute-start.11 = (bf16[3,384,384]{2,1,0:T(8,128)(2,1)}, bf16[3,384,384]{2,1,0:T(8,128)(2,1)}, u32[]{:S(2)}, u32[]{:S(2)}) collective-permute-start(bf16[3,384,384]{2,1,0:T(8,128)(2,1)} %get-tuple-element.496), channel_id=1, source_target_pairs={{0,24},{8,16},{16,8},{24,0},{1,25},{9,17},{17,9},{25,1},{2,26},{10... | collective-permute-start | bytes 2654216 | tf_op jit(solution)/shard_map/ppermute | solution.py:1408
  (46 other events, 249.9 us)
Sparse Core Ops, SparseCore 0:
  73.5 36.3 all-gather.9
  111.5 37.1 all-gather.7
  151.0 39.7 reduce-scatter.8
  217.0 36.7 all-gather.13
  255.9 39.2 reduce-scatter.10
  296.7 37.3 all-gather.11
  336.3 37.1 all-gather.15
  431.3 39.1 reduce-scatter.12
  484.3 39.2 all-gather.17
  553.1 39.1 reduce-scatter.14
  596.8 39.3 all-gather.19
  639.0 39.1 reduce-scatter.16
  692.5 41.7 reduce-scatter.20
  741.1 45.5 reduce-scatter.18
  796.7 50.3 reduce-scatter.22
